TPU v7x, 256 devices: a whole 4x4x8 slice. The times are simulated.
256 devices in a mesh: seq: 32 (over z_lo, x, core), heads: 8 (over z_hi, y).
Axes of the slice: x: 4, y: 4, z: 8 (z_hi: 2, z_lo: 4; z = z_hi * 4 + z_lo), core: 2. Of those that a mesh axis runs over, the one named last changes fastest.
Arguments:
- query_rows: bfloat16 [4096, 8192], P('seq', 'heads'), may hold values from -128 to 128
- key_rows: bfloat16 [4096, 1024], P('seq', 'heads'), may hold values from -8 to 8
- value_rows: bfloat16 [4096, 1024], P('seq', 'heads'), may hold values from -6 to 6
- out_grad: bfloat16 [4096, 8192], P('seq', 'heads'), may hold values from -6 to 6
- log_ratio: float32 [4096], P(('seq', 'heads')), may hold values from -12 to 12
- block_mask: int32 [32, 32], replicated, may hold values from 0 to 1, as said below
- response_bounds: int32 [9], replicated, may hold values from 128 to 4096, as said below
- pair_index: int32 [8, 2], replicated, may hold values from 0 to 7, all different within a row
Outputs:
- query_grad: bfloat16 [4096, 8192], P('seq', 'heads')
- key_grad: bfloat16 [4096, 1024], P('seq', 'heads')
- value_grad: bfloat16 [4096, 1024], P('seq', 'heads')
Inputs may be any that keep to these rules, and one draw needn't show every extreme that they name: block_mask[i, j] is 1 exactly where j <= i and block j lies in the prompt or in the same response as block i, as given by response_bounds. response_bounds[0] ends the prompt and response r covers positions response_bounds[r] to response_bounds[r+1] - 1; all are multiples of 128, strictly rising, the prompt is at least one block and the last entry is 4096. `pair_index`: each row names two different responses, preferred first.
All inputs are finite; a program needn't handle non-finite values.
Results may differ from a plain program's by a relative error of at most 0.039.
Values may be sent and summed in bfloat16 or wider, within the bound.
No kernel may reach another device: no remote copies, remote signals or barrier semaphores. Data moves between devices by JAX's collectives and lax.ppermute only.
A program may use at most 64 MiB of HBM per device.

v0:
```python
import math

import jax
import jax.numpy as jnp
from jax import lax
from jax.sharding import PartitionSpec as P

DH = 128
HQ = 64
KVH = 8
BLOCK = 128
RESP = 8
PAIRS = 8


loss_scale = 512.0
margin_target = 1.0
very_negative = -1e30


def response_sums(ratios, positions, starts, resp_ends):
    member = (positions[None, :] >= starts[:, None]) & (positions[None, :] < resp_ends[:, None])
    return jnp.sum(jnp.where(member, ratios[None, :], 0.0), axis=1)


def coefficients(means, pair_index):
    resp_ids = jnp.arange(RESP, dtype=jnp.int32)
    winner = (pair_index[:, 0:1] == resp_ids[None, :]).astype(jnp.float32)
    loser = (pair_index[:, 1:2] == resp_ids[None, :]).astype(jnp.float32)
    margin = jnp.sum(winner * means[None, :], axis=1) - jnp.sum(loser * means[None, :], axis=1)
    resid = margin - margin_target
    return 2.0 / PAIRS * jnp.sum(resid[:, None] * (winner - loser), axis=0)


def sweep_blocks(step_fn, initial, whole_keys, whole_values):
    block_rows = math.gcd(512, whole_keys.shape[0])

    def loop_body(block_index, carry):
        first_row = block_index * block_rows
        pieces = (
            lax.dynamic_slice_in_dim(whole_keys, first_row, block_rows, 0),
            lax.dynamic_slice_in_dim(whole_values, first_row, block_rows, 0),
        )
        return step_fn(carry, pieces, first_row)

    return lax.fori_loop(0, whole_keys.shape[0] // block_rows, loop_body, initial)


def shards(
    query_rows, key_rows, value_rows, out_grad, log_ratio, block_mask, response_bounds, pair_index
):
    tok_rows = query_rows.shape[0]
    kv_dev = key_rows.shape[1] // DH
    group_size = HQ // KVH
    all_tokens = tok_rows * lax.axis_size("seq")
    score_scale = 1.0 / math.sqrt(DH)
    starts = response_bounds[:RESP]
    resp_ends = response_bounds[1:]
    lengths = (resp_ends - starts).astype(jnp.float32)
    ratio_len = log_ratio.shape[0]
    ratio_pos = lax.axis_index(("seq", "heads")) * ratio_len + jnp.arange(
        ratio_len, dtype=jnp.int32
    )
    resp_sums = lax.psum(response_sums(log_ratio, ratio_pos, starts, resp_ends), ("seq", "heads"))
    coef_resp = coefficients(resp_sums / lengths, pair_index)
    query_pos = lax.axis_index("seq") * tok_rows + jnp.arange(tok_rows, dtype=jnp.int32)
    member = (query_pos[None, :] >= starts[:, None]) & (query_pos[None, :] < resp_ends[:, None])
    weight = jnp.sum(jnp.where(member, (coef_resp / lengths)[:, None], 0.0), axis=0)
    grad_out = (weight[:, None] * out_grad.astype(jnp.float32) * loss_scale).astype(jnp.bfloat16)
    query_heads = query_rows.reshape(tok_rows, kv_dev, group_size, DH)
    grad_heads = grad_out.reshape(tok_rows, kv_dev, group_size, DH)
    block_ids = jnp.arange(block_mask.shape[0], dtype=jnp.int32)
    row_select = ((query_pos // BLOCK)[:, None] == block_ids[None, :]).astype(jnp.float32)
    row_table = jnp.dot(
        row_select, block_mask.astype(jnp.float32), preferred_element_type=jnp.float32
    )

    def live_of(key_pos):
        col_select = (block_ids[:, None] == (key_pos // BLOCK)[None, :]).astype(jnp.float32)
        seen = jnp.dot(row_table, col_select, preferred_element_type=jnp.float32) > 0.5
        return seen & (key_pos[None, :] <= query_pos[:, None])

    def masked_scores(key_heads, is_live):
        scores = (
            jnp.einsum("tcgd,ncd->cgtn", query_heads, key_heads, preferred_element_type=jnp.float32)
            * score_scale
        )
        return jnp.where(is_live, scores, -jnp.inf)

    def attend(carry, key_piece, first_row):
        piece_keys, piece_values = key_piece
        width = piece_keys.shape[0]
        is_live = live_of(first_row + jnp.arange(width, dtype=jnp.int32))

        def work(state):
            run_max, run_sum, run_acc = state
            key_heads = piece_keys.reshape(width, kv_dev, DH)
            value_heads = piece_values.reshape(width, kv_dev, DH)
            scores = masked_scores(key_heads, is_live)
            new_max = jnp.maximum(run_max, jnp.max(scores, axis=-1))
            probs = jnp.exp(scores - new_max[..., None])
            rescale = jnp.exp(run_max - new_max)
            new_sum = run_sum * rescale + jnp.sum(probs, axis=-1)
            new_acc = run_acc * rescale[..., None] + jnp.einsum(
                "cgtn,ncd->cgtd",
                probs.astype(jnp.bfloat16),
                value_heads,
                preferred_element_type=jnp.float32,
            )
            return (new_max, new_sum, new_acc)

        return lax.cond(jnp.any(is_live), work, lambda state: state, carry)

    def backward_terms(key_heads, value_heads, is_live, log_norm, row_delta):
        scores = masked_scores(key_heads, is_live)
        prob_bf = lax.optimization_barrier(
            jnp.exp(scores - log_norm[..., None]).astype(jnp.bfloat16)
        )
        grad_prob = jnp.einsum(
            "tcgd,ncd->cgtn", grad_heads, value_heads, preferred_element_type=jnp.float32
        )
        grad_score = (prob_bf.astype(jnp.float32) * (grad_prob - row_delta[..., None])).astype(
            jnp.bfloat16
        )
        return (prob_bf, grad_score)

    def key_side(prob_bf, grad_score, width):
        key_part = (
            jnp.einsum(
                "cgtn,tcgd->ncd", grad_score, query_heads, preferred_element_type=jnp.float32
            )
            * score_scale
        )
        value_part = jnp.einsum(
            "cgtn,tcgd->ncd", prob_bf, grad_heads, preferred_element_type=jnp.float32
        )
        return (key_part.reshape(width, kv_dev * DH), value_part.reshape(width, kv_dev * DH))

    def make_steps(log_norm, row_delta):

        def descend(carry, key_piece, first_row):
            piece_keys, piece_values = key_piece
            width = piece_keys.shape[0]
            is_live = live_of(first_row + jnp.arange(width, dtype=jnp.int32))

            def work(state):
                query_acc, key_acc, value_acc = state
                key_heads = piece_keys.reshape(width, kv_dev, DH)
                value_heads = piece_values.reshape(width, kv_dev, DH)
                prob_bf, grad_score = backward_terms(
                    key_heads, value_heads, is_live, log_norm, row_delta
                )
                query_acc = (
                    query_acc
                    + jnp.einsum(
                        "cgtn,ncd->cgtd", grad_score, key_heads, preferred_element_type=jnp.float32
                    )
                    * score_scale
                )
                key_part, value_part = key_side(prob_bf, grad_score, width)
                key_acc = lax.dynamic_update_slice_in_dim(key_acc, key_part, first_row, 0)
                value_acc = lax.dynamic_update_slice_in_dim(value_acc, value_part, first_row, 0)
                return (query_acc, key_acc, value_acc)

            return lax.cond(jnp.any(is_live), work, lambda state: state, carry)

        def descend_queries(carry, key_piece, first_row):
            piece_keys, piece_values = key_piece
            width = piece_keys.shape[0]
            is_live = live_of(first_row + jnp.arange(width, dtype=jnp.int32))

            def work(state):
                key_heads = piece_keys.reshape(width, kv_dev, DH)
                value_heads = piece_values.reshape(width, kv_dev, DH)
                prob_bf, grad_score = backward_terms(
                    key_heads, value_heads, is_live, log_norm, row_delta
                )
                return (
                    state[0]
                    + jnp.einsum(
                        "cgtn,ncd->cgtd", grad_score, key_heads, preferred_element_type=jnp.float32
                    )
                    * score_scale,
                )

            return lax.cond(jnp.any(is_live), work, lambda state: state, carry)

        return (descend, descend_queries)

    stat_shape = (kv_dev, group_size, tok_rows)
    initial_fwd = (
        jnp.full(stat_shape, very_negative, jnp.float32),
        jnp.zeros(stat_shape, jnp.float32),
        jnp.zeros(stat_shape + (DH,), jnp.float32),
    )
    query_zero = jnp.zeros(stat_shape + (DH,), jnp.float32)
    key_zero = jnp.zeros((all_tokens, kv_dev * DH), jnp.float32)
    whole_keys, whole_values = (
        lax.all_gather(key_rows, "seq", axis=0, tiled=True),
        lax.all_gather(value_rows, "seq", axis=0, tiled=True),
    )
    run_max, run_sum, run_acc = sweep_blocks(attend, initial_fwd, whole_keys, whole_values)
    attn_out = (run_acc / run_sum[..., None]).astype(jnp.bfloat16)
    log_norm = run_max + jnp.log(run_sum)
    grad_t = jnp.transpose(grad_heads, (1, 2, 0, 3)).astype(jnp.float32)
    row_delta = jnp.sum(grad_t * attn_out.astype(jnp.float32), axis=-1)
    log_norm, row_delta = (log_norm, row_delta)
    descend, descend_queries = make_steps(log_norm, row_delta)
    query_acc, key_acc, value_acc = sweep_blocks(
        descend, (query_zero, key_zero, key_zero), whole_keys, whole_values
    )
    key_grad, value_grad = (
        lax.psum_scatter(
            key_acc.astype(jnp.bfloat16), "seq", scatter_dimension=0, tiled=True
        ).astype(jnp.float32),
        lax.psum_scatter(
            value_acc.astype(jnp.bfloat16), "seq", scatter_dimension=0, tiled=True
        ).astype(jnp.float32),
    )
    query_grad = jnp.transpose(query_acc, (2, 0, 1, 3)).reshape(tok_rows, kv_dev * group_size * DH)
    return (
        query_grad.astype(jnp.bfloat16),
        key_grad.astype(jnp.bfloat16),
        value_grad.astype(jnp.bfloat16),
    )


def solution(mesh):
    placed = (
        P("seq", "heads"),
        P("seq", "heads"),
        P("seq", "heads"),
        P("seq", "heads"),
        P(("seq", "heads")),
        P(),
        P(),
        P(),
    )
    return jax.shard_map(
        shards,
        mesh=mesh,
        in_specs=placed,
        out_specs=(P("seq", "heads"), P("seq", "heads"), P("seq", "heads")),
        check_vma=False,
    )
```

profile of v0, /device:TPU:24, one launch (start us, length us, event | category | flops | bytes accessed | tf_op | source)
XLA Modules:
  0.0 478.6 jit_solution(1055615901845084737)
XLA Ops:
  7.2 0.7 all-gather.3.cloned.1.call-update
  8.0 0.7 all-gather.5.cloned.1.call-update
  8.7 0.8 fusion.70
  9.5 0.8 select_reduce_fusion.3
  10.4 78.4 %psum.7 = f32[8]{0:T(128)S(1)} all-reduce(f32[8]{0:T(128)S(1)} %select_reduce_fusion.3), channel_id=1, replica_groups=mesh['seq'=32,'heads'=8] {'seq','heads'}, use_global_device_ids=true, to_apply=%region_8.9 | all-reduce | flops 8 | bytes 64 | tf_op jit(solution)/shard_map/psum | solution.py:64
  88.8 1.1 copy.29
  90.1 1.1 copy.32
  91.2 0.8 convert_divide_fusion
  92.0 0.8 slice_bitcast_fusion.1
  92.8 0.2 select_reduce_fusion.1
  93.1 0.8 multiply_divide_fusion
  94.3 0.2 fusion.64
  94.5 36.7 %all-gather.5.cloned.1.call-done = bf16[4096,128]{1,0:T(8,128)(2,1)} async-done(((bf16[128,128]{1,0:T(8,128)(2,1)}), bf16[4096,128]{1,0:T(8,128)(2,1)}) %all-gather.5.cloned.1.call-update) | async-done | bytes 1048592 | tf_op jit(solution)/shard_map/all_gather | solution.py:200
  131.3 16.0 %while.40 = (s32[]{:T(128)}, f32[1,8,128]{2,1,0:T(8,128)S(1)}, f32[1,8,128]{2,1,0:T(8,128)S(1)}, f32[1,8,128,128]{3,2,1,0:T(8,128)S(1)}, bf16[128,32]{1,0:T(8,12...) while((s32[]{:T(128)}, f32[1,8,128]{2,1,0:T(8,128)S(1)}, ...), condition=%wide.region_6.7_spmd.clone, body=%wide.region_0.6_spmd.clone.sunk | while | flops 276868224 | bytes 8078633 | solution.py:46
  131.3 0.9 fusion.80
  132.8 3.4 conditional.6
  132.8 1.3 fusion.68
  134.2 1.6 fusion.10
  135.8 0.3 fusion.9
  136.2 0.9 fusion.80
  137.8 0.9 fusion.80
  139.4 0.9 fusion.80
  141.0 0.9 fusion.80
  142.6 0.9 fusion.80
  144.2 0.9 fusion.80
  145.7 0.9 fusion.80
  147.3 0.2 copy.33
  147.8 18.0 %while.41 = (s32[]{:T(128)}, f32[1,8,128,128]{3,2,1,0:T(8,128)S(1)}, bf16[4096,128]{1,0:T(8,128)(2,1)S(1)}, bf16[4096,128]{1,0:T(8,128)(2,1)S(1)}, bf16[128,32]{...) while((s32[]{:T(128)}, ...), condition=%wide.region_18.19_spmd.clone, body=%wide.region_14.18_spmd.clone.sunk | while | flops 680108160 | bytes 9463141 | solution.py:46
  147.8 0.9 fusion.82
  149.4 5.4 %conditional.7 = ((f32[1,8,128,128]{3,2,1,0:T(8,128)S(1)}, bf16[4096,128]{1,0:T(8,128)(2,1)S(1)}, bf16[4096,128]{1,0:T(8,128)(2,1)S(1)})) conditional(s32[]{:T(128)} %convert_element_type.146, (f32[1,8,128,128]{3,2,1,0:T(8,128)S(1)}, bf16[4096,128]{1,0:T(8,128)(2,1)S(1)}, bf16[4096,128]{1,0:T(8,128)(2,1)S(1)}) %tuple.142, ...), branch_computations={%region_16.16_spmd, %region_17.17_spmd} | conditional | flops 675610624 | bytes 9379926 | solution.py:165
  149.4 1.5 fusion.26
  150.9 1.3 fusion.27
  152.3 1.4 fusion.29
  153.7 0.5 fusion.32
  154.2 0.5 fusion.30
  154.8 0.9 fusion.82
  156.4 0.9 fusion.82
  157.9 0.9 fusion.82
  159.5 0.9 fusion.82
  161.1 0.9 fusion.82
  162.7 0.9 fusion.82
  164.3 0.9 fusion.82
  165.8 1.0 copy-done
  166.9 0.3 copy-done.1
  167.2 0.3 reduce-scatter.3.cloned.1.call-update
  167.7 0.8 copy.43
  168.4 159.3 %reduce-scatter.5.cloned.1.call-done = bf16[128,128]{1,0:T(8,128)(2,1)} async-done(((bf16[4096,128]{1,0:T(8,128)(2,1)}), bf16[128,128]{1,0:T(8,128)(2,1)}) %reduce-scatter.5.cloned.1.call-update) | async-done | bytes 32784 | tf_op jit(solution)/shard_map/reduce_scatter | solution.py:216
  327.8 144.3 %reduce-scatter.3.cloned.1.call-done = bf16[128,128]{1,0:T(8,128)(2,1)} async-done(((bf16[4096,128]{1,0:T(8,128)(2,1)}), bf16[128,128]{1,0:T(8,128)(2,1)}) %reduce-scatter.3.cloned.1.call-update) | async-done | bytes 32784 | tf_op jit(solution)/shard_map/reduce_scatter | solution.py:213
  (78 shorter events, 1.8 us)
Async XLA Ops:
  7.2 87.1 %copy-start.2 = (s32[32,32]{1,0:T(8,128)S(1)}, s32[32,32]{1,0:T(8,128)}, u32[]{:S(2)}) copy-start(s32[32,32]{1,0:T(8,128)} %param.21) | copy-start | bytes 12292
  7.2 87.3 %all-gather.3.cloned.1.call-start = ((), (), s32[]{:S(2)}) async-start(), calls=%async_computation.2 | async-start | bytes 1081344 | tf_op jit(solution)/shard_map/all_gather | solution.py:199
  7.9 123.3 %all-gather.5.cloned.1.call-start = ((), (), s32[]{:S(2)}) async-start(), calls=%async_computation.3 | async-start | bytes 1081344 | tf_op jit(solution)/shard_map/all_gather | solution.py:200
  8.7 319.1 %reduce-scatter.5.cloned.1.call-start = ((), (), s32[]{:S(2)}) async-start(), calls=%async_computation.5 | async-start | bytes 1081344 | tf_op jit(solution)/shard_map/reduce_scatter | solution.py:216
  165.8 1.0 copy-start
  165.8 1.4 copy-start.1
  166.9 305.1 %reduce-scatter.3.cloned.1.call-start = ((), (), s32[]{:S(2)}) async-start(), calls=%async_computation.4 | async-start | bytes 1081344 | tf_op jit(solution)/shard_map/reduce_scatter | solution.py:213
Sparse Core Ops, SparseCore 0:
  9.9 61.5 all-gather.2
  73.3 57.8 all-gather.4
  167.0 160.7 reduce-scatter.4
  330.8 141.1 reduce-scatter.2
where the time goes:
time: 479 us
  waiting for transfers between devices  342 us (71%)
  blocking collectives  78.4 us (16%)
  matrix products  22.8 us (5%)
  between operations  13.9 us (3%)
  loops' own time  10.9 us (2%)
  local copies, waits for them, and re-layouts  6.79 us (1%)
    reduce_scatter x1, waiting for transfers between devices, shards(): lax.psum_scatter(value_acc.astype(jnp.bfloat16), 'seq', scatter_dimension...  159 us
    reduce_scatter x1, waiting for transfers between devices, shards(): lax.psum_scatter(key_acc.astype(jnp.bfloat16), 'seq', scatter_dimension=0...  144 us
    psum x1, blocking collectives, shards(): lax.psum(response_sums(log_ratio, ratio_pos, starts, resp_ends), ('seq',...  78.4 us
    all_gather x1, waiting for transfers between devices, shards(): lax.all_gather(value_rows, 'seq', axis=0, tiled=True)  36.7 us
    dot_general x16, matrix products, live_of(): jnp.dot(row_table, col_select, preferred_element_type=jnp.float32) > 0.5  14.3 us
    another operation x2, loops' own time, sweep_blocks(): lax.fori_loop(0, whole_keys.shape[0] // block_rows, loop_body, initial)  10.6 us
  transfers between devices with their start and end apart: 4, of which 3 were waited for; matrix products, arithmetic and copies ran while one was open for 2% of the time, Pallas kernels for 0%

commit v1 on v0

v1 whole, which is shorter than its diff:
```python
import math

import jax
import jax.numpy as jnp
from jax import lax
from jax.experimental import pallas as pl
from jax.experimental.pallas import tpu as pltpu
from jax.sharding import PartitionSpec as P

DH=128; BLOCK=128; RESP=8; GROUP=8
ROWS=GROUP*BLOCK
scale=1.0/math.sqrt(DH)
c2=scale*math.log2(math.e)
f32=jnp.float32; bf=jnp.bfloat16
NT=(((1,),(1,)),((),())); NN=(((1,),(0,)),((),()))
NB=4
KC=NB*BLOCK
W=1024
NCH=32//NB

def attend_body(me, bounds, q_ref, do_ref, bufs, dq_ref, keep_ref, send_ref, kk, vv, q2, g2, pb, dp_s, mt, mx, sm, dl, acc, sem):
    prompt = bounds[0]//BLOCK
    start = jnp.int32(0)
    for r in range(RESP):
        lo=bounds[r]//BLOCK
        start=jnp.where(me>=lo, lo, start)
    live = me>=prompt
    n = jnp.where(live, prompt + me - start + 1, 0)
    chunks = (n+NB-1)//NB
    z=me//8; x=(me//2)%4; c=me%2
    def where_is(t):
        j=jnp.where(t<prompt, t, start+t-prompt)
        return lax.rem(lax.rem(j,2)+c,2)*4 + lax.rem(x-lax.rem(j//2,4)+4,4), lax.rem(z-j//8+4,4)
    def fetch(t,_):
        b,sz=where_is(t)
        rows=pl.ds(pl.multiple_of(t*BLOCK,BLOCK),BLOCK)
        for nb,buf in enumerate(bufs):
            @pl.when(b==nb)
            def _(buf=buf):
                pltpu.make_async_copy(buf.at[sz,0],kk.at[rows],sem.at[0,t]).start()
                pltpu.make_async_copy(buf.at[sz,1],vv.at[rows],sem.at[1,t]).start()
        return 0
    lax.fori_loop(0,n,fetch,0)
    for h in range(GROUP):
        q2[h*128:(h+1)*128,:]=q_ref[:,h*128:(h+1)*128]
        g2[h*128:(h+1)*128,:]=do_ref[:,h*128:(h+1)*128]
    keep_ref[...]=jnp.zeros_like(keep_ref)
    send_ref[...]=jnp.zeros_like(send_ref)
    mx[...]=jnp.full_like(mx,-1e30)
    sm[...]=jnp.zeros_like(sm); dl[...]=jnp.zeros_like(dl)
    acc[...]=jnp.zeros_like(acc)
    def pad(t,_):
        rows=pl.ds(pl.multiple_of(t*BLOCK,BLOCK),BLOCK)
        kk[rows,:]=jnp.zeros((BLOCK,DH),bf); vv[rows,:]=jnp.zeros((BLOCK,DH),bf)
        return 0
    lax.fori_loop(n,chunks*NB,pad,0)
    def land(t,_):
        rows=pl.ds(pl.multiple_of(t*BLOCK,BLOCK),BLOCK)
        pltpu.make_async_copy(bufs[0].at[0,0],kk.at[rows],sem.at[0,t]).wait()
        pltpu.make_async_copy(bufs[0].at[0,1],vv.at[rows],sem.at[1,t]).wait()
        return 0
    lax.fori_loop(0,n,land,0)
    def forward(i,masked):
        rows=pl.ds(pl.multiple_of(i*KC,KC),KC)
        k=kk[rows,:]; v=vv[rows,:]
        def tile(w,_):
            sl=slice(w*W,(w+1)*W)
            s=lax.dot_general(k,q2[sl,:],NT,preferred_element_type=f32)*c2
            if masked:
                key=lax.broadcasted_iota(jnp.int32,(KC,W),0)+i*KC-(n-1)*BLOCK
                col=lax.rem(lax.broadcasted_iota(jnp.int32,(KC,W),1),BLOCK)
                s=jnp.where(key<=col,s,-jnp.inf)
            old=mx[0:1,sl]
            new=jnp.maximum(old,jnp.max(jnp.max(s.reshape(KC//8,8,W),axis=0),axis=0,keepdims=True))
            p=jnp.exp2(s-new)
            dp=lax.dot_general(v,g2[sl,:],NT,preferred_element_type=f32)
            fade=jnp.exp2(old-new)
            sm[:,sl]=sm[:,sl]*fade+jnp.sum(p.reshape(KC//8,8,W),axis=0)
            dl[:,sl]=dl[:,sl]*fade+jnp.sum((p*dp).reshape(KC//8,8,W),axis=0)
            mx[0:1,sl]=new
            mt[i,0:1,sl]=new
            pb[rows,sl]=p.astype(bf)
            dp_s[rows,sl]=dp.astype(dp_s.dtype)
            return 0
        [tile(w,0) for w in range(ROWS//W)]
    def step(i,_):
        forward(i,False)
        return 0
    lax.fori_loop(0,chunks-1,step,0)
    @pl.when(live)
    def _():
        forward(chunks-1,True)
        inv=1.0/jnp.sum(sm[...],axis=0,keepdims=True)
        dl[0:1,:]=jnp.sum(dl[...],axis=0,keepdims=True)*inv
        sm[0:1,:]=inv
    def backward(i,_):
        rows=pl.ds(pl.multiple_of(i*KC,KC),KC)
        kt=kk[rows,:].T
        def tile(w,carry):
            dk,dv=carry
            sl=slice(w*W,(w+1)*W)
            f=sm[0:1,sl]*jnp.exp2(mt[i,0:1,sl]-mx[0:1,sl])
            p=pb[rows,sl].astype(f32)*f
            g=(p*(dp_s[rows,sl].astype(f32)-dl[0:1,sl])).astype(bf)
            dk+=lax.dot_general(g,q2[sl,:],NN,preferred_element_type=f32)
            dv+=lax.dot_general(p.astype(bf),g2[sl,:],NN,preferred_element_type=f32)
            acc[:,sl]+=lax.dot_general(kt,g,NN,preferred_element_type=f32)
            return dk,dv
        zero=jnp.zeros((KC,DH),f32)
        dk,dv=zero,zero
        for w in range(ROWS//W): dk,dv=tile(w,(dk,dv))
        for u in range(NB):
            t=i*NB+u
            b,sz=where_is(t)
            crel=b//4; sx=lax.rem(b,4)
            a=(dk[u*128:(u+1)*128]*scale).astype(bf); e=dv[u*128:(u+1)*128].astype(bf)
            @pl.when((t<n)&(crel==0))
            def _():
                keep_ref[sx,sz,0]=a; keep_ref[sx,sz,1]=e
            @pl.when((t<n)&(crel==1))
            def _():
                send_ref[sx,sz,0]=a; send_ref[sx,sz,1]=e
        return 0
    lax.fori_loop(0,chunks,backward,0)
    for h in range(GROUP):
        sl=slice(h*128,(h+1)*128)
        dq_ref[:,sl]=(acc[:,sl]*scale).T

DPT=f32
def attn_call(me_fn, bounds, q, do, bufs, me=None):
    nb=len(bufs)
    def kern(*refs):
        if me is None: bnd=refs[0]; rest=refs[1:]; mv=me_fn()
        else: mr,bnd=refs[0],refs[1]; rest=refs[2:]; mv=mr[0]
        q_ref,do_ref=rest[:2]; bu=rest[2:2+nb]
        attend_body(mv,bnd,q_ref,do_ref,bu,*rest[2+nb:])
    S=pl.BlockSpec(memory_space=pltpu.SMEM); V=pl.BlockSpec(memory_space=pltpu.VMEM); A=pl.BlockSpec(memory_space=pl.ANY)
    pre=[bounds] if me is None else [me,bounds]
    return pl.pallas_call(kern,
        out_shape=(jax.ShapeDtypeStruct((BLOCK,ROWS),f32),jax.ShapeDtypeStruct((4,4,2,128,128),bf),jax.ShapeDtypeStruct((4,4,2,128,128),bf)),
        in_specs=[S]*len(pre)+[V,V]+[A]*nb, out_specs=(V,V,V),
        scratch_shapes=[pltpu.VMEM((32*BLOCK,DH),bf),pltpu.VMEM((32*BLOCK,DH),bf),pltpu.VMEM((ROWS,DH),bf),pltpu.VMEM((ROWS,DH),bf),
            pltpu.VMEM((32*BLOCK,ROWS),bf),pltpu.VMEM((32*BLOCK,ROWS),DPT),
            pltpu.VMEM((NCH,8,ROWS),f32),
            pltpu.VMEM((8,ROWS),f32),pltpu.VMEM((8,ROWS),f32),pltpu.VMEM((8,ROWS),f32),pltpu.VMEM((DH,ROWS),f32),
            pltpu.SemaphoreType.DMA((2,32))],
        compiler_params=pltpu.CompilerParams(vmem_limit_bytes=48*2**20),
        cost_estimate=pl.CostEstimate(flops=10**10,bytes_accessed=5*2**20,transcendentals=2**22),
    )(*pre,q,do,*bufs)

PAIRS = 8
SLICE_BYTES = 48 * 2**20


def seq_perm(move):
    pairs = []
    for z in range(4):
        for x in range(4):
            for c in range(2):
                nz, nx, nc = move(z, x, c)
                pairs.append(((z * 4 + x) * 2 + c, (nz * 4 + nx) * 2 + nc))
    return pairs


CORE = seq_perm(lambda z, x, c: (z, x, 1 - c))
X_UP = [seq_perm(lambda z, x, c, s=s: (z, (x + s) % 4, c)) for s in range(4)]
X_DOWN = [seq_perm(lambda z, x, c, s=s: (z, (x - s) % 4, c)) for s in range(4)]
X_FLIP = [seq_perm(lambda z, x, c, s=s: (z, x ^ s, c)) for s in (1, 2)]
Z_UP = [seq_perm(lambda z, x, c, s=s: ((z + s) % 4, x, c)) for s in range(4)]
Z_DOWN = [seq_perm(lambda z, x, c, s=s: ((z - s) % 4, x, c)) for s in range(4)]


def head_perm(bit):
    return [(h, h ^ bit) for h in range(8)]


def pack(keys, values, ratios):
    def kern(k_ref, v_ref, ratio_ref, out_ref):
        total = ratio_ref[0]
        for t in range(1, ratios.shape[0]):
            total = total + ratio_ref[t]
        whole = jnp.full((16, DH), total, f32)
        hi = whole.astype(bf).astype(f32)
        mid = (whole - hi).astype(bf).astype(f32)
        low = whole - hi - mid
        row = lax.broadcasted_iota(jnp.int32, (16, DH), 0)
        ride = jnp.where(row == 0, hi, jnp.where(row == 1, mid, jnp.where(row == 2, low, 0.0)))
        out_ref[:BLOCK, :] = k_ref[...]
        out_ref[BLOCK : 2 * BLOCK, :] = v_ref[...]
        out_ref[2 * BLOCK :, :] = ride.astype(bf)

    S = pl.BlockSpec(memory_space=pltpu.SMEM)
    V = pl.BlockSpec(memory_space=pltpu.VMEM)
    return pl.pallas_call(
        kern,
        out_shape=jax.ShapeDtypeStruct((2 * BLOCK + 16, DH), bf),
        in_specs=[V, V, S],
        out_specs=V,
    )(keys, values, ratios)


def unpack(bounds, packets):
    def kern(b_ref, p0, p1, p2, p3, col_ref, sums_ref):
        me = lax.axis_index("seq")
        row = lax.broadcasted_iota(jnp.int32, (RESP, DH), 0)
        sums = jnp.zeros((RESP, DH), f32)
        for s, packet in enumerate((p0, p1, p2, p3)):
            col_ref[s, 0] = packet[:BLOCK, :]
            col_ref[s, 1] = packet[BLOCK : 2 * BLOCK, :]
            first = (lax.rem(me // 8 - s + 4, 4) * 8 + lax.rem(me, 8)) * BLOCK
            resp = jnp.int32(-1)
            for r in range(RESP):
                resp = resp + (first >= b_ref[r]).astype(jnp.int32)
            part = jnp.sum(packet[2 * BLOCK :, :].astype(f32), axis=0, keepdims=True)
            sums = sums + jnp.where(row == resp, part, 0.0)
        sums_ref[...] = sums

    S = pl.BlockSpec(memory_space=pltpu.SMEM)
    V = pl.BlockSpec(memory_space=pltpu.VMEM)
    return pl.pallas_call(
        kern,
        out_shape=(
            jax.ShapeDtypeStruct((4, 2, BLOCK, DH), bf),
            jax.ShapeDtypeStruct((RESP, DH), f32),
        ),
        in_specs=[S, V, V, V, V],
        out_specs=(V, V),
    )(bounds, *packets)


def core_add(sums, bounds, pairs, keep, got):
    def kern(sums_ref, b_ref, p_ref, keep_ref, got_ref, o0, o1, o2, o3, w_ref, mean, coef):
        me = lax.axis_index("seq")
        for r in range(RESP):
            mean[r] = sums_ref[r, 0] / (b_ref[r + 1] - b_ref[r]).astype(f32)
            coef[r] = 0.0
        for p in range(PAIRS):
            win, lose = p_ref[p, 0], p_ref[p, 1]
            resid = mean[win] - mean[lose] - 1.0
            coef[win] = coef[win] + resid
            coef[lose] = coef[lose] - resid

        def weight(block):
            first = block * BLOCK
            w = jnp.float32(0.0)
            for r in range(RESP):
                inside = (first >= b_ref[r]) & (first < b_ref[r + 1])
                length = (b_ref[r + 1] - b_ref[r]).astype(f32)
                w = jnp.where(inside, 512.0 * (2.0 / PAIRS * coef[r] / length), w)
            return w

        mine = weight(me)
        theirs = weight(me + 1 - 2 * lax.rem(me, 2))
        w_ref[...] = jnp.full(w_ref.shape, mine, f32)
        for sx, out in enumerate((o0, o1, o2, o3)):
            for sz in range(4):
                for kvi in range(2):
                    out[sz, kvi] = (
                        keep_ref[sx, sz, kvi].astype(f32) * mine
                        + got_ref[sx, sz, kvi].astype(f32) * theirs
                    ).astype(bf)

    S = pl.BlockSpec(memory_space=pltpu.SMEM)
    V = pl.BlockSpec(memory_space=pltpu.VMEM)
    slot = jax.ShapeDtypeStruct((4, 2, 128, 128), bf)
    return pl.pallas_call(
        kern,
        out_shape=(slot, slot, slot, slot, jax.ShapeDtypeStruct((8, 128), f32)),
        in_specs=[S, S, S, V, V],
        out_specs=(V,) * 5,
        scratch_shapes=[pltpu.SMEM((RESP,), f32), pltpu.SMEM((RESP,), f32)],
        compiler_params=pltpu.CompilerParams(vmem_limit_bytes=SLICE_BYTES),
    )(sums, bounds, pairs, keep, got)


def x_add(a0, a1, a2, a3):
    def kern(i0, i1, i2, i3, *outs):
        for sz in range(4):
            for kvi in range(2):
                outs[sz][kvi] = (
                    (i0[sz, kvi].astype(f32) + i1[sz, kvi].astype(f32))
                    + (i2[sz, kvi].astype(f32) + i3[sz, kvi].astype(f32))
                ).astype(bf)

    V = pl.BlockSpec(memory_space=pltpu.VMEM)
    slot = jax.ShapeDtypeStruct((2, 128, 128), bf)
    return pl.pallas_call(
        kern,
        out_shape=(slot,) * 4,
        in_specs=[V] * 4,
        out_specs=(V,) * 4,
        compiler_params=pltpu.CompilerParams(vmem_limit_bytes=SLICE_BYTES),
    )(a0, a1, a2, a3)


def z_add(a0, a1, a2, a3):
    def kern(i0, i1, i2, i3, dk, dv):
        for kvi, out in enumerate((dk, dv)):
            out[...] = (
                (i0[kvi].astype(f32) + i1[kvi].astype(f32))
                + (i2[kvi].astype(f32) + i3[kvi].astype(f32))
            ).astype(bf)

    V = pl.BlockSpec(memory_space=pltpu.VMEM)
    out = jax.ShapeDtypeStruct((BLOCK, DH), bf)
    return pl.pallas_call(
        kern,
        out_shape=(out, out),
        in_specs=[V] * 4,
        out_specs=(V, V),
    )(a0, a1, a2, a3)


def shards(query_rows, key_rows, value_rows, out_grad, log_ratio, block_mask, bounds, pairs):
    def seq(v, perm):
        return lax.ppermute(v, "seq", perm)

    packet = pack(key_rows, value_rows, log_ratio)
    by_z = [packet] + [seq(packet, Z_UP[s]) for s in (1, 2, 3)]
    column, sums = unpack(bounds, by_z)
    by_x = [column] + [seq(column, X_UP[s]) for s in (1, 2, 3)]
    own_other = seq(column, CORE)
    for bit in (1, 2, 4):
        sums = sums + lax.ppermute(sums, "heads", head_perm(bit))
    sums, by_x, own_other = lax.optimization_barrier((sums, by_x, own_other))
    bufs = by_x + [own_other] + [seq(b, CORE) for b in by_x[1:]]
    sums = sums + seq(sums, CORE)
    sums = sums + seq(sums, X_FLIP[0])
    sums, bufs = lax.optimization_barrier((sums, bufs))
    dq, keep, send = attn_call(lambda: lax.axis_index("seq"), bounds, query_rows, out_grad, bufs)
    sums = sums + seq(sums, X_FLIP[1])
    got = seq(send, CORE)
    *by_shift, weight = core_add(sums, bounds, pairs, keep, got)
    summed = x_add(by_shift[0], *[seq(by_shift[s], X_DOWN[s]) for s in (1, 2, 3)])
    query_grad = (dq * weight[0, 0]).astype(bf)
    key_grad, value_grad = z_add(summed[0], *[seq(summed[s], Z_DOWN[s]) for s in (1, 2, 3)])
    return query_grad, key_grad, value_grad


def solution(mesh):
    whole = P("seq", "heads")
    return jax.shard_map(
        shards,
        mesh=mesh,
        in_specs=(whole, whole, whole, whole, P(("seq", "heads")), P(), P(), P()),
        out_specs=(whole, whole, whole),
        check_vma=False,
    )
```

time: 479 us -> 89.8 us (0.19)
  waiting for transfers between devices: 342 us -> 37.5 us
  blocking collectives: 78.4 us -> 0 us
  starting transfers between devices: 0.16 us -> 36 us
  matrix products: 22.8 us -> 0 us
  between operations: 13.9 us -> 0.79 us
  loops' own time: 10.9 us -> 0 us
  Pallas kernels: 0 us -> 8.89 us
    reduce_scatter x2 -> x0, waiting for transfers between devices: 304 us -> none  [the longest x1 159 us: shards(): lax.psum_scatter(value_acc.astype(jnp.bfloat16), 'seq', scatter_dimension...]
    psum x1 -> x0, blocking collectives: 78.4 us -> none  [shards(): lax.psum(response_sums(log_ratio, ratio_pos, starts, resp_ends), ('seq',...]
    ppermute x0 -> x23, waiting for transfers between devices: none -> 37.5 us  [the longest x20 28.9 us: seq(): return lax.ppermute(v, 'seq', perm)]
    all_gather x2 -> x0, waiting for transfers between devices: 36.7 us -> none  [the longest x1 36.7 us: shards(): lax.all_gather(value_rows, 'seq', axis=0, tiled=True)]
    ppermute x0 -> x23, starting transfers between devices: none -> 36 us  [the longest x20 28 us: seq(): return lax.ppermute(v, 'seq', perm)]
    dot_general x24 -> x0, matrix products: 22.8 us -> none  [the longest x16 14.3 us: live_of(): jnp.dot(row_table, col_select, preferred_element_type=jnp.float32) > 0.5]
    another operation x18 -> x0, loops' own time: 10.9 us -> none  [the longest x2 10.6 us: sweep_blocks(): lax.fori_loop(0, whole_keys.shape[0] // block_rows, loop_body, initial)]
    pallas_call x0 -> x6, Pallas kernels: none -> 8.89 us  [the longest x1 2.78 us: attn_call(): pl.pallas_call(kern, out_shape=(jax.ShapeDtypeStruct((BLOCK, ROWS), f32),...]
  transfers between devices with their start and end apart: 4 -> 23, of which waited for: 3 -> 14; matrix products, arithmetic and copies ran while one was open for 2% -> 3% of each run, Pallas kernels for 0% -> 0%
where the time goes in v1:
time: 89.8 us; the launch traced here: 89.3 us
  waiting for transfers between devices  37.5 us (42%)
  starting transfers between devices  36 us (40%)
  Pallas kernels  8.89 us (10%)
  local copies, waits for them, and re-layouts  4.03 us (4%)
  other arithmetic  2.09 us (2%)
    ppermute x20, waiting for transfers between devices, seq(): return lax.ppermute(v, 'seq', perm)  28.9 us
    ppermute x20, starting transfers between devices, seq(): return lax.ppermute(v, 'seq', perm)  28 us
    ppermute x3, waiting for transfers between devices, shards(): sums = sums + lax.ppermute(sums, 'heads', head_perm(bit))  8.53 us
    ppermute x3, starting transfers between devices, shards(): sums = sums + lax.ppermute(sums, 'heads', head_perm(bit))  8.08 us
    unnamed x25, local copies, waits for them, and re-layouts  3.51 us
    pallas_call x1, Pallas kernels, attn_call(): pl.pallas_call(kern, out_shape=(jax.ShapeDtypeStruct((BLOCK, ROWS), f32),...  2.78 us
  transfers between devices with their start and end apart: 23, of which 14 were waited for; matrix products, arithmetic and copies ran while one was open for 3% of the time, Pallas kernels for 0%

profile of v1, /device:TPU:24, one launch (start us, length us, event | category | flops | bytes accessed | tf_op | source)
XLA Modules:
  0.0 89.3 jit_solution(17625420611277183952)
XLA Ops:
  0.6 1.5 %shard_map.94.p0 = bf16[272,128]{1,0:T(8,128)(2,1)} custom-call(bf16[128,128]{1,0:T(8,128)(2,1)} %k_ref.1, bf16[128,128]{1,0:T(8,128)(2,1)} %v_ref.1, f32[16]{0:T(128)} %ratio_ref.1), custom_call_target="tpu_custom_call" | custom-call | tf_op jit(solution)/shard_map/pallas_call | solution.py:194
  2.1 1.9 %collective-permute-start = (bf16[272,128]{1,0:T(8,128)(2,1)}, bf16[272,128]{1,0:T(8,128)(2,1)S(1)}, u32[]{:S(2)}, u32[]{:S(2)}) collective-permute-start(bf16[272,128]{1,0:T(8,128)(2,1)} %shard_map.94.p0), channel_id=1, source_target_pairs={{0,64},{8,72},{16,80},{24,88},{32,96},{40,104},{48,112},{56,120},{... | collective-permute-start | bytes 208904 | tf_op jit(solution)/shard_map/ppermute | solution.py:316
  4.0 3.3 %collective-permute-start.1 = (bf16[272,128]{1,0:T(8,128)(2,1)}, bf16[272,128]{1,0:T(8,128)(2,1)S(1)}, u32[]{:S(2)}, u32[]{:S(2)}) collective-permute-start(bf16[272,128]{1,0:T(8,128)(2,1)} %shard_map.94.p0), channel_id=1, source_target_pairs={{0,128},{8,136},{16,144},{24,152},{32,160},{40,168},{48,176},{56,1... | collective-permute-start | bytes 208904 | tf_op jit(solution)/shard_map/ppermute | solution.py:316
  7.3 1.0 %collective-permute-start.2 = (bf16[272,128]{1,0:T(8,128)(2,1)}, bf16[272,128]{1,0:T(8,128)(2,1)S(1)}, u32[]{:S(2)}, u32[]{:S(2)}) collective-permute-start(bf16[272,128]{1,0:T(8,128)(2,1)} %shard_map.94.p0), channel_id=1, source_target_pairs={{0,192},{8,200},{16,208},{24,216},{32,224},{40,232},{48,240},{56,2... | collective-permute-start | bytes 208904 | tf_op jit(solution)/shard_map/ppermute | solution.py:316
  8.3 1.5 %collective-permute-done.p1 = bf16[272,128]{1,0:T(8,128)(2,1)S(1)} collective-permute-done((bf16[272,128]{1,0:T(8,128)(2,1)}, bf16[272,128]{1,0:T(8,128)(2,1)S(1)}, u32[]{:S(2)}, u32[]{:S(2)}) %collective-permute-start) | collective-permute-done | bytes 69664 | tf_op jit(solution)/shard_map/ppermute | solution.py:316
  9.8 2.4 %collective-permute-done.1.p2 = bf16[272,128]{1,0:T(8,128)(2,1)S(1)} collective-permute-done((bf16[272,128]{1,0:T(8,128)(2,1)}, bf16[272,128]{1,0:T(8,128)(2,1)S(1)}, u32[]{:S(2)}, u32[]{:S(2)}) %collective-permute-start.1) | collective-permute-done | bytes 69664 | tf_op jit(solution)/shard_map/ppermute | solution.py:316
  12.2 0.4 collective-permute-done.2.p3
  12.6 0.3 copy-done.6
  12.9 0.6 copy-done.7
  13.5 1.7 %shard_map.95 = (bf16[4,2,128,128]{3,2,1,0:T(8,128)(2,1)}, f32[8,128]{1,0:T(8,128)}) custom-call(s32[9]{0:T(128)} %b_ref.3, bf16[272,128]{1,0:T(8,128)(2,1)} %shard_map.94.p0, bf16[272,128]{1,0:T(8,128)(2,1)} %copy-done.5, bf16[272,128]{1,0:T(8,128)(2,1)} %copy-done.6, bf16[272,128]{1,0:T(8,128)(2,1)} %copy-done.7), custom_call_target="tpu_custom_call" | custom-call | tf_op jit(solution)/shard_map/pallas_call | solution.py:220
  15.2 1.5 %collective-permute-start.6 = (bf16[4,2,128,128]{3,2,1,0:T(8,128)(2,1)}, bf16[4,2,128,128]{3,2,1,0:T(8,128)(2,1)S(1)}, u32[]{:S(2)}, u32[]{:S(2)}) collective-permute-start(bf16[4,2,128,128]{3,2,1,0:T(8,128)(2,1)} %get-tuple-element.42.refs_3_), channel_id=1, source_target_pairs={{0,16},{8,24},{16,32},{24,40},{32,48},{40,56},{48,0},{56,8},{64,80... | collective-permute-start | bytes 786440 | tf_op jit(solution)/shard_map/ppermute | solution.py:316
  16.7 2.7 %collective-permute-start.7 = (bf16[4,2,128,128]{3,2,1,0:T(8,128)(2,1)}, bf16[4,2,128,128]{3,2,1,0:T(8,128)(2,1)S(1)}, u32[]{:S(2)}, u32[]{:S(2)}) collective-permute-start(bf16[4,2,128,128]{3,2,1,0:T(8,128)(2,1)} %get-tuple-element.42.refs_3_), channel_id=1, source_target_pairs={{0,32},{8,40},{16,48},{24,56},{32,0},{40,8},{48,16},{56,24},{64,96... | collective-permute-start | bytes 786440 | tf_op jit(solution)/shard_map/ppermute | solution.py:316
  19.4 1.4 %collective-permute-start.8 = (bf16[4,2,128,128]{3,2,1,0:T(8,128)(2,1)}, bf16[4,2,128,128]{3,2,1,0:T(8,128)(2,1)S(1)}, u32[]{:S(2)}, u32[]{:S(2)}) collective-permute-start(bf16[4,2,128,128]{3,2,1,0:T(8,128)(2,1)} %get-tuple-element.42.refs_3_), channel_id=1, source_target_pairs={{0,48},{8,56},{16,0},{24,8},{32,16},{40,24},{48,32},{56,40},{64,11... | collective-permute-start | bytes 786440 | tf_op jit(solution)/shard_map/ppermute | solution.py:316
  20.8 0.7 collective-permute-start.3
  21.6 3.1 %collective-permute-done.3 = f32[8,128]{1,0:T(8,128)S(1)} collective-permute-done((f32[8,128]{1,0:T(8,128)}, f32[8,128]{1,0:T(8,128)S(1)}, u32[]{:S(2)}, u32[]{:S(2)}) %collective-permute-start.3) | collective-permute-done | bytes 4128 | tf_op jit(solution)/shard_map/ppermute | solution.py:324
  24.7 0.7 add.18
  25.4 1.2 %collective-permute-start.4 = (f32[8,128]{1,0:T(8,128)S(1)}, f32[8,128]{1,0:T(8,128)S(1)}, u32[]{:S(2)}, u32[]{:S(2)}) collective-permute-start(f32[8,128]{1,0:T(8,128)S(1)} %add.18), channel_id=1, source_target_pairs={{0,2},{1,3},{2,0},{3,1},{4,6},{5,7},{6,4},{7,5},{8,10},{9,11},{10,... | collective-permute-start | bytes 12296 | tf_op jit(solution)/shard_map/ppermute | solution.py:324
  26.6 3.9 %collective-permute-done.4 = f32[8,128]{1,0:T(8,128)S(1)} collective-permute-done((f32[8,128]{1,0:T(8,128)S(1)}, f32[8,128]{1,0:T(8,128)S(1)}, u32[]{:S(2)}, u32[]{:S(2)}) %collective-permute-start.4) | collective-permute-done | bytes 4128 | tf_op jit(solution)/shard_map/ppermute | solution.py:324
  30.5 6.1 %collective-permute-start.5 = (f32[8,128]{1,0:T(8,128)S(1)}, f32[8,128]{1,0:T(8,128)S(1)}, u32[]{:S(2)}, u32[]{:S(2)}) collective-permute-start(f32[8,128]{1,0:T(8,128)S(1)} %add.19), channel_id=1, source_target_pairs={{0,4},{1,5},{2,6},{3,7},{4,0},{5,1},{6,2},{7,3},{8,12},{9,13},{10,... | collective-permute-start | bytes 12296 | tf_op jit(solution)/shard_map/ppermute | solution.py:324
  36.6 1.6 %collective-permute-done.5 = f32[8,128]{1,0:T(8,128)S(1)} collective-permute-done((f32[8,128]{1,0:T(8,128)S(1)}, f32[8,128]{1,0:T(8,128)S(1)}, u32[]{:S(2)}, u32[]{:S(2)}) %collective-permute-start.5) | collective-permute-done | bytes 4128 | tf_op jit(solution)/shard_map/ppermute | solution.py:324
  38.2 0.1 collective-permute-start.12
  38.3 0.5 collective-permute-start.13
  38.8 0.1 collective-permute-start.14
  38.9 0.4 collective-permute-start.10
  39.3 1.3 %collective-permute-done.10 = f32[8,128]{1,0:T(8,128)S(1)} collective-permute-done((f32[8,128]{1,0:T(8,128)S(1)}, f32[8,128]{1,0:T(8,128)S(1)}, u32[]{:S(2)}, u32[]{:S(2)}) %collective-permute-start.10) | collective-permute-done | bytes 4128 | tf_op jit(solution)/shard_map/ppermute | solution.py:316
  40.6 0.6 collective-permute-start.11
  41.2 3.0 %collective-permute-done.11 = f32[8,128]{1,0:T(8,128)S(1)} collective-permute-done((f32[8,128]{1,0:T(8,128)S(1)}, f32[8,128]{1,0:T(8,128)S(1)}, u32[]{:S(2)}, u32[]{:S(2)}) %collective-permute-start.11) | collective-permute-done | bytes 4128 | tf_op jit(solution)/shard_map/ppermute | solution.py:316
  44.2 0.9 %copy-done.3 = bf16[128,1024]{1,0:T(8,128)(2,1)S(1)} copy-done((bf16[128,1024]{1,0:T(8,128)(2,1)S(1)}, bf16[128,1024]{1,0:T(8,128)(2,1)}, u32[]{:S(2)}) %copy-start.3) | copy-done | bytes 262168
  45.2 0.9 %copy-done.4 = bf16[4,2,128,128]{3,2,1,0:T(8,128)(2,1)S(1)} copy-done((bf16[4,2,128,128]{3,2,1,0:T(8,128)(2,1)S(1)}, bf16[4,2,128,128]{3,2,1,0:T(8,128)(2,1)}, u32[]{:S(2)}) %copy-start.4) | copy-done | bytes 262168
  46.1 2.8 %shard_map.96 = (f32[128,1024]{1,0:T(8,128)S(1)}, bf16[4,4,2,128,128]{4,3,2,1,0:T(8,128)(2,1)S(1)}, bf16[4,4,2,128,128]{4,3,2,1,0:T(8,128)(2,1)}) custom-call(s32[9]{0:T(128)S(1)} %copy-done.1, bf16[128,1024]{1,0:T(8,128)(2,1)S(1)} %copy-done.2, bf16[128,1024]{1,0:T(8,128)(2,1)S(1)} %copy-done.3, bf16[4,2,128,128]{3,2,1,0:T(8,128)(2,1)S(1)} %copy-done.4, ...), custom_call_target="tpu_custom_call" | custom-call | flops 10000000000 | bytes 5242880 | tf_op jit(solution)/shard_map/pallas_call | solution.py:139
  48.9 0.1 collective-permute-start.16
  49.0 0.6 collective-permute-start.15
  49.7 4.5 %collective-permute-done.15 = f32[8,128]{1,0:T(8,128)S(1)} collective-permute-done((f32[8,128]{1,0:T(8,128)S(1)}, f32[8,128]{1,0:T(8,128)S(1)}, u32[]{:S(2)}, u32[]{:S(2)}) %collective-permute-start.15) | collective-permute-done | bytes 4128 | tf_op jit(solution)/shard_map/ppermute | solution.py:316
  54.2 1.2 %shard_map.97 = (bf16[4,2,128,128]{3,2,1,0:T(8,128)(2,1)S(1)}, bf16[4,2,128,128]{3,2,1,0:T(8,128)(2,1)S(1)}, bf16[4,2,128,128]{3,2,1,0:T(8,128)(2,1)S(1)}, bf16[...) custom-call(f32[8,128]{1,0:T(8,128)S(1)} %add.23.sums_ref, s32[9]{0:T(128)S(1)} %copy-done.1, s32[8,2]{1,0:T(8,128)S(1)} %copy.10.p_ref, ...), custom_call_target="tpu_custom_call" | custom-call | tf_op jit(solution)/shard_map/pallas_call | solution.py:266
  55.4 0.1 collective-permute-start.17
  55.5 2.6 %collective-permute-start.18 = (bf16[4,2,128,128]{3,2,1,0:T(8,128)(2,1)S(1)}, bf16[4,2,128,128]{3,2,1,0:T(8,128)(2,1)S(1)}, u32[]{:S(2)}, u32[]{:S(2)}) collective-permute-start(bf16[4,2,128,128]{3,2,1,0:T(8,128)(2,1)S(1)} %get-tuple-element.57), channel_id=1, source_target_pairs={{0,32},{8,40},{16,48},{24,56},{32,0},{40,8},{48,16},{56,24},{64,96... | collective-permute-start | bytes 786440 | tf_op jit(solution)/shard_map/ppermute | solution.py:316
  58.2 0.5 slice.3
  58.7 6.1 %collective-permute-done.17.i1 = bf16[4,2,128,128]{3,2,1,0:T(8,128)(2,1)S(1)} collective-permute-done((bf16[4,2,128,128]{3,2,1,0:T(8,128)(2,1)S(1)}, bf16[4,2,128,128]{3,2,1,0:T(8,128)(2,1)S(1)}, u32[]{:S(2)}, u32[]{:S(2)}) %collective-permute-start.17) | collective-permute-done | bytes 262176 | tf_op jit(solution)/shard_map/ppermute | solution.py:316
  64.8 1.6 %collective-permute-done.18.i2 = bf16[4,2,128,128]{3,2,1,0:T(8,128)(2,1)S(1)} collective-permute-done((bf16[4,2,128,128]{3,2,1,0:T(8,128)(2,1)S(1)}, bf16[4,2,128,128]{3,2,1,0:T(8,128)(2,1)S(1)}, u32[]{:S(2)}, u32[]{:S(2)}) %collective-permute-start.18) | collective-permute-done | bytes 262176 | tf_op jit(solution)/shard_map/ppermute | solution.py:316
  66.4 3.8 %collective-permute-done.19.i3 = bf16[4,2,128,128]{3,2,1,0:T(8,128)(2,1)S(1)} collective-permute-done((bf16[4,2,128,128]{3,2,1,0:T(8,128)(2,1)S(1)}, bf16[4,2,128,128]{3,2,1,0:T(8,128)(2,1)S(1)}, u32[]{:S(2)}, u32[]{:S(2)}) %collective-permute-start.19) | collective-permute-done | bytes 262176 | tf_op jit(solution)/shard_map/ppermute | solution.py:316
  70.2 0.1 shard_map.98
  70.4 10.3 %collective-permute-start.20 = (bf16[2,128,128]{2,1,0:T(8,128)(2,1)S(1)}, bf16[2,128,128]{2,1,0:T(8,128)(2,1)S(1)}, u32[]{:S(2)}, u32[]{:S(2)}) collective-permute-start(bf16[2,128,128]{2,1,0:T(8,128)(2,1)S(1)} %get-tuple-element.60), channel_id=1, source_target_pairs={{0,192},{8,200},{16,208},{24,216},{32,224},{40,232},{48,240},{56,2... | collective-permute-start | bytes 196616 | tf_op jit(solution)/shard_map/ppermute | solution.py:316
  80.7 0.7 collective-permute-start.22
  81.4 1.4 %multiply_convert_fusion = bf16[128,1024]{1,0:T(8,128)(2,1)} fusion(f32[128,1024]{1,0:T(8,128)S(1)} %get-tuple-element.50, f32[]{:T(128)} %bitcast), kind=kLoop, calls=%fused_computation | loop fusion | flops 262144 | bytes 786436 | tf_op jit(solution)/shard_map/convert_element_type | solution.py:335
  82.8 0.4 collective-permute-done.20.i1
  83.2 3.9 %collective-permute-done.21.i2 = bf16[2,128,128]{2,1,0:T(8,128)(2,1)S(1)} collective-permute-done((bf16[2,128,128]{2,1,0:T(8,128)(2,1)S(1)}, bf16[2,128,128]{2,1,0:T(8,128)(2,1)S(1)}, u32[]{:S(2)}, u32[]{:S(2)}) %collective-permute-start.21) | collective-permute-done | bytes 65568 | tf_op jit(solution)/shard_map/ppermute | solution.py:316
  87.1 0.6 copy-done.9
  87.7 1.6 %shard_map.99 = (bf16[128,128]{1,0:T(8,128)(2,1)}, bf16[128,128]{1,0:T(8,128)(2,1)}) custom-call(bf16[2,128,128]{2,1,0:T(8,128)(2,1)} %copy-done, bf16[2,128,128]{2,1,0:T(8,128)(2,1)} %copy-done.8, bf16[2,128,128]{2,1,0:T(8,128)(2,1)} %copy-done.9, bf16[2,128,128]{2,1,0:T(8,128)(2,1)} %copy-done.10), custom_call_target="tpu_custom_call" | custom-call | tf_op jit(solution)/shard_map/pallas_call | solution.py:306
  (37 shorter events, 0.2 us)
Async XLA Ops:
  0.6 43.6 %copy-start.2 = (bf16[128,1024]{1,0:T(8,128)(2,1)S(1)}, bf16[128,1024]{1,0:T(8,128)(2,1)}, u32[]{:S(2)}) copy-start(bf16[128,1024]{1,0:T(8,128)(2,1)} %refs_1_.1) | copy-start | bytes 786436
  2.1 7.7 %collective-permute-start = (bf16[272,128]{1,0:T(8,128)(2,1)}, bf16[272,128]{1,0:T(8,128)(2,1)S(1)}, u32[]{:S(2)}, u32[]{:S(2)}) collective-permute-start(bf16[272,128]{1,0:T(8,128)(2,1)} %shard_map.94.p0), channel_id=1, source_target_pairs={{0,64},{8,72},{16,80},{24,88},{32,96},{40,104},{48,112},{56,120},{... | collective-permute-start | bytes 208904 | tf_op jit(solution)/shard_map/ppermute | solution.py:316
  4.0 8.2 %collective-permute-start.1 = (bf16[272,128]{1,0:T(8,128)(2,1)}, bf16[272,128]{1,0:T(8,128)(2,1)S(1)}, u32[]{:S(2)}, u32[]{:S(2)}) collective-permute-start(bf16[272,128]{1,0:T(8,128)(2,1)} %shard_map.94.p0), channel_id=1, source_target_pairs={{0,128},{8,136},{16,144},{24,152},{32,160},{40,168},{48,176},{56,1... | collective-permute-start | bytes 208904 | tf_op jit(solution)/shard_map/ppermute | solution.py:316
  7.3 5.3 %collective-permute-start.2 = (bf16[272,128]{1,0:T(8,128)(2,1)}, bf16[272,128]{1,0:T(8,128)(2,1)S(1)}, u32[]{:S(2)}, u32[]{:S(2)}) collective-permute-start(bf16[272,128]{1,0:T(8,128)(2,1)} %shard_map.94.p0), channel_id=1, source_target_pairs={{0,192},{8,200},{16,208},{24,216},{32,224},{40,232},{48,240},{56,2... | collective-permute-start | bytes 208904 | tf_op jit(solution)/shard_map/ppermute | solution.py:316
  9.8 2.8 %copy-start.5 = (bf16[272,128]{1,0:T(8,128)(2,1)}, bf16[272,128]{1,0:T(8,128)(2,1)S(1)}, u32[]{:S(2)}) copy-start(bf16[272,128]{1,0:T(8,128)(2,1)S(1)} %collective-permute-done.p1) | copy-start | bytes 208900
  12.2 0.6 copy-start.6
  12.9 0.6 copy-start.7
  15.2 23.0 %collective-permute-start.6 = (bf16[4,2,128,128]{3,2,1,0:T(8,128)(2,1)}, bf16[4,2,128,128]{3,2,1,0:T(8,128)(2,1)S(1)}, u32[]{:S(2)}, u32[]{:S(2)}) collective-permute-start(bf16[4,2,128,128]{3,2,1,0:T(8,128)(2,1)} %get-tuple-element.42.refs_3_), channel_id=1, source_target_pairs={{0,16},{8,24},{16,32},{24,40},{32,48},{40,56},{48,0},{56,8},{64,80... | collective-permute-start | bytes 786440 | tf_op jit(solution)/shard_map/ppermute | solution.py:316
  16.7 21.5 %collective-permute-start.7 = (bf16[4,2,128,128]{3,2,1,0:T(8,128)(2,1)}, bf16[4,2,128,128]{3,2,1,0:T(8,128)(2,1)S(1)}, u32[]{:S(2)}, u32[]{:S(2)}) collective-permute-start(bf16[4,2,128,128]{3,2,1,0:T(8,128)(2,1)} %get-tuple-element.42.refs_3_), channel_id=1, source_target_pairs={{0,32},{8,40},{16,48},{24,56},{32,0},{40,8},{48,16},{56,24},{64,96... | collective-permute-start | bytes 786440 | tf_op jit(solution)/shard_map/ppermute | solution.py:316
  19.4 18.8 %collective-permute-start.8 = (bf16[4,2,128,128]{3,2,1,0:T(8,128)(2,1)}, bf16[4,2,128,128]{3,2,1,0:T(8,128)(2,1)S(1)}, u32[]{:S(2)}, u32[]{:S(2)}) collective-permute-start(bf16[4,2,128,128]{3,2,1,0:T(8,128)(2,1)} %get-tuple-element.42.refs_3_), channel_id=1, source_target_pairs={{0,48},{8,56},{16,0},{24,8},{32,16},{40,24},{48,32},{56,40},{64,11... | collective-permute-start | bytes 786440 | tf_op jit(solution)/shard_map/ppermute | solution.py:316
  20.8 17.3 %collective-permute-start.9 = (bf16[4,2,128,128]{3,2,1,0:T(8,128)(2,1)}, bf16[4,2,128,128]{3,2,1,0:T(8,128)(2,1)S(1)}, u32[]{:S(2)}, u32[]{:S(2)}) collective-permute-start(bf16[4,2,128,128]{3,2,1,0:T(8,128)(2,1)} %get-tuple-element.42.refs_3_), channel_id=1, source_target_pairs={{0,8},{8,0},{16,24},{24,16},{32,40},{40,32},{48,56},{56,48},{64,72... | collective-permute-start | bytes 786440 | tf_op jit(solution)/shard_map/ppermute | solution.py:316
  20.8 3.8 %collective-permute-start.3 = (f32[8,128]{1,0:T(8,128)}, f32[8,128]{1,0:T(8,128)S(1)}, u32[]{:S(2)}, u32[]{:S(2)}) collective-permute-start(f32[8,128]{1,0:T(8,128)} %get-tuple-element.34), channel_id=1, source_target_pairs={{0,1},{1,0},{2,3},{3,2},{4,5},{5,4},{6,7},{7,6},{8,9},{9,8},{10,11... | collective-permute-start | bytes 12296 | tf_op jit(solution)/shard_map/ppermute | solution.py:324
  25.4 5.1 %collective-permute-start.4 = (f32[8,128]{1,0:T(8,128)S(1)}, f32[8,128]{1,0:T(8,128)S(1)}, u32[]{:S(2)}, u32[]{:S(2)}) collective-permute-start(f32[8,128]{1,0:T(8,128)S(1)} %add.18), channel_id=1, source_target_pairs={{0,2},{1,3},{2,0},{3,1},{4,6},{5,7},{6,4},{7,5},{8,10},{9,11},{10,... | collective-permute-start | bytes 12296 | tf_op jit(solution)/shard_map/ppermute | solution.py:324
  30.5 7.7 %collective-permute-start.5 = (f32[8,128]{1,0:T(8,128)S(1)}, f32[8,128]{1,0:T(8,128)S(1)}, u32[]{:S(2)}, u32[]{:S(2)}) collective-permute-start(f32[8,128]{1,0:T(8,128)S(1)} %add.19), channel_id=1, source_target_pairs={{0,4},{1,5},{2,6},{3,7},{4,0},{5,1},{6,2},{7,3},{8,12},{9,13},{10,... | collective-permute-start | bytes 12296 | tf_op jit(solution)/shard_map/ppermute | solution.py:324
  38.2 6.0 %collective-permute-start.12 = (bf16[4,2,128,128]{3,2,1,0:T(8,128)(2,1)S(1)}, bf16[4,2,128,128]{3,2,1,0:T(8,128)(2,1)S(1)}, u32[]{:S(2)}, u32[]{:S(2)}) collective-permute-start(bf16[4,2,128,128]{3,2,1,0:T(8,128)(2,1)S(1)} %collective-permute-done.6.refs_4_), channel_id=1, source_target_pairs={{0,8},{8,0},{16,24},{24,16},{32,40},{40,32},{48,56},{56,48},{64,72... | collective-permute-start | bytes 786440 | tf_op jit(solution)/shard_map/ppermute | solution.py:316
  38.3 5.9 %collective-permute-start.13 = (bf16[4,2,128,128]{3,2,1,0:T(8,128)(2,1)S(1)}, bf16[4,2,128,128]{3,2,1,0:T(8,128)(2,1)S(1)}, u32[]{:S(2)}, u32[]{:S(2)}) collective-permute-start(bf16[4,2,128,128]{3,2,1,0:T(8,128)(2,1)S(1)} %collective-permute-done.7.refs_5_), channel_id=1, source_target_pairs={{0,8},{8,0},{16,24},{24,16},{32,40},{40,32},{48,56},{56,48},{64,72... | collective-permute-start | bytes 786440 | tf_op jit(solution)/shard_map/ppermute | solution.py:316
  38.8 5.4 %collective-permute-start.14 = (bf16[4,2,128,128]{3,2,1,0:T(8,128)(2,1)S(1)}, bf16[4,2,128,128]{3,2,1,0:T(8,128)(2,1)S(1)}, u32[]{:S(2)}, u32[]{:S(2)}) collective-permute-start(bf16[4,2,128,128]{3,2,1,0:T(8,128)(2,1)S(1)} %collective-permute-done.8.refs_6_), channel_id=1, source_target_pairs={{0,8},{8,0},{16,24},{24,16},{32,40},{40,32},{48,56},{56,48},{64,72... | collective-permute-start | bytes 786440 | tf_op jit(solution)/shard_map/ppermute | solution.py:316
  38.9 1.7 %collective-permute-start.10 = (f32[8,128]{1,0:T(8,128)S(1)}, f32[8,128]{1,0:T(8,128)S(1)}, u32[]{:S(2)}, u32[]{:S(2)}) collective-permute-start(f32[8,128]{1,0:T(8,128)S(1)} %add.20), channel_id=1, source_target_pairs={{0,8},{8,0},{16,24},{24,16},{32,40},{40,32},{48,56},{56,48},{64,72... | collective-permute-start | bytes 12296 | tf_op jit(solution)/shard_map/ppermute | solution.py:316
  40.6 3.6 %copy-start.1 = (s32[9]{0:T(128)S(1)}, s32[9]{0:T(128)}, u32[]{:S(2)}) copy-start(s32[9]{0:T(128)} %b_ref.3) | copy-start | bytes 112
  40.6 3.6 %collective-permute-start.11 = (f32[8,128]{1,0:T(8,128)S(1)}, f32[8,128]{1,0:T(8,128)S(1)}, u32[]{:S(2)}, u32[]{:S(2)}) collective-permute-start(f32[8,128]{1,0:T(8,128)S(1)} %add.21), channel_id=1, source_target_pairs={{0,16},{8,24},{16,0},{24,8},{32,48},{40,56},{48,32},{56,40},{64,80... | collective-permute-start | bytes 12296 | tf_op jit(solution)/shard_map/ppermute | solution.py:316
  44.2 1.0 %copy-start.3 = (bf16[128,1024]{1,0:T(8,128)(2,1)S(1)}, bf16[128,1024]{1,0:T(8,128)(2,1)}, u32[]{:S(2)}) copy-start(bf16[128,1024]{1,0:T(8,128)(2,1)} %refs_2_.1) | copy-start | bytes 786436
  45.2 0.9 %copy-start.4 = (bf16[4,2,128,128]{3,2,1,0:T(8,128)(2,1)S(1)}, bf16[4,2,128,128]{3,2,1,0:T(8,128)(2,1)}, u32[]{:S(2)}) copy-start(bf16[4,2,128,128]{3,2,1,0:T(8,128)(2,1)} %get-tuple-element.42.refs_3_) | copy-start | bytes 786436
  48.9 0.7 copy-start.11
  48.9 5.3 %collective-permute-start.16 = (bf16[4,4,2,128,128]{4,3,2,1,0:T(8,128)(2,1)}, bf16[4,4,2,128,128]{4,3,2,1,0:T(8,128)(2,1)S(1)}, u32[]{:S(2)}, u32[]{:S(2)}) collective-permute-start(bf16[4,4,2,128,128]{4,3,2,1,0:T(8,128)(2,1)} %get-tuple-element.53), channel_id=1, source_target_pairs={{0,8},{8,0},{16,24},{24,16},{32,40},{40,32},{48,56},{56,48},{64,72... | collective-permute-start | bytes 3145736 | tf_op jit(solution)/shard_map/ppermute | solution.py:316
  49.0 5.2 %collective-permute-start.15 = (f32[8,128]{1,0:T(8,128)S(1)}, f32[8,128]{1,0:T(8,128)S(1)}, u32[]{:S(2)}, u32[]{:S(2)}) collective-permute-start(f32[8,128]{1,0:T(8,128)S(1)} %add.22), channel_id=1, source_target_pairs={{0,32},{8,40},{16,48},{24,56},{32,0},{40,8},{48,16},{56,24},{64,96... | collective-permute-start | bytes 12296 | tf_op jit(solution)/shard_map/ppermute | solution.py:316
  55.4 9.3 %collective-permute-start.17 = (bf16[4,2,128,128]{3,2,1,0:T(8,128)(2,1)S(1)}, bf16[4,2,128,128]{3,2,1,0:T(8,128)(2,1)S(1)}, u32[]{:S(2)}, u32[]{:S(2)}) collective-permute-start(bf16[4,2,128,128]{3,2,1,0:T(8,128)(2,1)S(1)} %get-tuple-element.56), channel_id=1, source_target_pairs={{0,48},{8,56},{16,0},{24,8},{32,16},{40,24},{48,32},{56,40},{64,11... | collective-permute-start | bytes 786440 | tf_op jit(solution)/shard_map/ppermute | solution.py:316
  55.5 10.9 %collective-permute-start.18 = (bf16[4,2,128,128]{3,2,1,0:T(8,128)(2,1)S(1)}, bf16[4,2,128,128]{3,2,1,0:T(8,128)(2,1)S(1)}, u32[]{:S(2)}, u32[]{:S(2)}) collective-permute-start(bf16[4,2,128,128]{3,2,1,0:T(8,128)(2,1)S(1)} %get-tuple-element.57), channel_id=1, source_target_pairs={{0,32},{8,40},{16,48},{24,56},{32,0},{40,8},{48,16},{56,24},{64,96... | collective-permute-start | bytes 786440 | tf_op jit(solution)/shard_map/ppermute | solution.py:316
  58.2 12.1 %collective-permute-start.19 = (bf16[4,2,128,128]{3,2,1,0:T(8,128)(2,1)S(1)}, bf16[4,2,128,128]{3,2,1,0:T(8,128)(2,1)S(1)}, u32[]{:S(2)}, u32[]{:S(2)}) collective-permute-start(bf16[4,2,128,128]{3,2,1,0:T(8,128)(2,1)S(1)} %get-tuple-element.58), channel_id=1, source_target_pairs={{0,16},{8,24},{16,32},{24,40},{32,48},{40,56},{48,0},{56,8},{64,80... | collective-permute-start | bytes 786440 | tf_op jit(solution)/shard_map/ppermute | solution.py:316
  70.4 12.4 %copy-start = (bf16[2,128,128]{2,1,0:T(8,128)(2,1)}, bf16[2,128,128]{2,1,0:T(8,128)(2,1)S(1)}, u32[]{:S(2)}) copy-start(bf16[2,128,128]{2,1,0:T(8,128)(2,1)S(1)} %get-tuple-element.59.i0) | copy-start | bytes 196612
  70.4 12.8 %collective-permute-start.20 = (bf16[2,128,128]{2,1,0:T(8,128)(2,1)S(1)}, bf16[2,128,128]{2,1,0:T(8,128)(2,1)S(1)}, u32[]{:S(2)}, u32[]{:S(2)}) collective-permute-start(bf16[2,128,128]{2,1,0:T(8,128)(2,1)S(1)} %get-tuple-element.60), channel_id=1, source_target_pairs={{0,192},{8,200},{16,208},{24,216},{32,224},{40,232},{48,240},{56,2... | collective-permute-start | bytes 196616 | tf_op jit(solution)/shard_map/ppermute | solution.py:316
  80.7 6.4 %collective-permute-start.21 = (bf16[2,128,128]{2,1,0:T(8,128)(2,1)S(1)}, bf16[2,128,128]{2,1,0:T(8,128)(2,1)S(1)}, u32[]{:S(2)}, u32[]{:S(2)}) collective-permute-start(bf16[2,128,128]{2,1,0:T(8,128)(2,1)S(1)} %get-tuple-element.61), channel_id=1, source_target_pairs={{0,128},{8,136},{16,144},{24,152},{32,160},{40,168},{48,176},{56,1... | collective-permute-start | bytes 196616 | tf_op jit(solution)/shard_map/ppermute | solution.py:316
  80.7 6.4 %collective-permute-start.22 = (bf16[2,128,128]{2,1,0:T(8,128)(2,1)S(1)}, bf16[2,128,128]{2,1,0:T(8,128)(2,1)S(1)}, u32[]{:S(2)}, u32[]{:S(2)}) collective-permute-start(bf16[2,128,128]{2,1,0:T(8,128)(2,1)S(1)} %get-tuple-element.62), channel_id=1, source_target_pairs={{0,64},{8,72},{16,80},{24,88},{32,96},{40,104},{48,112},{56,120},{... | collective-permute-start | bytes 196616 | tf_op jit(solution)/shard_map/ppermute | solution.py:316
  83.2 3.9 %copy-start.8 = (bf16[2,128,128]{2,1,0:T(8,128)(2,1)}, bf16[2,128,128]{2,1,0:T(8,128)(2,1)S(1)}, u32[]{:S(2)}) copy-start(bf16[2,128,128]{2,1,0:T(8,128)(2,1)S(1)} %collective-permute-done.20.i1) | copy-start | bytes 196612
  87.1 0.6 copy-start.9
  87.1 0.6 copy-start.10

commit v2 on v1

v2 whole, which is shorter than its diff:
```python
import math

import jax
import jax.numpy as jnp
from jax import lax
from jax.experimental import pallas as pl
from jax.experimental.pallas import tpu as pltpu
from jax.sharding import PartitionSpec as P

DH = 128
BLOCK = 128
RESP = 8
GROUP = 8
ROWS = GROUP * BLOCK
PACKET = 2 * BLOCK + 16
NB = 4
KC = NB * BLOCK
scale = 1.0 / math.sqrt(DH)
c2 = scale * math.log2(math.e)
f32 = jnp.float32
bf = jnp.bfloat16
NT = (((1,), (1,)), ((), ()))
NN = (((1,), (0,)), ((), ()))
S = pl.BlockSpec(memory_space=pltpu.SMEM)
V = pl.BlockSpec(memory_space=pltpu.VMEM)
A = pl.BlockSpec(memory_space=pl.ANY)


def attend_body(
    bounds, q_ref, do_ref, bufs, dq_ref, keep_ref, send_ref,
    kk, vv, q2, g2, pb, dp_s, mt, mx, sm, dl, acc, sem,
):
    me = lax.axis_index("seq")
    prompt = bounds[0] // BLOCK
    start = jnp.int32(0)
    for r in range(RESP):
        lo = bounds[r] // BLOCK
        start = jnp.where(me >= lo, lo, start)
    live = me >= prompt
    n = jnp.where(live, prompt + me - start + 1, 0)
    chunks = (n + NB - 1) // NB
    z = me // 8
    x = lax.rem(me // 2, 4)
    c = lax.rem(me, 2)

    def where_is(t):
        j = jnp.where(t < prompt, t, start + t - prompt)
        column = lax.rem(lax.rem(j, 2) + c, 2) * 4 + lax.rem(x - lax.rem(j // 2, 4) + 4, 4)
        return column, lax.rem(z - j // 8 + 4, 4)

    def rows_of(t):
        return pl.ds(pl.multiple_of(t * BLOCK, BLOCK), BLOCK)

    def fetch(t, _):
        b, sz = where_is(t)
        for nb, buf in enumerate(bufs):

            @pl.when(b == nb)
            def _(buf=buf):
                key, value = buf.at[sz, pl.ds(0, BLOCK)], buf.at[sz, pl.ds(BLOCK, BLOCK)]
                pltpu.make_async_copy(key, kk.at[rows_of(t)], sem.at[0, t]).start()
                pltpu.make_async_copy(value, vv.at[rows_of(t)], sem.at[1, t]).start()

        return 0

    lax.fori_loop(0, n, fetch, 0)
    for h in range(GROUP):
        at = slice(h * DH, (h + 1) * DH)
        q2[h * BLOCK : (h + 1) * BLOCK, :] = q_ref[:, at]
        g2[h * BLOCK : (h + 1) * BLOCK, :] = do_ref[:, at]
    keep_ref[...] = jnp.zeros_like(keep_ref)
    send_ref[...] = jnp.zeros_like(send_ref)
    mx[...] = jnp.full_like(mx, -1e30)
    sm[...] = jnp.zeros_like(sm)
    dl[...] = jnp.zeros_like(dl)
    acc[...] = jnp.zeros_like(acc)

    def pad(t, _):
        kk[rows_of(t), :] = jnp.zeros((BLOCK, DH), bf)
        vv[rows_of(t), :] = jnp.zeros((BLOCK, DH), bf)
        return 0

    lax.fori_loop(n, chunks * NB, pad, 0)

    def land(t, _):
        pltpu.make_async_copy(bufs[0].at[0, pl.ds(0, BLOCK)], kk.at[rows_of(t)], sem.at[0, t]).wait()
        pltpu.make_async_copy(bufs[0].at[0, pl.ds(0, BLOCK)], vv.at[rows_of(t)], sem.at[1, t]).wait()
        return 0

    def forward(i, masked):
        rows = pl.ds(pl.multiple_of(i * KC, KC), KC)
        lax.fori_loop(i * NB, jnp.minimum(i * NB + NB, n), land, 0)
        s = lax.dot_general(kk[rows, :], q2[...], NT, preferred_element_type=f32) * c2
        if masked:
            key = lax.broadcasted_iota(jnp.int32, (KC, ROWS), 0) + i * KC - (n - 1) * BLOCK
            query = lax.rem(lax.broadcasted_iota(jnp.int32, (KC, ROWS), 1), BLOCK)
            s = jnp.where(key <= query, s, -jnp.inf)
        old = mx[0:1, :]
        top = jnp.max(s.reshape(KC // 8, 8, ROWS), axis=0)
        new = jnp.maximum(old, jnp.max(top, axis=0, keepdims=True))
        p = jnp.exp2(s - new)
        dp = lax.dot_general(vv[rows, :], g2[...], NT, preferred_element_type=f32)
        fade = jnp.exp2(old - new)
        sm[...] = sm[...] * fade + jnp.sum(p.reshape(KC // 8, 8, ROWS), axis=0)
        dl[...] = dl[...] * fade + jnp.sum((p * dp).reshape(KC // 8, 8, ROWS), axis=0)
        mx[0:1, :] = new
        mt[i, 0:1, :] = new
        pb[rows, :] = p.astype(bf)
        dp_s[rows, :] = dp

    def step(i, _):
        forward(i, False)
        return 0

    lax.fori_loop(0, chunks - 1, step, 0)

    @pl.when(live)
    def _():
        forward(chunks - 1, True)
        inv = 1.0 / jnp.sum(sm[...], axis=0, keepdims=True)
        dl[0:1, :] = jnp.sum(dl[...], axis=0, keepdims=True) * inv
        sm[0:1, :] = inv

    def backward(i, _):
        rows = pl.ds(pl.multiple_of(i * KC, KC), KC)
        f = sm[0:1, :] * jnp.exp2(mt[i, 0:1, :] - mx[0:1, :])
        p = pb[rows, :].astype(f32) * f
        g = (p * (dp_s[rows, :] - dl[0:1, :])).astype(bf)
        dk = lax.dot_general(g, q2[...], NN, preferred_element_type=f32)
        dv = lax.dot_general(p.astype(bf), g2[...], NN, preferred_element_type=f32)
        acc[...] += lax.dot_general(kk[rows, :].T, g, NN, preferred_element_type=f32)
        for u in range(NB):
            t = i * NB + u
            b, sz = where_is(t)
            sx = lax.rem(b, 4)
            dk_u = (dk[u * BLOCK : (u + 1) * BLOCK] * scale).astype(bf)
            dv_u = dv[u * BLOCK : (u + 1) * BLOCK].astype(bf)
            for crel, out in enumerate((keep_ref, send_ref)):

                @pl.when((t < n) & (b // 4 == crel))
                def _(out=out):
                    out[sx, sz, 0] = dk_u
                    out[sx, sz, 1] = dv_u

        return 0

    lax.fori_loop(0, chunks, backward, 0)
    for h in range(GROUP):
        at = slice(h * BLOCK, (h + 1) * BLOCK)
        dq_ref[:, at] = (acc[:, at] * scale).T


def attend(bounds, q, do, bufs):
    nb = len(bufs)

    def kern(*refs):
        attend_body(refs[0], refs[1], refs[2], refs[3 : 3 + nb], *refs[3 + nb :])

    partial = jax.ShapeDtypeStruct((4, 4, 2, BLOCK, DH), bf)
    return pl.pallas_call(
        kern,
        out_shape=(jax.ShapeDtypeStruct((BLOCK, ROWS), f32), partial, partial),
        in_specs=[S, V, V] + [A] * nb,
        out_specs=(V, V, V),
        scratch_shapes=[
            pltpu.VMEM((32 * BLOCK, DH), bf),
            pltpu.VMEM((32 * BLOCK, DH), bf),
            pltpu.VMEM((ROWS, DH), bf),
            pltpu.VMEM((ROWS, DH), bf),
            pltpu.VMEM((32 * BLOCK, ROWS), bf),
            pltpu.VMEM((32 * BLOCK, ROWS), f32),
            pltpu.VMEM((32 // NB, 8, ROWS), f32),
            pltpu.VMEM((8, ROWS), f32),
            pltpu.VMEM((8, ROWS), f32),
            pltpu.VMEM((8, ROWS), f32),
            pltpu.VMEM((DH, ROWS), f32),
            pltpu.SemaphoreType.DMA((2, 32)),
        ],
        compiler_params=pltpu.CompilerParams(vmem_limit_bytes=44 * 2**20),
        cost_estimate=pl.CostEstimate(
            flops=10**10, bytes_accessed=5 * 2**20, transcendentals=2**22
        ),
    )(bounds, q, do, *bufs)

PAIRS = 8
SMALL = pltpu.CompilerParams(vmem_limit_bytes=8 * 2**20)


def seq_perm(move):
    pairs = []
    for z in range(4):
        for x in range(4):
            for c in range(2):
                nz, nx, nc = move(z, x, c)
                pairs.append(((z * 4 + x) * 2 + c, (nz * 4 + nx) * 2 + nc))
    return pairs


CORE = seq_perm(lambda z, x, c: (z, x, 1 - c))
X_UP = [seq_perm(lambda z, x, c, s=s: (z, (x + s) % 4, c)) for s in range(4)]
X_DOWN = [seq_perm(lambda z, x, c, s=s: (z, (x - s) % 4, c)) for s in range(4)]
Z_UP = [seq_perm(lambda z, x, c, s=s: ((z + s) % 4, x, c)) for s in range(4)]
Z_DOWN = [seq_perm(lambda z, x, c, s=s: ((z - s) % 4, x, c)) for s in range(4)]


HEAD_Y = [[(h, h // 4 * 4 + m[h % 4]) for h in range(8)] for m in ((1, 0, 3, 2), (3, 2, 1, 0))]
X_FLIP = [seq_perm(lambda z, x, c, m=m: (z, m[x], c)) for m in ((1, 0, 3, 2), (3, 2, 1, 0))]
HALVES = []
for seq_at in range(32):
    for head_at in range(8):
        far = (head_at // 4 * 4 + seq_at // 8) ^ 6
        HALVES.append(
            (seq_at * 8 + head_at, (far % 4 * 8 + seq_at % 8) * 8 + far // 4 * 4 + head_at % 4)
        )


def pack(keys, values, ratios):
    def kern(k_ref, v_ref, ratio_ref, out_ref):
        total = ratio_ref[0]
        for t in range(1, ratios.shape[0]):
            total = total + ratio_ref[t]
        whole = jnp.full((16, DH), total, f32)
        hi = whole.astype(bf).astype(f32)
        mid = (whole - hi).astype(bf).astype(f32)
        low = whole - hi - mid
        row = lax.broadcasted_iota(jnp.int32, (16, DH), 0)
        ride = jnp.where(row == 0, hi, jnp.where(row == 1, mid, jnp.where(row == 2, low, 0.0)))
        out_ref[:BLOCK, :] = k_ref[...]
        out_ref[BLOCK : 2 * BLOCK, :] = v_ref[...]
        out_ref[2 * BLOCK :, :] = ride.astype(bf)

    return pl.pallas_call(
        kern,
        out_shape=jax.ShapeDtypeStruct((2 * BLOCK + 16, DH), bf),
        in_specs=[V, V, S],
        out_specs=V,
    )(keys, values, ratios)


def block_sums(bounds, packets):
    def kern(b_ref, p0, p1, p2, p3, sums_ref):
        me = lax.axis_index("seq")
        row = lax.broadcasted_iota(jnp.int32, (RESP, DH), 0)
        sums = jnp.zeros((RESP, DH), f32)
        for s, packet in enumerate((p0, p1, p2, p3)):
            first = (lax.rem(me // 8 - s + 4, 4) * 8 + lax.rem(me, 8)) * BLOCK
            resp = jnp.int32(-1)
            for r in range(RESP):
                resp = resp + (first >= b_ref[r]).astype(jnp.int32)
            part = jnp.sum(packet[2 * BLOCK :, :].astype(f32), axis=0, keepdims=True)
            sums = sums + jnp.where(row == resp, part, 0.0)
        sums_ref[...] = sums

    return pl.pallas_call(
        kern,
        out_shape=jax.ShapeDtypeStruct((RESP, DH), f32),
        in_specs=[S, V, V, V, V],
        out_specs=V,
        compiler_params=SMALL,
    )(bounds, *packets)


def core_add(sums, bounds, pairs, keep, got):
    def kern(sums_ref, b_ref, p_ref, keep_ref, got_ref, o0, o1, o2, o3, w_ref, mean, coef):
        me = lax.axis_index("seq")
        for r in range(RESP):
            mean[r] = sums_ref[r, 0] / (b_ref[r + 1] - b_ref[r]).astype(f32)
            coef[r] = 0.0
        for p in range(PAIRS):
            win, lose = p_ref[p, 0], p_ref[p, 1]
            resid = mean[win] - mean[lose] - 1.0
            coef[win] = coef[win] + resid
            coef[lose] = coef[lose] - resid

        def weight(block):
            first = block * BLOCK
            w = jnp.float32(0.0)
            for r in range(RESP):
                inside = (first >= b_ref[r]) & (first < b_ref[r + 1])
                length = (b_ref[r + 1] - b_ref[r]).astype(f32)
                w = jnp.where(inside, 512.0 * (2.0 / PAIRS * coef[r] / length), w)
            return w

        mine = weight(me)
        theirs = weight(me + 1 - 2 * lax.rem(me, 2))
        w_ref[...] = jnp.full(w_ref.shape, mine, f32)
        for sx, out in enumerate((o0, o1, o2, o3)):
            for sz in range(4):
                for kvi in range(2):
                    out[sz, kvi] = (
                        keep_ref[sx, sz, kvi].astype(f32) * mine
                        + got_ref[sx, sz, kvi].astype(f32) * theirs
                    ).astype(bf)

    slot = jax.ShapeDtypeStruct((4, 2, 128, 128), bf)
    return pl.pallas_call(
        kern,
        out_shape=(slot, slot, slot, slot, jax.ShapeDtypeStruct((8, 128), f32)),
        in_specs=[S, S, S, V, V],
        out_specs=(V,) * 5,
        scratch_shapes=[pltpu.SMEM((RESP,), f32), pltpu.SMEM((RESP,), f32)],
        compiler_params=SMALL,
    )(sums, bounds, pairs, keep, got)


def x_add(a0, a1, a2, a3):
    def kern(i0, i1, i2, i3, *outs):
        for sz in range(4):
            for kvi in range(2):
                outs[sz][kvi] = (
                    (i0[sz, kvi].astype(f32) + i1[sz, kvi].astype(f32))
                    + (i2[sz, kvi].astype(f32) + i3[sz, kvi].astype(f32))
                ).astype(bf)

    slot = jax.ShapeDtypeStruct((2, 128, 128), bf)
    return pl.pallas_call(
        kern,
        out_shape=(slot,) * 4,
        in_specs=[V] * 4,
        out_specs=(V,) * 4,
        compiler_params=SMALL,
    )(a0, a1, a2, a3)


def z_add(a0, a1, a2, a3):
    def kern(i0, i1, i2, i3, dk, dv):
        for kvi, out in enumerate((dk, dv)):
            out[...] = (
                (i0[kvi].astype(f32) + i1[kvi].astype(f32))
                + (i2[kvi].astype(f32) + i3[kvi].astype(f32))
            ).astype(bf)

    out = jax.ShapeDtypeStruct((BLOCK, DH), bf)
    return pl.pallas_call(
        kern,
        out_shape=(out, out),
        in_specs=[V] * 4,
        out_specs=(V, V),
        compiler_params=SMALL,
    )(a0, a1, a2, a3)


def shards(query_rows, key_rows, value_rows, out_grad, log_ratio, block_mask, bounds, pairs):
    def seq(v, perm):
        return lax.ppermute(v, "seq", perm)

    packet = pack(key_rows, value_rows, log_ratio)
    by_z = [packet] + [seq(packet, Z_UP[s]) for s in (1, 2, 3)]
    column = jnp.stack([p[: 2 * BLOCK] for p in by_z])
    column, by_z = lax.optimization_barrier((column, by_z))
    by_x = [column] + [seq(column, X_UP[s]) for s in (1, 2, 3)]
    sums = block_sums(bounds, by_z)
    for turn in HEAD_Y:
        sums = sums + lax.ppermute(sums, "heads", turn)
    sums = sums + lax.ppermute(sums, ("seq", "heads"), HALVES)
    sums, by_x = lax.optimization_barrier((sums, by_x))
    bufs = by_x + [seq(b, CORE) for b in by_x]
    sums = sums + seq(sums, CORE)
    sums, bufs = lax.optimization_barrier((sums, bufs))
    turned = seq(sums, X_FLIP[0])
    dq, keep, send = attend(bounds, query_rows, out_grad, bufs)
    sums, send = lax.optimization_barrier((sums + turned, send))
    got = seq(send, CORE)
    sums = sums + seq(sums, X_FLIP[1])
    *by_shift, weight = core_add(sums, bounds, pairs, keep, got)
    summed = x_add(by_shift[0], *[seq(by_shift[s], X_DOWN[s]) for s in (1, 2, 3)])
    query_grad = (dq * weight[0, 0]).astype(bf)
    key_grad, value_grad = z_add(summed[0], *[seq(summed[s], Z_DOWN[s]) for s in (1, 2, 3)])
    return query_grad, key_grad, value_grad


def solution(mesh):
    whole = P("seq", "heads")
    return jax.shard_map(
        shards,
        mesh=mesh,
        in_specs=(whole, whole, whole, whole, P(("seq", "heads")), P(), P(), P()),
        out_specs=(whole, whole, whole),
        check_vma=False,
    )
```

time: 89.8 us -> 80.8 us (0.90)
  starting transfers between devices: 36 us -> 33.2 us
  local copies, waits for them, and re-layouts: 4.03 us -> 1.72 us
  Pallas kernels: 8.89 us -> 6.83 us
    unnamed x25 -> x11, local copies, waits for them, and re-layouts: 3.51 us -> 0.31 us
    ppermute x3, starting transfers between devices: 8.08 us -> 5.63 us  [the longest x1 4.57 us: shards(): sums = sums + lax.ppermute(sums, ('seq', 'heads'), HALVES)]
    ppermute x20, waiting for transfers between devices: 28.9 us -> 27.7 us  [seq(): return lax.ppermute(v, 'seq', perm)]
    pallas_call x2, Pallas kernels: 4.49 us -> 3.38 us  [the longest x1 2.78 us: attend(): pl.pallas_call(kern, out_shape=(jax.ShapeDtypeStruct((BLOCK, ROWS), f32),...]
    pallas_call x1, Pallas kernels: 1.58 us -> 0.65 us  [z_add(): pl.pallas_call(kern, out_shape=(out, out), in_specs=[V] * 4, out_specs=(V...]
  transfers between devices with their start and end apart: 23 -> 23, of which waited for: 14 -> 13; matrix products, arithmetic and copies ran while one was open for 3% -> 4% of each run, Pallas kernels for 0% -> 4%
where the time goes in v2:
time: 80.8 us; the launch traced here: 80.7 us
  waiting for transfers between devices  36.7 us (45%)
  starting transfers between devices  33.2 us (41%)
  Pallas kernels  6.83 us (8%)
  local copies, waits for them, and re-layouts  1.72 us (2%)
  other arithmetic  1.44 us (2%)
    ppermute x20, waiting for transfers between devices, seq(): return lax.ppermute(v, 'seq', perm)  27.7 us
    ppermute x20, starting transfers between devices, seq(): return lax.ppermute(v, 'seq', perm)  27.6 us
    ppermute x2, waiting for transfers between devices, shards(): sums = sums + lax.ppermute(sums, 'heads', turn)  7.46 us
    ppermute x1, starting transfers between devices, shards(): sums = sums + lax.ppermute(sums, ('seq', 'heads'), HALVES)  4.57 us
    pallas_call x1, Pallas kernels, attend(): pl.pallas_call(kern, out_shape=(jax.ShapeDtypeStruct((BLOCK, ROWS), f32),...  2.78 us
  transfers between devices with their start and end apart: 23, of which 13 were waited for; matrix products, arithmetic and copies ran while one was open for 4% of the time, Pallas kernels for 4%

profile of v2, /device:TPU:24, one launch (start us, length us, event | category | flops | bytes accessed | tf_op | source)
XLA Modules:
  0.0 80.7 jit_solution(7175961741228415892)
XLA Ops:
  0.6 1.5 %shard_map.94.p0 = bf16[272,128]{1,0:T(8,128)(2,1)} custom-call(bf16[128,128]{1,0:T(8,128)(2,1)} %k_ref.1, bf16[128,128]{1,0:T(8,128)(2,1)} %v_ref.1, f32[16]{0:T(128)} %ratio_ref.1), custom_call_target="tpu_custom_call" | custom-call | tf_op jit(solution)/shard_map/pallas_call | solution.py:232
  2.1 4.6 %collective-permute-start.2 = (bf16[272,128]{1,0:T(8,128)(2,1)}, bf16[272,128]{1,0:T(8,128)(2,1)S(1)}, u32[]{:S(2)}, u32[]{:S(2)}) collective-permute-start(bf16[272,128]{1,0:T(8,128)(2,1)} %shard_map.94.p0), channel_id=1, source_target_pairs={{0,192},{8,200},{16,208},{24,216},{32,224},{40,232},{48,240},{56,2... | collective-permute-start | bytes 208904 | tf_op jit(solution)/shard_map/ppermute | solution.py:345
  6.7 0.0 collective-permute-start.1
  6.7 0.7 collective-permute-start
  7.4 0.9 %slice_bitcast_fusion.3 = bf16[1,256,128]{2,1,0:T(8,128)(2,1)S(1)} fusion(bf16[272,128]{1,0:T(8,128)(2,1)} %shard_map.94.p0), kind=kLoop, calls=%fused_computation.5 | loop fusion | bytes 131072 | tf_op jit(solution)/shard_map/stack | solution.py:349
  8.3 1.4 %collective-permute-done.2.p3 = bf16[272,128]{1,0:T(8,128)(2,1)S(1)} collective-permute-done((bf16[272,128]{1,0:T(8,128)(2,1)}, bf16[272,128]{1,0:T(8,128)(2,1)S(1)}, u32[]{:S(2)}, u32[]{:S(2)}) %collective-permute-start.2) | collective-permute-done | bytes 69664 | tf_op jit(solution)/shard_map/ppermute | solution.py:345
  9.6 4.0 %collective-permute-done.1.p2 = bf16[272,128]{1,0:T(8,128)(2,1)S(1)} collective-permute-done((bf16[272,128]{1,0:T(8,128)(2,1)}, bf16[272,128]{1,0:T(8,128)(2,1)S(1)}, u32[]{:S(2)}, u32[]{:S(2)}) %collective-permute-start.1) | collective-permute-done | bytes 69664 | tf_op jit(solution)/shard_map/ppermute | solution.py:345
  13.6 0.0 copy-start
  13.6 0.0 copy-start.1
  13.6 0.0 copy-start.3
  13.7 0.0 copy-start.2
  13.7 1.6 %collective-permute-start.6 = (bf16[4,256,128]{2,1,0:T(8,128)(2,1)S(1)}, bf16[4,256,128]{2,1,0:T(8,128)(2,1)S(1)}, u32[]{:S(2)}, u32[]{:S(2)}) collective-permute-start(bf16[4,256,128]{2,1,0:T(8,128)(2,1)S(1)} %pad_maximum_fusion.refs_3_), channel_id=1, source_target_pairs={{0,16},{8,24},{16,32},{24,40},{32,48},{40,56},{48,0},{56,8},{64,80... | collective-permute-start | bytes 786440 | tf_op jit(solution)/shard_map/ppermute | solution.py:345
  15.3 2.7 %collective-permute-start.7 = (bf16[4,256,128]{2,1,0:T(8,128)(2,1)S(1)}, bf16[4,256,128]{2,1,0:T(8,128)(2,1)S(1)}, u32[]{:S(2)}, u32[]{:S(2)}) collective-permute-start(bf16[4,256,128]{2,1,0:T(8,128)(2,1)S(1)} %pad_maximum_fusion.refs_3_), channel_id=1, source_target_pairs={{0,32},{8,40},{16,48},{24,56},{32,0},{40,8},{48,16},{56,24},{64,96... | collective-permute-start | bytes 786440 | tf_op jit(solution)/shard_map/ppermute | solution.py:345
  18.0 1.4 %collective-permute-start.8 = (bf16[4,256,128]{2,1,0:T(8,128)(2,1)S(1)}, bf16[4,256,128]{2,1,0:T(8,128)(2,1)S(1)}, u32[]{:S(2)}, u32[]{:S(2)}) collective-permute-start(bf16[4,256,128]{2,1,0:T(8,128)(2,1)S(1)} %pad_maximum_fusion.refs_3_), channel_id=1, source_target_pairs={{0,48},{8,56},{16,0},{24,8},{32,16},{40,24},{48,32},{56,40},{64,11... | collective-permute-start | bytes 786440 | tf_op jit(solution)/shard_map/ppermute | solution.py:345
  19.4 0.6 shard_map.95
  20.0 0.8 %collective-permute-start.3 = (f32[8,128]{1,0:T(8,128)S(1)}, f32[8,128]{1,0:T(8,128)S(1)}, u32[]{:S(2)}, u32[]{:S(2)}) collective-permute-start(f32[8,128]{1,0:T(8,128)S(1)} %shard_map.95), channel_id=1, source_target_pairs={{0,1},{1,0},{2,3},{3,2},{4,5},{5,4},{6,7},{7,6},{8,9},{9,8},{10,11... | collective-permute-start | bytes 12296 | tf_op jit(solution)/shard_map/ppermute | solution.py:354
  20.9 2.9 %collective-permute-done.3 = f32[8,128]{1,0:T(8,128)S(1)} collective-permute-done((f32[8,128]{1,0:T(8,128)S(1)}, f32[8,128]{1,0:T(8,128)S(1)}, u32[]{:S(2)}, u32[]{:S(2)}) %collective-permute-start.3) | collective-permute-done | bytes 4128 | tf_op jit(solution)/shard_map/ppermute | solution.py:354
  23.7 0.2 collective-permute-start.4
  24.0 4.6 %collective-permute-done.4 = f32[8,128]{1,0:T(8,128)S(1)} collective-permute-done((f32[8,128]{1,0:T(8,128)S(1)}, f32[8,128]{1,0:T(8,128)S(1)}, u32[]{:S(2)}, u32[]{:S(2)}) %collective-permute-start.4) | collective-permute-done | bytes 4128 | tf_op jit(solution)/shard_map/ppermute | solution.py:354
  28.6 4.6 %collective-permute-start.5 = (f32[8,128]{1,0:T(8,128)S(1)}, f32[8,128]{1,0:T(8,128)S(1)}, u32[]{:S(2)}, u32[]{:S(2)}) collective-permute-start(f32[8,128]{1,0:T(8,128)S(1)} %add.19), channel_id=1, source_target_pairs={{0,132},{1,133},{2,134},{3,135},{4,128},{5,129},{6,130},{7,131},{8... | collective-permute-start | bytes 12296 | tf_op jit(solution)/shard_map/ppermute | solution.py:355
  33.1 1.6 %collective-permute-done.5 = f32[8,128]{1,0:T(8,128)S(1)} collective-permute-done((f32[8,128]{1,0:T(8,128)S(1)}, f32[8,128]{1,0:T(8,128)S(1)}, u32[]{:S(2)}, u32[]{:S(2)}) %collective-permute-start.5) | collective-permute-done | bytes 4128 | tf_op jit(solution)/shard_map/ppermute | solution.py:355
  34.8 0.1 collective-permute-start.10
  34.9 0.5 collective-permute-start.11
  35.3 0.1 collective-permute-start.12
  35.5 0.4 collective-permute-start.13
  35.9 0.1 collective-permute-start.9
  36.0 1.5 %collective-permute-done.9 = f32[8,128]{1,0:T(8,128)S(1)} collective-permute-done((f32[8,128]{1,0:T(8,128)S(1)}, f32[8,128]{1,0:T(8,128)S(1)}, u32[]{:S(2)}, u32[]{:S(2)}) %collective-permute-start.9) | collective-permute-done | bytes 4128 | tf_op jit(solution)/shard_map/ppermute | solution.py:345
  37.5 0.7 collective-permute-start.14
  38.2 2.8 %shard_map.96 = (f32[128,1024]{1,0:T(8,128)S(1)}, bf16[4,4,2,128,128]{4,3,2,1,0:T(8,128)(2,1)S(1)}, bf16[4,4,2,128,128]{4,3,2,1,0:T(8,128)(2,1)}) custom-call(s32[9]{0:T(128)S(1)} %copy-done.1, bf16[128,1024]{1,0:T(8,128)(2,1)S(1)} %copy-done.2, bf16[128,1024]{1,0:T(8,128)(2,1)S(1)} %copy-done.3, bf16[4,256,128]{2,1,0:T(8,128)(2,1)S(1)} %pad_maximum_fusion.refs_3_, ...), custom_call_target="tpu_custom_call" | custom-call | flops 10000000000 | bytes 5242880 | tf_op jit(solution)/shard_map/pallas_call | solution.py:160
  41.0 0.2 collective-permute-done.14
  41.2 0.5 collective-permute-start.15
  41.7 0.2 copy-done.4
  41.9 0.1 copy.10.p_ref
  42.0 4.2 %collective-permute-done.15 = f32[8,128]{1,0:T(8,128)S(1)} collective-permute-done((f32[8,128]{1,0:T(8,128)S(1)}, f32[8,128]{1,0:T(8,128)S(1)}, u32[]{:S(2)}, u32[]{:S(2)}) %collective-permute-start.15) | collective-permute-done | bytes 4128 | tf_op jit(solution)/shard_map/ppermute | solution.py:345
  46.2 1.2 %shard_map.97 = (bf16[4,2,128,128]{3,2,1,0:T(8,128)(2,1)S(1)}, bf16[4,2,128,128]{3,2,1,0:T(8,128)(2,1)S(1)}, bf16[4,2,128,128]{3,2,1,0:T(8,128)(2,1)S(1)}, bf16[...) custom-call(f32[8,128]{1,0:T(8,128)S(1)} %add.23.sums_ref, s32[9]{0:T(128)S(1)} %copy-done.1, s32[8,2]{1,0:T(8,128)S(1)} %copy.10.p_ref, ...), custom_call_target="tpu_custom_call" | custom-call | tf_op jit(solution)/shard_map/pallas_call | solution.py:296
  47.4 0.5 collective-permute-start.17
  47.8 1.8 %collective-permute-start.18 = (bf16[4,2,128,128]{3,2,1,0:T(8,128)(2,1)S(1)}, bf16[4,2,128,128]{3,2,1,0:T(8,128)(2,1)S(1)}, u32[]{:S(2)}, u32[]{:S(2)}) collective-permute-start(bf16[4,2,128,128]{3,2,1,0:T(8,128)(2,1)S(1)} %get-tuple-element.65), channel_id=1, source_target_pairs={{0,32},{8,40},{16,48},{24,56},{32,0},{40,8},{48,16},{56,24},{64,96... | collective-permute-start | bytes 786440 | tf_op jit(solution)/shard_map/ppermute | solution.py:345
  49.6 0.5 slice.19
  50.2 6.5 %collective-permute-done.17.i1 = bf16[4,2,128,128]{3,2,1,0:T(8,128)(2,1)S(1)} collective-permute-done((bf16[4,2,128,128]{3,2,1,0:T(8,128)(2,1)S(1)}, bf16[4,2,128,128]{3,2,1,0:T(8,128)(2,1)S(1)}, u32[]{:S(2)}, u32[]{:S(2)}) %collective-permute-start.17) | collective-permute-done | bytes 262176 | tf_op jit(solution)/shard_map/ppermute | solution.py:345
  56.7 1.9 %collective-permute-done.18.i2 = bf16[4,2,128,128]{3,2,1,0:T(8,128)(2,1)S(1)} collective-permute-done((bf16[4,2,128,128]{3,2,1,0:T(8,128)(2,1)S(1)}, bf16[4,2,128,128]{3,2,1,0:T(8,128)(2,1)S(1)}, u32[]{:S(2)}, u32[]{:S(2)}) %collective-permute-start.18) | collective-permute-done | bytes 262176 | tf_op jit(solution)/shard_map/ppermute | solution.py:345
  58.6 3.5 %collective-permute-done.19.i3 = bf16[4,2,128,128]{3,2,1,0:T(8,128)(2,1)S(1)} collective-permute-done((bf16[4,2,128,128]{3,2,1,0:T(8,128)(2,1)S(1)}, bf16[4,2,128,128]{3,2,1,0:T(8,128)(2,1)S(1)}, u32[]{:S(2)}, u32[]{:S(2)}) %collective-permute-start.19) | collective-permute-done | bytes 262176 | tf_op jit(solution)/shard_map/ppermute | solution.py:345
  62.2 0.1 shard_map.98
  62.3 11.3 %collective-permute-start.20 = (bf16[2,128,128]{2,1,0:T(8,128)(2,1)S(1)}, bf16[2,128,128]{2,1,0:T(8,128)(2,1)S(1)}, u32[]{:S(2)}, u32[]{:S(2)}) collective-permute-start(bf16[2,128,128]{2,1,0:T(8,128)(2,1)S(1)} %get-tuple-element.68), channel_id=1, source_target_pairs={{0,192},{8,200},{16,208},{24,216},{32,224},{40,232},{48,240},{56,2... | collective-permute-start | bytes 196616 | tf_op jit(solution)/shard_map/ppermute | solution.py:345
  73.6 0.7 collective-permute-start.22
  74.2 1.4 %multiply_convert_fusion = bf16[128,1024]{1,0:T(8,128)(2,1)} fusion(f32[128,1024]{1,0:T(8,128)S(1)} %get-tuple-element.56, f32[]{:T(128)} %bitcast.4), kind=kLoop, calls=%fused_computation | loop fusion | flops 262144 | bytes 786436 | tf_op jit(solution)/shard_map/convert_element_type | solution.py:367
  75.6 0.4 collective-permute-done.20.i1
  76.1 4.0 %collective-permute-done.21.i2 = bf16[2,128,128]{2,1,0:T(8,128)(2,1)S(1)} collective-permute-done((bf16[2,128,128]{2,1,0:T(8,128)(2,1)S(1)}, bf16[2,128,128]{2,1,0:T(8,128)(2,1)S(1)}, u32[]{:S(2)}, u32[]{:S(2)}) %collective-permute-start.21) | collective-permute-done | bytes 65568 | tf_op jit(solution)/shard_map/ppermute | solution.py:345
  80.1 0.7 shard_map.99
  (28 shorter events, 0.1 us)
Async XLA Ops:
  2.1 7.5 %collective-permute-start.2 = (bf16[272,128]{1,0:T(8,128)(2,1)}, bf16[272,128]{1,0:T(8,128)(2,1)S(1)}, u32[]{:S(2)}, u32[]{:S(2)}) collective-permute-start(bf16[272,128]{1,0:T(8,128)(2,1)} %shard_map.94.p0), channel_id=1, source_target_pairs={{0,192},{8,200},{16,208},{24,216},{32,224},{40,232},{48,240},{56,2... | collective-permute-start | bytes 208904 | tf_op jit(solution)/shard_map/ppermute | solution.py:345
  6.7 6.9 %collective-permute-start.1 = (bf16[272,128]{1,0:T(8,128)(2,1)}, bf16[272,128]{1,0:T(8,128)(2,1)S(1)}, u32[]{:S(2)}, u32[]{:S(2)}) collective-permute-start(bf16[272,128]{1,0:T(8,128)(2,1)} %shard_map.94.p0), channel_id=1, source_target_pairs={{0,128},{8,136},{16,144},{24,152},{32,160},{40,168},{48,176},{56,1... | collective-permute-start | bytes 208904 | tf_op jit(solution)/shard_map/ppermute | solution.py:345
  6.7 6.9 %collective-permute-start = (bf16[272,128]{1,0:T(8,128)(2,1)}, bf16[272,128]{1,0:T(8,128)(2,1)S(1)}, u32[]{:S(2)}, u32[]{:S(2)}) collective-permute-start(bf16[272,128]{1,0:T(8,128)(2,1)} %shard_map.94.p0), channel_id=1, source_target_pairs={{0,64},{8,72},{16,80},{24,88},{32,96},{40,104},{48,112},{56,120},{... | collective-permute-start | bytes 208904 | tf_op jit(solution)/shard_map/ppermute | solution.py:345
  13.6 5.8 %copy-start = (bf16[272,128]{1,0:T(8,128)(2,1)S(1)}, bf16[272,128]{1,0:T(8,128)(2,1)}, u32[]{:S(2)}) copy-start(bf16[272,128]{1,0:T(8,128)(2,1)} %shard_map.94.p0) | copy-start | bytes 208900
  13.6 5.8 %copy-start.1 = (s32[9]{0:T(128)S(1)}, s32[9]{0:T(128)}, u32[]{:S(2)}) copy-start(s32[9]{0:T(128)} %b_ref.3) | copy-start | bytes 112
  13.6 24.6 %copy-start.3 = (bf16[128,1024]{1,0:T(8,128)(2,1)S(1)}, bf16[128,1024]{1,0:T(8,128)(2,1)}, u32[]{:S(2)}) copy-start(bf16[128,1024]{1,0:T(8,128)(2,1)} %refs_2_.1) | copy-start | bytes 786436
  13.7 24.5 %copy-start.2 = (bf16[128,1024]{1,0:T(8,128)(2,1)S(1)}, bf16[128,1024]{1,0:T(8,128)(2,1)}, u32[]{:S(2)}) copy-start(bf16[128,1024]{1,0:T(8,128)(2,1)} %refs_1_.1) | copy-start | bytes 786436
  13.7 21.0 %collective-permute-start.6 = (bf16[4,256,128]{2,1,0:T(8,128)(2,1)S(1)}, bf16[4,256,128]{2,1,0:T(8,128)(2,1)S(1)}, u32[]{:S(2)}, u32[]{:S(2)}) collective-permute-start(bf16[4,256,128]{2,1,0:T(8,128)(2,1)S(1)} %pad_maximum_fusion.refs_3_), channel_id=1, source_target_pairs={{0,16},{8,24},{16,32},{24,40},{32,48},{40,56},{48,0},{56,8},{64,80... | collective-permute-start | bytes 786440 | tf_op jit(solution)/shard_map/ppermute | solution.py:345
  15.3 19.5 %collective-permute-start.7 = (bf16[4,256,128]{2,1,0:T(8,128)(2,1)S(1)}, bf16[4,256,128]{2,1,0:T(8,128)(2,1)S(1)}, u32[]{:S(2)}, u32[]{:S(2)}) collective-permute-start(bf16[4,256,128]{2,1,0:T(8,128)(2,1)S(1)} %pad_maximum_fusion.refs_3_), channel_id=1, source_target_pairs={{0,32},{8,40},{16,48},{24,56},{32,0},{40,8},{48,16},{56,24},{64,96... | collective-permute-start | bytes 786440 | tf_op jit(solution)/shard_map/ppermute | solution.py:345
  18.0 16.7 %collective-permute-start.8 = (bf16[4,256,128]{2,1,0:T(8,128)(2,1)S(1)}, bf16[4,256,128]{2,1,0:T(8,128)(2,1)S(1)}, u32[]{:S(2)}, u32[]{:S(2)}) collective-permute-start(bf16[4,256,128]{2,1,0:T(8,128)(2,1)S(1)} %pad_maximum_fusion.refs_3_), channel_id=1, source_target_pairs={{0,48},{8,56},{16,0},{24,8},{32,16},{40,24},{48,32},{56,40},{64,11... | collective-permute-start | bytes 786440 | tf_op jit(solution)/shard_map/ppermute | solution.py:345
  20.0 3.7 %collective-permute-start.3 = (f32[8,128]{1,0:T(8,128)S(1)}, f32[8,128]{1,0:T(8,128)S(1)}, u32[]{:S(2)}, u32[]{:S(2)}) collective-permute-start(f32[8,128]{1,0:T(8,128)S(1)} %shard_map.95), channel_id=1, source_target_pairs={{0,1},{1,0},{2,3},{3,2},{4,5},{5,4},{6,7},{7,6},{8,9},{9,8},{10,11... | collective-permute-start | bytes 12296 | tf_op jit(solution)/shard_map/ppermute | solution.py:354
  23.7 4.8 %collective-permute-start.4 = (f32[8,128]{1,0:T(8,128)S(1)}, f32[8,128]{1,0:T(8,128)S(1)}, u32[]{:S(2)}, u32[]{:S(2)}) collective-permute-start(f32[8,128]{1,0:T(8,128)S(1)} %add.18), channel_id=1, source_target_pairs={{0,3},{1,2},{2,1},{3,0},{4,7},{5,6},{6,5},{7,4},{8,11},{9,10},{10,... | collective-permute-start | bytes 12296 | tf_op jit(solution)/shard_map/ppermute | solution.py:354
  28.6 6.2 %collective-permute-start.5 = (f32[8,128]{1,0:T(8,128)S(1)}, f32[8,128]{1,0:T(8,128)S(1)}, u32[]{:S(2)}, u32[]{:S(2)}) collective-permute-start(f32[8,128]{1,0:T(8,128)S(1)} %add.19), channel_id=1, source_target_pairs={{0,132},{1,133},{2,134},{3,135},{4,128},{5,129},{6,130},{7,131},{8... | collective-permute-start | bytes 12296 | tf_op jit(solution)/shard_map/ppermute | solution.py:355
  34.8 2.8 %collective-permute-start.10 = (bf16[4,256,128]{2,1,0:T(8,128)(2,1)S(1)}, bf16[4,256,128]{2,1,0:T(8,128)(2,1)S(1)}, u32[]{:S(2)}, u32[]{:S(2)}) collective-permute-start(bf16[4,256,128]{2,1,0:T(8,128)(2,1)S(1)} %pad_maximum_fusion.refs_3_), channel_id=1, source_target_pairs={{0,8},{8,0},{16,24},{24,16},{32,40},{40,32},{48,56},{56,48},{64,72... | collective-permute-start | bytes 786440 | tf_op jit(solution)/shard_map/ppermute | solution.py:345
  34.9 2.7 %collective-permute-start.11 = (bf16[4,256,128]{2,1,0:T(8,128)(2,1)S(1)}, bf16[4,256,128]{2,1,0:T(8,128)(2,1)S(1)}, u32[]{:S(2)}, u32[]{:S(2)}) collective-permute-start(bf16[4,256,128]{2,1,0:T(8,128)(2,1)S(1)} %collective-permute-done.6.refs_4_), channel_id=1, source_target_pairs={{0,8},{8,0},{16,24},{24,16},{32,40},{40,32},{48,56},{56,48},{64,72... | collective-permute-start | bytes 786440 | tf_op jit(solution)/shard_map/ppermute | solution.py:345
  35.3 2.2 %collective-permute-start.12 = (bf16[4,256,128]{2,1,0:T(8,128)(2,1)S(1)}, bf16[4,256,128]{2,1,0:T(8,128)(2,1)S(1)}, u32[]{:S(2)}, u32[]{:S(2)}) collective-permute-start(bf16[4,256,128]{2,1,0:T(8,128)(2,1)S(1)} %collective-permute-done.7.refs_5_), channel_id=1, source_target_pairs={{0,8},{8,0},{16,24},{24,16},{32,40},{40,32},{48,56},{56,48},{64,72... | collective-permute-start | bytes 786440 | tf_op jit(solution)/shard_map/ppermute | solution.py:345
  35.5 2.1 %collective-permute-start.13 = (bf16[4,256,128]{2,1,0:T(8,128)(2,1)S(1)}, bf16[4,256,128]{2,1,0:T(8,128)(2,1)S(1)}, u32[]{:S(2)}, u32[]{:S(2)}) collective-permute-start(bf16[4,256,128]{2,1,0:T(8,128)(2,1)S(1)} %collective-permute-done.8.refs_6_), channel_id=1, source_target_pairs={{0,8},{8,0},{16,24},{24,16},{32,40},{40,32},{48,56},{56,48},{64,72... | collective-permute-start | bytes 786440 | tf_op jit(solution)/shard_map/ppermute | solution.py:345
  35.9 1.6 %collective-permute-start.9 = (f32[8,128]{1,0:T(8,128)S(1)}, f32[8,128]{1,0:T(8,128)S(1)}, u32[]{:S(2)}, u32[]{:S(2)}) collective-permute-start(f32[8,128]{1,0:T(8,128)S(1)} %add.20), channel_id=1, source_target_pairs={{0,8},{8,0},{16,24},{24,16},{32,40},{40,32},{48,56},{56,48},{64,72... | collective-permute-start | bytes 12296 | tf_op jit(solution)/shard_map/ppermute | solution.py:345
  37.5 3.7 %collective-permute-start.14 = (f32[8,128]{1,0:T(8,128)S(1)}, f32[8,128]{1,0:T(8,128)S(1)}, u32[]{:S(2)}, u32[]{:S(2)}) collective-permute-start(f32[8,128]{1,0:T(8,128)S(1)} %add.21), channel_id=1, source_target_pairs={{0,16},{8,24},{16,0},{24,8},{32,48},{40,56},{48,32},{56,40},{64,80... | collective-permute-start | bytes 12296 | tf_op jit(solution)/shard_map/ppermute | solution.py:345
  41.2 0.7 copy-start.4
  41.2 4.9 %collective-permute-start.16 = (bf16[4,4,2,128,128]{4,3,2,1,0:T(8,128)(2,1)}, bf16[4,4,2,128,128]{4,3,2,1,0:T(8,128)(2,1)S(1)}, u32[]{:S(2)}, u32[]{:S(2)}) collective-permute-start(bf16[4,4,2,128,128]{4,3,2,1,0:T(8,128)(2,1)} %get-tuple-element.61), channel_id=1, source_target_pairs={{0,8},{8,0},{16,24},{24,16},{32,40},{40,32},{48,56},{56,48},{64,72... | collective-permute-start | bytes 3145736 | tf_op jit(solution)/shard_map/ppermute | solution.py:345
  41.2 4.9 %collective-permute-start.15 = (f32[8,128]{1,0:T(8,128)S(1)}, f32[8,128]{1,0:T(8,128)S(1)}, u32[]{:S(2)}, u32[]{:S(2)}) collective-permute-start(f32[8,128]{1,0:T(8,128)S(1)} %add.22), channel_id=1, source_target_pairs={{0,48},{8,56},{16,32},{24,40},{32,16},{40,24},{48,0},{56,8},{64,11... | collective-permute-start | bytes 12296 | tf_op jit(solution)/shard_map/ppermute | solution.py:345
  47.4 9.3 %collective-permute-start.17 = (bf16[4,2,128,128]{3,2,1,0:T(8,128)(2,1)S(1)}, bf16[4,2,128,128]{3,2,1,0:T(8,128)(2,1)S(1)}, u32[]{:S(2)}, u32[]{:S(2)}) collective-permute-start(bf16[4,2,128,128]{3,2,1,0:T(8,128)(2,1)S(1)} %get-tuple-element.64), channel_id=1, source_target_pairs={{0,48},{8,56},{16,0},{24,8},{32,16},{40,24},{48,32},{56,40},{64,11... | collective-permute-start | bytes 786440 | tf_op jit(solution)/shard_map/ppermute | solution.py:345
  47.8 10.8 %collective-permute-start.18 = (bf16[4,2,128,128]{3,2,1,0:T(8,128)(2,1)S(1)}, bf16[4,2,128,128]{3,2,1,0:T(8,128)(2,1)S(1)}, u32[]{:S(2)}, u32[]{:S(2)}) collective-permute-start(bf16[4,2,128,128]{3,2,1,0:T(8,128)(2,1)S(1)} %get-tuple-element.65), channel_id=1, source_target_pairs={{0,32},{8,40},{16,48},{24,56},{32,0},{40,8},{48,16},{56,24},{64,96... | collective-permute-start | bytes 786440 | tf_op jit(solution)/shard_map/ppermute | solution.py:345
  49.6 12.5 %collective-permute-start.19 = (bf16[4,2,128,128]{3,2,1,0:T(8,128)(2,1)S(1)}, bf16[4,2,128,128]{3,2,1,0:T(8,128)(2,1)S(1)}, u32[]{:S(2)}, u32[]{:S(2)}) collective-permute-start(bf16[4,2,128,128]{3,2,1,0:T(8,128)(2,1)S(1)} %get-tuple-element.66), channel_id=1, source_target_pairs={{0,16},{8,24},{16,32},{24,40},{32,48},{40,56},{48,0},{56,8},{64,80... | collective-permute-start | bytes 786440 | tf_op jit(solution)/shard_map/ppermute | solution.py:345
  62.3 13.8 %collective-permute-start.20 = (bf16[2,128,128]{2,1,0:T(8,128)(2,1)S(1)}, bf16[2,128,128]{2,1,0:T(8,128)(2,1)S(1)}, u32[]{:S(2)}, u32[]{:S(2)}) collective-permute-start(bf16[2,128,128]{2,1,0:T(8,128)(2,1)S(1)} %get-tuple-element.68), channel_id=1, source_target_pairs={{0,192},{8,200},{16,208},{24,216},{32,224},{40,232},{48,240},{56,2... | collective-permute-start | bytes 196616 | tf_op jit(solution)/shard_map/ppermute | solution.py:345
  73.6 6.5 %collective-permute-start.21 = (bf16[2,128,128]{2,1,0:T(8,128)(2,1)S(1)}, bf16[2,128,128]{2,1,0:T(8,128)(2,1)S(1)}, u32[]{:S(2)}, u32[]{:S(2)}) collective-permute-start(bf16[2,128,128]{2,1,0:T(8,128)(2,1)S(1)} %get-tuple-element.69), channel_id=1, source_target_pairs={{0,128},{8,136},{16,144},{24,152},{32,160},{40,168},{48,176},{56,1... | collective-permute-start | bytes 196616 | tf_op jit(solution)/shard_map/ppermute | solution.py:345
  73.6 6.5 %collective-permute-start.22 = (bf16[2,128,128]{2,1,0:T(8,128)(2,1)S(1)}, bf16[2,128,128]{2,1,0:T(8,128)(2,1)S(1)}, u32[]{:S(2)}, u32[]{:S(2)}) collective-permute-start(bf16[2,128,128]{2,1,0:T(8,128)(2,1)S(1)} %get-tuple-element.70), channel_id=1, source_target_pairs={{0,64},{8,72},{16,80},{24,88},{32,96},{40,104},{48,112},{56,120},{... | collective-permute-start | bytes 196616 | tf_op jit(solution)/shard_map/ppermute | solution.py:345

commit v3 on v2

--- a/solution.py
+++ b/solution.py
@@ -28,7 +28,7 @@
 
 def attend_body(
     bounds, q_ref, do_ref, bufs, dq_ref, keep_ref, send_ref,
-    kk, vv, q2, g2, pb, dp_s, mt, mx, sm, dl, acc, sem,
+    kv, q2, g2, pb, dp_s, mt, mx, sm, dl, acc, sem,
 ):
     me = lax.axis_index("seq")
     prompt = bounds[0] // BLOCK
@@ -48,22 +48,16 @@
         column = lax.rem(lax.rem(j, 2) + c, 2) * 4 + lax.rem(x - lax.rem(j // 2, 4) + 4, 4)
         return column, lax.rem(z - j // 8 + 4, 4)
 
-    def rows_of(t):
-        return pl.ds(pl.multiple_of(t * BLOCK, BLOCK), BLOCK)
-
-    def fetch(t, _):
-        b, sz = where_is(t)
+    for zz in range(4):
+        sz = lax.rem(z + 4 - zz, 4)
         for nb, buf in enumerate(bufs):
-
-            @pl.when(b == nb)
-            def _(buf=buf):
-                key, value = buf.at[sz, pl.ds(0, BLOCK)], buf.at[sz, pl.ds(BLOCK, BLOCK)]
-                pltpu.make_async_copy(key, kk.at[rows_of(t)], sem.at[0, t]).start()
-                pltpu.make_async_copy(value, vv.at[rows_of(t)], sem.at[1, t]).start()
-
-        return 0
-
-    lax.fori_loop(0, n, fetch, 0)
+            j = zz * 8 + lax.rem(x + 4 - nb % 4, 4) * 2 + lax.rem(c + nb // 4, 2)
+            t = jnp.where(j < prompt, j, j - start + prompt)
+
+            @pl.when(live & (j <= me) & ((j < prompt) | (j >= start)))
+            def _(buf=buf, sz=sz, t=t):
+                pltpu.make_async_copy(buf.at[sz], kv.at[t], sem.at[t]).start()
+
     for h in range(GROUP):
         at = slice(h * DH, (h + 1) * DH)
         q2[h * BLOCK : (h + 1) * BLOCK, :] = q_ref[:, at]
@@ -76,21 +70,23 @@
     acc[...] = jnp.zeros_like(acc)
 
     def pad(t, _):
-        kk[rows_of(t), :] = jnp.zeros((BLOCK, DH), bf)
-        vv[rows_of(t), :] = jnp.zeros((BLOCK, DH), bf)
+        kv[t] = jnp.zeros((2 * BLOCK, DH), bf)
         return 0
 
     lax.fori_loop(n, chunks * NB, pad, 0)
 
     def land(t, _):
-        pltpu.make_async_copy(bufs[0].at[0, pl.ds(0, BLOCK)], kk.at[rows_of(t)], sem.at[0, t]).wait()
-        pltpu.make_async_copy(bufs[0].at[0, pl.ds(0, BLOCK)], vv.at[rows_of(t)], sem.at[1, t]).wait()
+        pltpu.make_async_copy(bufs[0].at[0], kv.at[t], sem.at[t]).wait()
         return 0
+
+    def part_of(i, kvi):
+        blocks = kv[pl.ds(i * NB, NB), kvi * BLOCK : (kvi + 1) * BLOCK, :]
+        return blocks.reshape(KC, DH)
 
     def forward(i, masked):
         rows = pl.ds(pl.multiple_of(i * KC, KC), KC)
         lax.fori_loop(i * NB, jnp.minimum(i * NB + NB, n), land, 0)
-        s = lax.dot_general(kk[rows, :], q2[...], NT, preferred_element_type=f32) * c2
+        s = lax.dot_general(part_of(i, 0), q2[...], NT, preferred_element_type=f32) * c2
         if masked:
             key = lax.broadcasted_iota(jnp.int32, (KC, ROWS), 0) + i * KC - (n - 1) * BLOCK
             query = lax.rem(lax.broadcasted_iota(jnp.int32, (KC, ROWS), 1), BLOCK)
@@ -99,7 +95,7 @@
         top = jnp.max(s.reshape(KC // 8, 8, ROWS), axis=0)
         new = jnp.maximum(old, jnp.max(top, axis=0, keepdims=True))
         p = jnp.exp2(s - new)
-        dp = lax.dot_general(vv[rows, :], g2[...], NT, preferred_element_type=f32)
+        dp = lax.dot_general(part_of(i, 1), g2[...], NT, preferred_element_type=f32)
         fade = jnp.exp2(old - new)
         sm[...] = sm[...] * fade + jnp.sum(p.reshape(KC // 8, 8, ROWS), axis=0)
         dl[...] = dl[...] * fade + jnp.sum((p * dp).reshape(KC // 8, 8, ROWS), axis=0)
@@ -128,7 +124,7 @@
         g = (p * (dp_s[rows, :] - dl[0:1, :])).astype(bf)
         dk = lax.dot_general(g, q2[...], NN, preferred_element_type=f32)
         dv = lax.dot_general(p.astype(bf), g2[...], NN, preferred_element_type=f32)
-        acc[...] += lax.dot_general(kk[rows, :].T, g, NN, preferred_element_type=f32)
+        acc[...] += lax.dot_general(part_of(i, 0).T, g, NN, preferred_element_type=f32)
         for u in range(NB):
             t = i * NB + u
             b, sz = where_is(t)
@@ -163,8 +159,7 @@
         in_specs=[S, V, V] + [A] * nb,
         out_specs=(V, V, V),
         scratch_shapes=[
-            pltpu.VMEM((32 * BLOCK, DH), bf),
-            pltpu.VMEM((32 * BLOCK, DH), bf),
+            pltpu.VMEM((32, 2 * BLOCK, DH), bf),
             pltpu.VMEM((ROWS, DH), bf),
             pltpu.VMEM((ROWS, DH), bf),
             pltpu.VMEM((32 * BLOCK, ROWS), bf),
@@ -174,9 +169,9 @@
             pltpu.VMEM((8, ROWS), f32),
             pltpu.VMEM((8, ROWS), f32),
             pltpu.VMEM((DH, ROWS), f32),
-            pltpu.SemaphoreType.DMA((2, 32)),
+            pltpu.SemaphoreType.DMA((32,)),
         ],
-        compiler_params=pltpu.CompilerParams(vmem_limit_bytes=44 * 2**20),
+        compiler_params=pltpu.CompilerParams(vmem_limit_bytes=36 * 2**20),
         cost_estimate=pl.CostEstimate(
             flops=10**10, bytes_accessed=5 * 2**20, transcendentals=2**22
         ),
@@ -238,24 +233,32 @@
 
 
 def block_sums(bounds, packets):
-    def kern(b_ref, p0, p1, p2, p3, sums_ref):
+    def kern(b_ref, p0, p1, p2, p3, sums_ref, rides, sem):
+        copies = [
+            pltpu.make_async_copy(p.at[pl.ds(2 * BLOCK, 16)], rides.at[k], sem.at[k])
+            for k, p in enumerate((p0, p1, p2, p3))
+        ]
+        for copy in copies:
+            copy.start()
         me = lax.axis_index("seq")
         row = lax.broadcasted_iota(jnp.int32, (RESP, DH), 0)
         sums = jnp.zeros((RESP, DH), f32)
-        for s, packet in enumerate((p0, p1, p2, p3)):
+        for s in range(4):
             first = (lax.rem(me // 8 - s + 4, 4) * 8 + lax.rem(me, 8)) * BLOCK
             resp = jnp.int32(-1)
             for r in range(RESP):
                 resp = resp + (first >= b_ref[r]).astype(jnp.int32)
-            part = jnp.sum(packet[2 * BLOCK :, :].astype(f32), axis=0, keepdims=True)
+            copies[s].wait()
+            part = jnp.sum(rides[s].astype(f32), axis=0, keepdims=True)
             sums = sums + jnp.where(row == resp, part, 0.0)
         sums_ref[...] = sums
 
     return pl.pallas_call(
         kern,
         out_shape=jax.ShapeDtypeStruct((RESP, DH), f32),
-        in_specs=[S, V, V, V, V],
+        in_specs=[S, A, A, A, A],
         out_specs=V,
+        scratch_shapes=[pltpu.VMEM((4, 16, DH), bf), pltpu.SemaphoreType.DMA((4,))],
         compiler_params=SMALL,
     )(bounds, *packets)
 
@@ -348,10 +351,15 @@
     by_z = [packet] + [seq(packet, Z_UP[s]) for s in (1, 2, 3)]
     column = jnp.stack([p[: 2 * BLOCK] for p in by_z])
     column, by_z = lax.optimization_barrier((column, by_z))
-    by_x = [column] + [seq(column, X_UP[s]) for s in (1, 2, 3)]
-    sums = block_sums(bounds, by_z)
-    for turn in HEAD_Y:
-        sums = sums + lax.ppermute(sums, "heads", turn)
+    far = seq(column, X_UP[2])
+    sums, column = lax.optimization_barrier((block_sums(bounds, by_z), column))
+    turned = lax.ppermute(sums, "heads", HEAD_Y[0])
+    before = seq(column, X_UP[1])
+    sums, column = lax.optimization_barrier((sums + turned, column))
+    turned = lax.ppermute(sums, "heads", HEAD_Y[1])
+    after = seq(column, X_UP[3])
+    sums = sums + turned
+    by_x = [column, before, far, after]
     sums = sums + lax.ppermute(sums, ("seq", "heads"), HALVES)
     sums, by_x = lax.optimization_barrier((sums, by_x))
     bufs = by_x + [seq(b, CORE) for b in by_x]

time: 80.8 us -> 77.3 us (0.957)
  waiting for transfers between devices: 36.7 us -> 31.1 us
  starting transfers between devices: 33.2 us -> 34.9 us
    ppermute x2, waiting for transfers between devices: 7.46 us -> 3.76 us  [the longest x1 3.76 us: shards(): turned = lax.ppermute(sums, 'heads', HEAD_Y[1])]
    ppermute x20, waiting for transfers between devices: 27.7 us -> 25.8 us  [seq(): return lax.ppermute(v, 'seq', perm)]
    ppermute x20, starting transfers between devices: 27.6 us -> 28.5 us  [seq(): return lax.ppermute(v, 'seq', perm)]
    ppermute x2, starting transfers between devices: 1.05 us -> 1.89 us  [the longest x1 1.06 us: shards(): turned = lax.ppermute(sums, 'heads', HEAD_Y[1])]
where the time goes in v3:
time: 77.3 us; the launch traced here: 77.5 us
  starting transfers between devices  34.9 us (45%)
  waiting for transfers between devices  31.1 us (40%)
  Pallas kernels  6.93 us (9%)
  local copies, waits for them, and re-layouts  2.31 us (3%)
  other arithmetic  1.44 us (2%)
  between operations  0.79 us (1%)
    ppermute x20, starting transfers between devices, seq(): return lax.ppermute(v, 'seq', perm)  28.5 us
    ppermute x20, waiting for transfers between devices, seq(): return lax.ppermute(v, 'seq', perm)  25.8 us
    ppermute x1, starting transfers between devices, shards(): sums = sums + lax.ppermute(sums, ('seq', 'heads'), HALVES)  4.58 us
    ppermute x1, waiting for transfers between devices, shards(): turned = lax.ppermute(sums, 'heads', HEAD_Y[1])  3.76 us
    pallas_call x1, Pallas kernels, attend(): pl.pallas_call(kern, out_shape=(jax.ShapeDtypeStruct((BLOCK, ROWS), f32),...  2.8 us
    ppermute x1, waiting for transfers between devices, shards(): sums = sums + lax.ppermute(sums, ('seq', 'heads'), HALVES)  1.58 us
  transfers between devices with their start and end apart: 23, of which 13 were waited for; matrix products, arithmetic and copies ran while one was open for 4% of the time, Pallas kernels for 4%

profile of v3, /device:TPU:24, one launch (start us, length us, event | category | flops | bytes accessed | tf_op | source)
XLA Modules:
  0.0 77.5 jit_solution(9887683350370109043)
XLA Ops:
  0.6 1.5 %shard_map.94.p0 = bf16[272,128]{1,0:T(8,128)(2,1)} custom-call(bf16[128,128]{1,0:T(8,128)(2,1)} %k_ref.1, bf16[128,128]{1,0:T(8,128)(2,1)} %v_ref.1, f32[16]{0:T(128)} %ratio_ref.1), custom_call_target="tpu_custom_call" | custom-call | tf_op jit(solution)/shard_map/pallas_call | solution.py:227
  2.1 4.6 %collective-permute-start.2 = (bf16[272,128]{1,0:T(8,128)(2,1)}, bf16[272,128]{1,0:T(8,128)(2,1)S(1)}, u32[]{:S(2)}, u32[]{:S(2)}) collective-permute-start(bf16[272,128]{1,0:T(8,128)(2,1)} %shard_map.94.p0), channel_id=1, source_target_pairs={{0,192},{8,200},{16,208},{24,216},{32,224},{40,232},{48,240},{56,2... | collective-permute-start | bytes 208904 | tf_op jit(solution)/shard_map/ppermute | solution.py:348
  6.7 0.0 collective-permute-start.1
  6.7 0.7 collective-permute-start
  7.4 0.9 %slice_bitcast_fusion.3 = bf16[1,256,128]{2,1,0:T(8,128)(2,1)S(1)} fusion(bf16[272,128]{1,0:T(8,128)(2,1)} %shard_map.94.p0), kind=kLoop, calls=%fused_computation.5 | loop fusion | bytes 131072 | tf_op jit(solution)/shard_map/stack | solution.py:352
  8.3 1.4 %collective-permute-done.2.p3 = bf16[272,128]{1,0:T(8,128)(2,1)S(1)} collective-permute-done((bf16[272,128]{1,0:T(8,128)(2,1)}, bf16[272,128]{1,0:T(8,128)(2,1)S(1)}, u32[]{:S(2)}, u32[]{:S(2)}) %collective-permute-start.2) | collective-permute-done | bytes 69664 | tf_op jit(solution)/shard_map/ppermute | solution.py:348
  9.6 4.0 %collective-permute-done.1.p2 = bf16[272,128]{1,0:T(8,128)(2,1)S(1)} collective-permute-done((bf16[272,128]{1,0:T(8,128)(2,1)}, bf16[272,128]{1,0:T(8,128)(2,1)S(1)}, u32[]{:S(2)}, u32[]{:S(2)}) %collective-permute-start.1) | collective-permute-done | bytes 69664 | tf_op jit(solution)/shard_map/ppermute | solution.py:348
  13.6 0.0 collective-permute-done.p1
  13.6 0.0 copy-start
  13.6 0.0 copy-start.1
  13.6 0.0 copy-start.3
  13.7 0.8 %copy-done = bf16[272,128]{1,0:T(8,128)(2,1)S(1)} copy-done((bf16[272,128]{1,0:T(8,128)(2,1)S(1)}, bf16[272,128]{1,0:T(8,128)(2,1)}, u32[]{:S(2)}) %copy-start) | copy-done | bytes 69656
  14.5 0.7 shard_map.95
  15.2 0.8 %collective-permute-start.3 = (f32[8,128]{1,0:T(8,128)S(1)}, f32[8,128]{1,0:T(8,128)S(1)}, u32[]{:S(2)}, u32[]{:S(2)}) collective-permute-start(f32[8,128]{1,0:T(8,128)S(1)} %shard_map.95), channel_id=1, source_target_pairs={{0,1},{1,0},{2,3},{3,2},{4,5},{5,4},{6,7},{7,6},{8,9},{9,8},{10,11... | collective-permute-start | bytes 12296 | tf_op jit(solution)/shard_map/ppermute | solution.py:356
  16.0 3.0 %collective-permute-start.7 = (bf16[4,256,128]{2,1,0:T(8,128)(2,1)S(1)}, bf16[4,256,128]{2,1,0:T(8,128)(2,1)S(1)}, u32[]{:S(2)}, u32[]{:S(2)}) collective-permute-start(bf16[4,256,128]{2,1,0:T(8,128)(2,1)S(1)} %pad_maximum_fusion.refs_3_), channel_id=1, source_target_pairs={{0,32},{8,40},{16,48},{24,56},{32,0},{40,8},{48,16},{56,24},{64,96... | collective-permute-start | bytes 786440 | tf_op jit(solution)/shard_map/ppermute | solution.py:348
  19.0 0.6 collective-permute-start.6
  19.6 2.6 %collective-permute-start.8 = (bf16[4,256,128]{2,1,0:T(8,128)(2,1)S(1)}, bf16[4,256,128]{2,1,0:T(8,128)(2,1)S(1)}, u32[]{:S(2)}, u32[]{:S(2)}) collective-permute-start(bf16[4,256,128]{2,1,0:T(8,128)(2,1)S(1)} %pad_maximum_fusion.refs_3_), channel_id=1, source_target_pairs={{0,48},{8,56},{16,0},{24,8},{32,16},{40,24},{48,32},{56,40},{64,11... | collective-permute-start | bytes 786440 | tf_op jit(solution)/shard_map/ppermute | solution.py:348
  22.3 1.1 %collective-permute-start.4 = (f32[8,128]{1,0:T(8,128)S(1)}, f32[8,128]{1,0:T(8,128)S(1)}, u32[]{:S(2)}, u32[]{:S(2)}) collective-permute-start(f32[8,128]{1,0:T(8,128)S(1)} %add.18), channel_id=1, source_target_pairs={{0,3},{1,2},{2,1},{3,0},{4,7},{5,6},{6,5},{7,4},{8,11},{9,10},{10,... | collective-permute-start | bytes 12296 | tf_op jit(solution)/shard_map/ppermute | solution.py:359
  23.3 3.8 %collective-permute-done.4 = f32[8,128]{1,0:T(8,128)S(1)} collective-permute-done((f32[8,128]{1,0:T(8,128)S(1)}, f32[8,128]{1,0:T(8,128)S(1)}, u32[]{:S(2)}, u32[]{:S(2)}) %collective-permute-start.4) | collective-permute-done | bytes 4128 | tf_op jit(solution)/shard_map/ppermute | solution.py:359
  27.1 4.6 %collective-permute-start.5 = (f32[8,128]{1,0:T(8,128)S(1)}, f32[8,128]{1,0:T(8,128)S(1)}, u32[]{:S(2)}, u32[]{:S(2)}) collective-permute-start(f32[8,128]{1,0:T(8,128)S(1)} %add.19), channel_id=1, source_target_pairs={{0,132},{1,133},{2,134},{3,135},{4,128},{5,129},{6,130},{7,131},{8... | collective-permute-start | bytes 12296 | tf_op jit(solution)/shard_map/ppermute | solution.py:363
  31.7 1.6 %collective-permute-done.5 = f32[8,128]{1,0:T(8,128)S(1)} collective-permute-done((f32[8,128]{1,0:T(8,128)S(1)}, f32[8,128]{1,0:T(8,128)S(1)}, u32[]{:S(2)}, u32[]{:S(2)}) %collective-permute-start.5) | collective-permute-done | bytes 4128 | tf_op jit(solution)/shard_map/ppermute | solution.py:363
  33.3 0.1 collective-permute-start.10
  33.4 0.5 collective-permute-start.11
  33.9 0.1 collective-permute-start.12
  34.0 0.4 collective-permute-start.13
  34.4 0.1 collective-permute-start.9
  34.5 1.5 %collective-permute-done.9 = f32[8,128]{1,0:T(8,128)S(1)} collective-permute-done((f32[8,128]{1,0:T(8,128)S(1)}, f32[8,128]{1,0:T(8,128)S(1)}, u32[]{:S(2)}, u32[]{:S(2)}) %collective-permute-start.9) | collective-permute-done | bytes 4128 | tf_op jit(solution)/shard_map/ppermute | solution.py:348
  36.1 0.1 collective-permute-start.14
  36.2 2.8 %shard_map.96 = (f32[128,1024]{1,0:T(8,128)S(1)}, bf16[4,4,2,128,128]{4,3,2,1,0:T(8,128)(2,1)S(1)}, bf16[4,4,2,128,128]{4,3,2,1,0:T(8,128)(2,1)}) custom-call(s32[9]{0:T(128)S(1)} %copy-done.1, bf16[128,1024]{1,0:T(8,128)(2,1)S(1)} %copy-done.2, bf16[128,1024]{1,0:T(8,128)(2,1)S(1)} %copy-done.3, bf16[4,256,128]{2,1,0:T(8,128)(2,1)S(1)} %pad_maximum_fusion.refs_3_, ...), custom_call_target="tpu_custom_call" | custom-call | flops 10000000000 | bytes 5242880 | tf_op jit(solution)/shard_map/pallas_call | solution.py:156
  39.0 0.8 collective-permute-done.14
  39.8 4.6 %collective-permute-start.15 = (f32[8,128]{1,0:T(8,128)S(1)}, f32[8,128]{1,0:T(8,128)S(1)}, u32[]{:S(2)}, u32[]{:S(2)}) collective-permute-start(f32[8,128]{1,0:T(8,128)S(1)} %add.22), channel_id=1, source_target_pairs={{0,48},{8,56},{16,32},{24,40},{32,16},{40,24},{48,0},{56,8},{64,11... | collective-permute-start | bytes 12296 | tf_op jit(solution)/shard_map/ppermute | solution.py:348
  44.4 0.1 copy.10.p_ref
  44.5 1.5 %collective-permute-done.15 = f32[8,128]{1,0:T(8,128)S(1)} collective-permute-done((f32[8,128]{1,0:T(8,128)S(1)}, f32[8,128]{1,0:T(8,128)S(1)}, u32[]{:S(2)}, u32[]{:S(2)}) %collective-permute-start.15) | collective-permute-done | bytes 4128 | tf_op jit(solution)/shard_map/ppermute | solution.py:348
  46.0 1.2 %shard_map.97 = (bf16[4,2,128,128]{3,2,1,0:T(8,128)(2,1)S(1)}, bf16[4,2,128,128]{3,2,1,0:T(8,128)(2,1)S(1)}, bf16[4,2,128,128]{3,2,1,0:T(8,128)(2,1)S(1)}, bf16[...) custom-call(f32[8,128]{1,0:T(8,128)S(1)} %add.23.sums_ref, s32[9]{0:T(128)S(1)} %copy-done.1, s32[8,2]{1,0:T(8,128)S(1)} %copy.10.p_ref, ...), custom_call_target="tpu_custom_call" | custom-call | tf_op jit(solution)/shard_map/pallas_call | solution.py:299
  47.2 3.3 %collective-permute-start.17 = (bf16[4,2,128,128]{3,2,1,0:T(8,128)(2,1)S(1)}, bf16[4,2,128,128]{3,2,1,0:T(8,128)(2,1)S(1)}, u32[]{:S(2)}, u32[]{:S(2)}) collective-permute-start(bf16[4,2,128,128]{3,2,1,0:T(8,128)(2,1)S(1)} %get-tuple-element.72), channel_id=1, source_target_pairs={{0,48},{8,56},{16,0},{24,8},{32,16},{40,24},{48,32},{56,40},{64,11... | collective-permute-start | bytes 786440 | tf_op jit(solution)/shard_map/ppermute | solution.py:348
  50.5 1.0 %collective-permute-start.19 = (bf16[4,2,128,128]{3,2,1,0:T(8,128)(2,1)S(1)}, bf16[4,2,128,128]{3,2,1,0:T(8,128)(2,1)S(1)}, u32[]{:S(2)}, u32[]{:S(2)}) collective-permute-start(bf16[4,2,128,128]{3,2,1,0:T(8,128)(2,1)S(1)} %get-tuple-element.74), channel_id=1, source_target_pairs={{0,16},{8,24},{16,32},{24,40},{32,48},{40,56},{48,0},{56,8},{64,80... | collective-permute-start | bytes 786440 | tf_op jit(solution)/shard_map/ppermute | solution.py:348
  51.5 0.5 slice.19
  52.0 9.2 %collective-permute-done.17.i1 = bf16[4,2,128,128]{3,2,1,0:T(8,128)(2,1)S(1)} collective-permute-done((bf16[4,2,128,128]{3,2,1,0:T(8,128)(2,1)S(1)}, bf16[4,2,128,128]{3,2,1,0:T(8,128)(2,1)S(1)}, u32[]{:S(2)}, u32[]{:S(2)}) %collective-permute-start.17) | collective-permute-done | bytes 262176 | tf_op jit(solution)/shard_map/ppermute | solution.py:348
  61.1 0.1 collective-permute-done.18.i2
  61.3 3.3 %collective-permute-done.19.i3 = bf16[4,2,128,128]{3,2,1,0:T(8,128)(2,1)S(1)} collective-permute-done((bf16[4,2,128,128]{3,2,1,0:T(8,128)(2,1)S(1)}, bf16[4,2,128,128]{3,2,1,0:T(8,128)(2,1)S(1)}, u32[]{:S(2)}, u32[]{:S(2)}) %collective-permute-start.19) | collective-permute-done | bytes 262176 | tf_op jit(solution)/shard_map/ppermute | solution.py:348
  64.5 0.1 shard_map.98
  64.7 6.1 %collective-permute-start.20 = (bf16[2,128,128]{2,1,0:T(8,128)(2,1)S(1)}, bf16[2,128,128]{2,1,0:T(8,128)(2,1)S(1)}, u32[]{:S(2)}, u32[]{:S(2)}) collective-permute-start(bf16[2,128,128]{2,1,0:T(8,128)(2,1)S(1)} %get-tuple-element.76), channel_id=1, source_target_pairs={{0,192},{8,200},{16,208},{24,216},{32,224},{40,232},{48,240},{56,2... | collective-permute-start | bytes 196616 | tf_op jit(solution)/shard_map/ppermute | solution.py:348
  70.8 0.7 collective-permute-start.22
  71.4 1.4 %multiply_convert_fusion = bf16[128,1024]{1,0:T(8,128)(2,1)} fusion(f32[128,1024]{1,0:T(8,128)S(1)} %get-tuple-element.64, f32[]{:T(128)} %bitcast.4), kind=kLoop, calls=%fused_computation | loop fusion | flops 262144 | bytes 786436 | tf_op jit(solution)/shard_map/convert_element_type | solution.py:375
  72.8 0.5 collective-permute-done.20.i1
  73.3 2.9 %collective-permute-done.21.i2 = bf16[2,128,128]{2,1,0:T(8,128)(2,1)S(1)} collective-permute-done((bf16[2,128,128]{2,1,0:T(8,128)(2,1)S(1)}, bf16[2,128,128]{2,1,0:T(8,128)(2,1)S(1)}, u32[]{:S(2)}, u32[]{:S(2)}) %collective-permute-start.21) | collective-permute-done | bytes 65568 | tf_op jit(solution)/shard_map/ppermute | solution.py:348
  76.2 0.7 collective-permute-done.22.i3
  76.9 0.7 shard_map.99
  (28 shorter events, 0.1 us)
Async XLA Ops:
  2.1 7.5 %collective-permute-start.2 = (bf16[272,128]{1,0:T(8,128)(2,1)}, bf16[272,128]{1,0:T(8,128)(2,1)S(1)}, u32[]{:S(2)}, u32[]{:S(2)}) collective-permute-start(bf16[272,128]{1,0:T(8,128)(2,1)} %shard_map.94.p0), channel_id=1, source_target_pairs={{0,192},{8,200},{16,208},{24,216},{32,224},{40,232},{48,240},{56,2... | collective-permute-start | bytes 208904 | tf_op jit(solution)/shard_map/ppermute | solution.py:348
  6.7 6.9 %collective-permute-start.1 = (bf16[272,128]{1,0:T(8,128)(2,1)}, bf16[272,128]{1,0:T(8,128)(2,1)S(1)}, u32[]{:S(2)}, u32[]{:S(2)}) collective-permute-start(bf16[272,128]{1,0:T(8,128)(2,1)} %shard_map.94.p0), channel_id=1, source_target_pairs={{0,128},{8,136},{16,144},{24,152},{32,160},{40,168},{48,176},{56,1... | collective-permute-start | bytes 208904 | tf_op jit(solution)/shard_map/ppermute | solution.py:348
  6.7 6.9 %collective-permute-start = (bf16[272,128]{1,0:T(8,128)(2,1)}, bf16[272,128]{1,0:T(8,128)(2,1)S(1)}, u32[]{:S(2)}, u32[]{:S(2)}) collective-permute-start(bf16[272,128]{1,0:T(8,128)(2,1)} %shard_map.94.p0), channel_id=1, source_target_pairs={{0,64},{8,72},{16,80},{24,88},{32,96},{40,104},{48,112},{56,120},{... | collective-permute-start | bytes 208904 | tf_op jit(solution)/shard_map/ppermute | solution.py:348
  13.6 0.9 %copy-start = (bf16[272,128]{1,0:T(8,128)(2,1)S(1)}, bf16[272,128]{1,0:T(8,128)(2,1)}, u32[]{:S(2)}) copy-start(bf16[272,128]{1,0:T(8,128)(2,1)} %shard_map.94.p0) | copy-start | bytes 208900
  13.6 0.9 %copy-start.1 = (s32[9]{0:T(128)S(1)}, s32[9]{0:T(128)}, u32[]{:S(2)}) copy-start(s32[9]{0:T(128)} %b_ref.3) | copy-start | bytes 112
  13.6 22.6 %copy-start.3 = (bf16[128,1024]{1,0:T(8,128)(2,1)S(1)}, bf16[128,1024]{1,0:T(8,128)(2,1)}, u32[]{:S(2)}) copy-start(bf16[128,1024]{1,0:T(8,128)(2,1)} %refs_2_.1) | copy-start | bytes 786436
  14.5 21.7 %copy-start.2 = (bf16[128,1024]{1,0:T(8,128)(2,1)S(1)}, bf16[128,1024]{1,0:T(8,128)(2,1)}, u32[]{:S(2)}) copy-start(bf16[128,1024]{1,0:T(8,128)(2,1)} %refs_1_.1) | copy-start | bytes 786436
  15.2 4.5 %collective-permute-start.3 = (f32[8,128]{1,0:T(8,128)S(1)}, f32[8,128]{1,0:T(8,128)S(1)}, u32[]{:S(2)}, u32[]{:S(2)}) collective-permute-start(f32[8,128]{1,0:T(8,128)S(1)} %shard_map.95), channel_id=1, source_target_pairs={{0,1},{1,0},{2,3},{3,2},{4,5},{5,4},{6,7},{7,6},{8,9},{9,8},{10,11... | collective-permute-start | bytes 12296 | tf_op jit(solution)/shard_map/ppermute | solution.py:356
  16.0 17.3 %collective-permute-start.7 = (bf16[4,256,128]{2,1,0:T(8,128)(2,1)S(1)}, bf16[4,256,128]{2,1,0:T(8,128)(2,1)S(1)}, u32[]{:S(2)}, u32[]{:S(2)}) collective-permute-start(bf16[4,256,128]{2,1,0:T(8,128)(2,1)S(1)} %pad_maximum_fusion.refs_3_), channel_id=1, source_target_pairs={{0,32},{8,40},{16,48},{24,56},{32,0},{40,8},{48,16},{56,24},{64,96... | collective-permute-start | bytes 786440 | tf_op jit(solution)/shard_map/ppermute | solution.py:348
  19.0 14.2 %collective-permute-start.6 = (bf16[4,256,128]{2,1,0:T(8,128)(2,1)S(1)}, bf16[4,256,128]{2,1,0:T(8,128)(2,1)S(1)}, u32[]{:S(2)}, u32[]{:S(2)}) collective-permute-start(bf16[4,256,128]{2,1,0:T(8,128)(2,1)S(1)} %pad_maximum_fusion.refs_3_), channel_id=1, source_target_pairs={{0,16},{8,24},{16,32},{24,40},{32,48},{40,56},{48,0},{56,8},{64,80... | collective-permute-start | bytes 786440 | tf_op jit(solution)/shard_map/ppermute | solution.py:348
  19.6 13.6 %collective-permute-start.8 = (bf16[4,256,128]{2,1,0:T(8,128)(2,1)S(1)}, bf16[4,256,128]{2,1,0:T(8,128)(2,1)S(1)}, u32[]{:S(2)}, u32[]{:S(2)}) collective-permute-start(bf16[4,256,128]{2,1,0:T(8,128)(2,1)S(1)} %pad_maximum_fusion.refs_3_), channel_id=1, source_target_pairs={{0,48},{8,56},{16,0},{24,8},{32,16},{40,24},{48,32},{56,40},{64,11... | collective-permute-start | bytes 786440 | tf_op jit(solution)/shard_map/ppermute | solution.py:348
  22.3 4.8 %collective-permute-start.4 = (f32[8,128]{1,0:T(8,128)S(1)}, f32[8,128]{1,0:T(8,128)S(1)}, u32[]{:S(2)}, u32[]{:S(2)}) collective-permute-start(f32[8,128]{1,0:T(8,128)S(1)} %add.18), channel_id=1, source_target_pairs={{0,3},{1,2},{2,1},{3,0},{4,7},{5,6},{6,5},{7,4},{8,11},{9,10},{10,... | collective-permute-start | bytes 12296 | tf_op jit(solution)/shard_map/ppermute | solution.py:359
  27.1 6.2 %collective-permute-start.5 = (f32[8,128]{1,0:T(8,128)S(1)}, f32[8,128]{1,0:T(8,128)S(1)}, u32[]{:S(2)}, u32[]{:S(2)}) collective-permute-start(f32[8,128]{1,0:T(8,128)S(1)} %add.19), channel_id=1, source_target_pairs={{0,132},{1,133},{2,134},{3,135},{4,128},{5,129},{6,130},{7,131},{8... | collective-permute-start | bytes 12296 | tf_op jit(solution)/shard_map/ppermute | solution.py:363
  33.3 2.8 %collective-permute-start.10 = (bf16[4,256,128]{2,1,0:T(8,128)(2,1)S(1)}, bf16[4,256,128]{2,1,0:T(8,128)(2,1)S(1)}, u32[]{:S(2)}, u32[]{:S(2)}) collective-permute-start(bf16[4,256,128]{2,1,0:T(8,128)(2,1)S(1)} %pad_maximum_fusion.refs_3_), channel_id=1, source_target_pairs={{0,8},{8,0},{16,24},{24,16},{32,40},{40,32},{48,56},{56,48},{64,72... | collective-permute-start | bytes 786440 | tf_op jit(solution)/shard_map/ppermute | solution.py:348
  33.4 2.7 %collective-permute-start.11 = (bf16[4,256,128]{2,1,0:T(8,128)(2,1)S(1)}, bf16[4,256,128]{2,1,0:T(8,128)(2,1)S(1)}, u32[]{:S(2)}, u32[]{:S(2)}) collective-permute-start(bf16[4,256,128]{2,1,0:T(8,128)(2,1)S(1)} %collective-permute-done.6.refs_4_), channel_id=1, source_target_pairs={{0,8},{8,0},{16,24},{24,16},{32,40},{40,32},{48,56},{56,48},{64,72... | collective-permute-start | bytes 786440 | tf_op jit(solution)/shard_map/ppermute | solution.py:348
  33.9 2.2 %collective-permute-start.12 = (bf16[4,256,128]{2,1,0:T(8,128)(2,1)S(1)}, bf16[4,256,128]{2,1,0:T(8,128)(2,1)S(1)}, u32[]{:S(2)}, u32[]{:S(2)}) collective-permute-start(bf16[4,256,128]{2,1,0:T(8,128)(2,1)S(1)} %collective-permute-done.7.refs_5_), channel_id=1, source_target_pairs={{0,8},{8,0},{16,24},{24,16},{32,40},{40,32},{48,56},{56,48},{64,72... | collective-permute-start | bytes 786440 | tf_op jit(solution)/shard_map/ppermute | solution.py:348
  34.0 2.1 %collective-permute-start.13 = (bf16[4,256,128]{2,1,0:T(8,128)(2,1)S(1)}, bf16[4,256,128]{2,1,0:T(8,128)(2,1)S(1)}, u32[]{:S(2)}, u32[]{:S(2)}) collective-permute-start(bf16[4,256,128]{2,1,0:T(8,128)(2,1)S(1)} %collective-permute-done.8.refs_6_), channel_id=1, source_target_pairs={{0,8},{8,0},{16,24},{24,16},{32,40},{40,32},{48,56},{56,48},{64,72... | collective-permute-start | bytes 786440 | tf_op jit(solution)/shard_map/ppermute | solution.py:348
  34.4 1.6 %collective-permute-start.9 = (f32[8,128]{1,0:T(8,128)S(1)}, f32[8,128]{1,0:T(8,128)S(1)}, u32[]{:S(2)}, u32[]{:S(2)}) collective-permute-start(f32[8,128]{1,0:T(8,128)S(1)} %add.20), channel_id=1, source_target_pairs={{0,8},{8,0},{16,24},{24,16},{32,40},{40,32},{48,56},{56,48},{64,72... | collective-permute-start | bytes 12296 | tf_op jit(solution)/shard_map/ppermute | solution.py:348
  36.1 3.7 %collective-permute-start.14 = (f32[8,128]{1,0:T(8,128)S(1)}, f32[8,128]{1,0:T(8,128)S(1)}, u32[]{:S(2)}, u32[]{:S(2)}) collective-permute-start(f32[8,128]{1,0:T(8,128)S(1)} %add.21), channel_id=1, source_target_pairs={{0,16},{8,24},{16,0},{24,8},{32,48},{40,56},{48,32},{56,40},{64,80... | collective-permute-start | bytes 12296 | tf_op jit(solution)/shard_map/ppermute | solution.py:348
  39.8 4.6 %copy-start.4 = (s32[8,2]{0,1:T(2,128)S(1)}, s32[8,2]{0,1:T(2,128)}, u32[]{:S(2)}) copy-start(s32[8,2]{0,1:T(2,128)} %param.14) | copy-start | bytes 196
  39.8 6.2 %collective-permute-start.16 = (bf16[4,4,2,128,128]{4,3,2,1,0:T(8,128)(2,1)}, bf16[4,4,2,128,128]{4,3,2,1,0:T(8,128)(2,1)S(1)}, u32[]{:S(2)}, u32[]{:S(2)}) collective-permute-start(bf16[4,4,2,128,128]{4,3,2,1,0:T(8,128)(2,1)} %get-tuple-element.69), channel_id=1, source_target_pairs={{0,8},{8,0},{16,24},{24,16},{32,40},{40,32},{48,56},{56,48},{64,72... | collective-permute-start | bytes 3145736 | tf_op jit(solution)/shard_map/ppermute | solution.py:348
  39.8 6.2 %collective-permute-start.15 = (f32[8,128]{1,0:T(8,128)S(1)}, f32[8,128]{1,0:T(8,128)S(1)}, u32[]{:S(2)}, u32[]{:S(2)}) collective-permute-start(f32[8,128]{1,0:T(8,128)S(1)} %add.22), channel_id=1, source_target_pairs={{0,48},{8,56},{16,32},{24,40},{32,16},{40,24},{48,0},{56,8},{64,11... | collective-permute-start | bytes 12296 | tf_op jit(solution)/shard_map/ppermute | solution.py:348
  47.2 13.9 %collective-permute-start.17 = (bf16[4,2,128,128]{3,2,1,0:T(8,128)(2,1)S(1)}, bf16[4,2,128,128]{3,2,1,0:T(8,128)(2,1)S(1)}, u32[]{:S(2)}, u32[]{:S(2)}) collective-permute-start(bf16[4,2,128,128]{3,2,1,0:T(8,128)(2,1)S(1)} %get-tuple-element.72), channel_id=1, source_target_pairs={{0,48},{8,56},{16,0},{24,8},{32,16},{40,24},{48,32},{56,40},{64,11... | collective-permute-start | bytes 786440 | tf_op jit(solution)/shard_map/ppermute | solution.py:348
  50.5 10.8 %collective-permute-start.18 = (bf16[4,2,128,128]{3,2,1,0:T(8,128)(2,1)S(1)}, bf16[4,2,128,128]{3,2,1,0:T(8,128)(2,1)S(1)}, u32[]{:S(2)}, u32[]{:S(2)}) collective-permute-start(bf16[4,2,128,128]{3,2,1,0:T(8,128)(2,1)S(1)} %get-tuple-element.73), channel_id=1, source_target_pairs={{0,32},{8,40},{16,48},{24,56},{32,0},{40,8},{48,16},{56,24},{64,96... | collective-permute-start | bytes 786440 | tf_op jit(solution)/shard_map/ppermute | solution.py:348
  50.5 14.0 %collective-permute-start.19 = (bf16[4,2,128,128]{3,2,1,0:T(8,128)(2,1)S(1)}, bf16[4,2,128,128]{3,2,1,0:T(8,128)(2,1)S(1)}, u32[]{:S(2)}, u32[]{:S(2)}) collective-permute-start(bf16[4,2,128,128]{3,2,1,0:T(8,128)(2,1)S(1)} %get-tuple-element.74), channel_id=1, source_target_pairs={{0,16},{8,24},{16,32},{24,40},{32,48},{40,56},{48,0},{56,8},{64,80... | collective-permute-start | bytes 786440 | tf_op jit(solution)/shard_map/ppermute | solution.py:348
  64.7 8.6 %collective-permute-start.20 = (bf16[2,128,128]{2,1,0:T(8,128)(2,1)S(1)}, bf16[2,128,128]{2,1,0:T(8,128)(2,1)S(1)}, u32[]{:S(2)}, u32[]{:S(2)}) collective-permute-start(bf16[2,128,128]{2,1,0:T(8,128)(2,1)S(1)} %get-tuple-element.76), channel_id=1, source_target_pairs={{0,192},{8,200},{16,208},{24,216},{32,224},{40,232},{48,240},{56,2... | collective-permute-start | bytes 196616 | tf_op jit(solution)/shard_map/ppermute | solution.py:348
  70.8 5.4 %collective-permute-start.21 = (bf16[2,128,128]{2,1,0:T(8,128)(2,1)S(1)}, bf16[2,128,128]{2,1,0:T(8,128)(2,1)S(1)}, u32[]{:S(2)}, u32[]{:S(2)}) collective-permute-start(bf16[2,128,128]{2,1,0:T(8,128)(2,1)S(1)} %get-tuple-element.77), channel_id=1, source_target_pairs={{0,128},{8,136},{16,144},{24,152},{32,160},{40,168},{48,176},{56,1... | collective-permute-start | bytes 196616 | tf_op jit(solution)/shard_map/ppermute | solution.py:348
  70.8 6.1 %collective-permute-start.22 = (bf16[2,128,128]{2,1,0:T(8,128)(2,1)S(1)}, bf16[2,128,128]{2,1,0:T(8,128)(2,1)S(1)}, u32[]{:S(2)}, u32[]{:S(2)}) collective-permute-start(bf16[2,128,128]{2,1,0:T(8,128)(2,1)S(1)} %get-tuple-element.78), channel_id=1, source_target_pairs={{0,64},{8,72},{16,80},{24,88},{32,96},{40,104},{48,112},{56,120},{... | collective-permute-start | bytes 196616 | tf_op jit(solution)/shard_map/ppermute | solution.py:348

commit v4 on v3

--- a/solution.py
+++ b/solution.py
@@ -232,38 +232,78 @@
     )(keys, values, ratios)
 
 
-def block_sums(bounds, packets):
-    def kern(b_ref, p0, p1, p2, p3, sums_ref, rides, sem):
+def block_sums(bounds, ratios, packets):
+    def kern(b_ref, ratio_ref, p1, p2, p3, sums_ref, rides, sem):
         copies = [
             pltpu.make_async_copy(p.at[pl.ds(2 * BLOCK, 16)], rides.at[k], sem.at[k])
-            for k, p in enumerate((p0, p1, p2, p3))
+            for k, p in enumerate((p1, p2, p3))
         ]
         for copy in copies:
             copy.start()
         me = lax.axis_index("seq")
         row = lax.broadcasted_iota(jnp.int32, (RESP, DH), 0)
+        own = ratio_ref[0]
+        for t in range(1, ratios.shape[0]):
+            own = own + ratio_ref[t]
+        part = jnp.full((1, DH), own, f32)
         sums = jnp.zeros((RESP, DH), f32)
         for s in range(4):
             first = (lax.rem(me // 8 - s + 4, 4) * 8 + lax.rem(me, 8)) * BLOCK
             resp = jnp.int32(-1)
             for r in range(RESP):
                 resp = resp + (first >= b_ref[r]).astype(jnp.int32)
-            copies[s].wait()
-            part = jnp.sum(rides[s].astype(f32), axis=0, keepdims=True)
+            if s:
+                copies[s - 1].wait()
+                part = jnp.sum(rides[s - 1].astype(f32), axis=0, keepdims=True)
             sums = sums + jnp.where(row == resp, part, 0.0)
         sums_ref[...] = sums
 
     return pl.pallas_call(
         kern,
         out_shape=jax.ShapeDtypeStruct((RESP, DH), f32),
-        in_specs=[S, A, A, A, A],
+        in_specs=[S, S, A, A, A],
         out_specs=V,
-        scratch_shapes=[pltpu.VMEM((4, 16, DH), bf), pltpu.SemaphoreType.DMA((4,))],
+        scratch_shapes=[pltpu.VMEM((3, 16, DH), bf), pltpu.SemaphoreType.DMA((3,))],
         compiler_params=SMALL,
-    )(bounds, *packets)
-
-
-def core_add(sums, bounds, pairs, keep, got):
+    )(bounds, ratios, *packets)
+
+
+def live_planes(b_ref, z):
+    prompt = b_ref[0] // BLOCK
+    start = jnp.int32(0)
+    for r in range(RESP):
+        lo = b_ref[r] // BLOCK
+        start = jnp.where(z * 8 >= lo, lo, start)
+
+    def live(plane, column):
+        j = plane * 8 + column
+        return (plane < z) & ((j < prompt) | ((z * 8 >= prompt) & (j >= start)))
+
+    return live
+
+
+def slots_needed(bounds):
+    def kern(b_ref, out_ref):
+        most = jnp.int32(0)
+        for z in range(1, 4):
+            live = live_planes(b_ref, jnp.int32(z))
+            for column in range(8):
+                count = jnp.int32(0)
+                for plane in range(z):
+                    count = count + live(jnp.int32(plane), column).astype(jnp.int32)
+                most = jnp.maximum(most, count)
+        out_ref[0] = most + 1
+
+    return pl.pallas_call(
+        kern,
+        out_shape=jax.ShapeDtypeStruct((1,), jnp.int32),
+        in_specs=[S],
+        out_specs=S,
+        compiler_params=SMALL,
+    )(bounds)
+
+
+def core_add(slots, sums, bounds, pairs, keep, got):
     def kern(sums_ref, b_ref, p_ref, keep_ref, got_ref, o0, o1, o2, o3, w_ref, mean, coef):
         me = lax.axis_index("seq")
         for r in range(RESP):
@@ -287,15 +327,30 @@
         mine = weight(me)
         theirs = weight(me + 1 - 2 * lax.rem(me, 2))
         w_ref[...] = jnp.full(w_ref.shape, mine, f32)
+        z = me // 8
+        live = live_planes(b_ref, z)
         for sx, out in enumerate((o0, o1, o2, o3)):
-            for sz in range(4):
+            column = lax.rem(me // 2 - sx + 4, 4) * 2 + lax.rem(me, 2)
+
+            def fill(slot, sz, sx=sx, out=out):
                 for kvi in range(2):
-                    out[sz, kvi] = (
+                    out[slot, kvi] = (
                         keep_ref[sx, sz, kvi].astype(f32) * mine
                         + got_ref[sx, sz, kvi].astype(f32) * theirs
                     ).astype(bf)
 
-    slot = jax.ShapeDtypeStruct((4, 2, 128, 128), bf)
+            fill(0, 0)
+            slot = jnp.int32(1)
+            for plane in range(3):
+                used = live(jnp.int32(plane), column)
+
+                @pl.when(used)
+                def _(slot=slot, plane=plane, fill=fill):
+                    fill(slot, z - plane)
+
+                slot = slot + used.astype(jnp.int32)
+
+    slot = jax.ShapeDtypeStruct((slots, 2, 128, 128), bf)
     return pl.pallas_call(
         kern,
         out_shape=(slot, slot, slot, slot, jax.ShapeDtypeStruct((8, 128), f32)),
@@ -306,23 +361,45 @@
     )(sums, bounds, pairs, keep, got)
 
 
-def x_add(a0, a1, a2, a3):
-    def kern(i0, i1, i2, i3, *outs):
-        for sz in range(4):
-            for kvi in range(2):
-                outs[sz][kvi] = (
-                    (i0[sz, kvi].astype(f32) + i1[sz, kvi].astype(f32))
-                    + (i2[sz, kvi].astype(f32) + i3[sz, kvi].astype(f32))
-                ).astype(bf)
+def x_add(bounds, parts):
+    def kern(b_ref, i0, i1, i2, i3, *outs):
+        me = lax.axis_index("seq")
+        z = me // 8
+        live = live_planes(b_ref, z)
+        used = [live(jnp.int32(plane), lax.rem(me, 8)).astype(jnp.int32) for plane in range(3)]
+
+        def total(slot, kvi):
+            return (
+                (i0[slot, kvi].astype(f32) + i1[slot, kvi].astype(f32))
+                + (i2[slot, kvi].astype(f32) + i3[slot, kvi].astype(f32))
+            ).astype(bf)
+
+        for kvi in range(2):
+            outs[0][kvi] = total(0, kvi)
+        for sz in range(1, 4):
+            plane = z - sz
+            slot = 1 + jnp.where(plane > 0, used[0], 0) + jnp.where(plane > 1, used[1], 0)
+            here = jnp.int32(0)
+            for p in range(3):
+                here = jnp.where(plane == p, used[p], here)
+
+            @pl.when(here == 1)
+            def _(sz=sz, slot=slot):
+                for kvi in range(2):
+                    outs[sz][kvi] = total(slot, kvi)
+
+            @pl.when(here == 0)
+            def _(sz=sz):
+                outs[sz][...] = jnp.zeros_like(outs[sz])
 
     slot = jax.ShapeDtypeStruct((2, 128, 128), bf)
     return pl.pallas_call(
         kern,
         out_shape=(slot,) * 4,
-        in_specs=[V] * 4,
+        in_specs=[S] + [V] * 4,
         out_specs=(V,) * 4,
         compiler_params=SMALL,
-    )(a0, a1, a2, a3)
+    )(bounds, *parts)
 
 
 def z_add(a0, a1, a2, a3):
@@ -348,11 +425,12 @@
         return lax.ppermute(v, "seq", perm)
 
     packet = pack(key_rows, value_rows, log_ratio)
+    slots = slots_needed(bounds)[0]
     by_z = [packet] + [seq(packet, Z_UP[s]) for s in (1, 2, 3)]
     column = jnp.stack([p[: 2 * BLOCK] for p in by_z])
     column, by_z = lax.optimization_barrier((column, by_z))
     far = seq(column, X_UP[2])
-    sums, column = lax.optimization_barrier((block_sums(bounds, by_z), column))
+    sums, column = lax.optimization_barrier((block_sums(bounds, log_ratio, by_z[1:]), column))
     turned = lax.ppermute(sums, "heads", HEAD_Y[0])
     before = seq(column, X_UP[1])
     sums, column = lax.optimization_barrier((sums + turned, column))
@@ -370,8 +448,18 @@
     sums, send = lax.optimization_barrier((sums + turned, send))
     got = seq(send, CORE)
     sums = sums + seq(sums, X_FLIP[1])
-    *by_shift, weight = core_add(sums, bounds, pairs, keep, got)
-    summed = x_add(by_shift[0], *[seq(by_shift[s], X_DOWN[s]) for s in (1, 2, 3)])
+
+    def across_x(slots):
+        def branch(sums, keep, got):
+            *by_shift, weight = core_add(slots, sums, bounds, pairs, keep, got)
+            moved = [seq(by_shift[s], X_DOWN[s]) for s in (1, 2, 3)]
+            return x_add(bounds, [by_shift[0]] + moved), weight
+
+        return branch
+
+    summed, weight = lax.switch(
+        slots - 2, [across_x(2), across_x(3), across_x(4)], sums, keep, got
+    )
     query_grad = (dq * weight[0, 0]).astype(bf)
     key_grad, value_grad = z_add(summed[0], *[seq(summed[s], Z_DOWN[s]) for s in (1, 2, 3)])
     return query_grad, key_grad, value_grad

time: 77.3 us -> 72.4 us (0.937)
  waiting for transfers between devices: 31.1 us -> 24.9 us
  starting transfers between devices: 34.9 us -> 33.6 us
  Pallas kernels: 6.93 us -> 7.72 us
    ppermute x20, waiting for transfers between devices: 25.8 us -> 19.6 us  [seq(): return lax.ppermute(v, 'seq', perm)]
    pallas_call x1 -> x2, Pallas kernels: 0.13 us -> 1.89 us  [the longest x1 1.23 us: slots_needed(): pl.pallas_call(kern, out_shape=jax.ShapeDtypeStruct((1,), jnp.int32), in_...]
    ppermute x20, starting transfers between devices: 28.5 us -> 27.2 us  [seq(): return lax.ppermute(v, 'seq', perm)]
    pallas_call x1, Pallas kernels: 2.8 us -> 2 us  [attend(): pl.pallas_call(kern, out_shape=(jax.ShapeDtypeStruct((BLOCK, ROWS), f32),...]
  transfers between devices with their start and end apart: 23 -> 23, of which waited for: 13 -> 11; matrix products, arithmetic and copies ran while one was open for 4% -> 4% of each run, Pallas kernels for 4% -> 4%
where the time goes in v4:
time: 72.4 us; the launch traced here: 72 us
  starting transfers between devices  33.6 us (46%)
  waiting for transfers between devices  24.9 us (34%)
  Pallas kernels  7.72 us (11%)
  local copies, waits for them, and re-layouts  2.77 us (4%)
  between operations  1.47 us (2%)
  other arithmetic  1.45 us (2%)
    ppermute x20, starting transfers between devices, seq(): return lax.ppermute(v, 'seq', perm)  27.2 us
    ppermute x20, waiting for transfers between devices, seq(): return lax.ppermute(v, 'seq', perm)  19.6 us
    ppermute x1, starting transfers between devices, shards(): sums = sums + lax.ppermute(sums, ('seq', 'heads'), HALVES)  4.58 us
    ppermute x1, waiting for transfers between devices, shards(): turned = lax.ppermute(sums, 'heads', HEAD_Y[1])  3.76 us
    pallas_call x1, Pallas kernels, attend(): pl.pallas_call(kern, out_shape=(jax.ShapeDtypeStruct((BLOCK, ROWS), f32),...  2 us
    ppermute x1, waiting for transfers between devices, shards(): sums = sums + lax.ppermute(sums, ('seq', 'heads'), HALVES)  1.58 us
    pallas_call x1, Pallas kernels, pack(): pl.pallas_call(kern, out_shape=jax.ShapeDtypeStruct((2 * BLOCK + 16, DH),...  1.46 us
  transfers between devices with their start and end apart: 23, of which 11 were waited for; matrix products, arithmetic and copies ran while one was open for 4% of the time, Pallas kernels for 4%

profile of v4, /device:TPU:24, one launch (start us, length us, event | category | flops | bytes accessed | tf_op | source)
XLA Modules:
  0.0 72.0 jit_solution(18299510428015260949)
XLA Ops:
  0.6 1.5 %shard_map.94 = bf16[272,128]{1,0:T(8,128)(2,1)} custom-call(bf16[128,128]{1,0:T(8,128)(2,1)} %k_ref.1, bf16[128,128]{1,0:T(8,128)(2,1)} %v_ref.1, f32[16]{0:T(128)} %ratio_ref.3), custom_call_target="tpu_custom_call" | custom-call | tf_op jit(solution)/shard_map/pallas_call | solution.py:227
  2.1 4.6 %collective-permute-start.11 = (bf16[272,128]{1,0:T(8,128)(2,1)}, bf16[272,128]{1,0:T(8,128)(2,1)S(1)}, u32[]{:S(2)}, u32[]{:S(2)}) collective-permute-start(bf16[272,128]{1,0:T(8,128)(2,1)} %shard_map.94), channel_id=1, source_target_pairs={{0,192},{8,200},{16,208},{24,216},{32,224},{40,232},{48,240},{56,2... | collective-permute-start | bytes 208904 | tf_op jit(solution)/shard_map/ppermute | solution.py:425
  6.7 0.7 collective-permute-start.9
  7.4 0.9 %slice_bitcast_fusion.3 = bf16[1,256,128]{2,1,0:T(8,128)(2,1)S(1)} fusion(bf16[272,128]{1,0:T(8,128)(2,1)} %shard_map.94), kind=kLoop, calls=%fused_computation.5 | loop fusion | bytes 131072 | tf_op jit(solution)/shard_map/stack | solution.py:430
  8.3 1.4 %collective-permute-done.11.p3 = bf16[272,128]{1,0:T(8,128)(2,1)S(1)} collective-permute-done((bf16[272,128]{1,0:T(8,128)(2,1)}, bf16[272,128]{1,0:T(8,128)(2,1)S(1)}, u32[]{:S(2)}, u32[]{:S(2)}) %collective-permute-start.11) | collective-permute-done | bytes 69664 | tf_op jit(solution)/shard_map/ppermute | solution.py:425
  9.6 4.0 %collective-permute-done.10.p2 = bf16[272,128]{1,0:T(8,128)(2,1)S(1)} collective-permute-done((bf16[272,128]{1,0:T(8,128)(2,1)}, bf16[272,128]{1,0:T(8,128)(2,1)S(1)}, u32[]{:S(2)}, u32[]{:S(2)}) %collective-permute-start.10) | collective-permute-done | bytes 69664 | tf_op jit(solution)/shard_map/ppermute | solution.py:425
  13.6 0.0 copy-start
  13.6 0.0 copy-start.2
  13.7 0.6 copy-done
  14.3 0.0 copy-done.3
  14.3 0.7 shard_map.95
  15.0 0.8 %collective-permute-start.12 = (f32[8,128]{1,0:T(8,128)S(1)}, f32[8,128]{1,0:T(8,128)S(1)}, u32[]{:S(2)}, u32[]{:S(2)}) collective-permute-start(f32[8,128]{1,0:T(8,128)S(1)} %shard_map.95), channel_id=1, source_target_pairs={{0,1},{1,0},{2,3},{3,2},{4,5},{5,4},{6,7},{7,6},{8,9},{9,8},{10,11... | collective-permute-start | bytes 12296 | tf_op jit(solution)/shard_map/ppermute | solution.py:434
  15.8 3.0 %collective-permute-start.16 = (bf16[4,256,128]{2,1,0:T(8,128)(2,1)S(1)}, bf16[4,256,128]{2,1,0:T(8,128)(2,1)S(1)}, u32[]{:S(2)}, u32[]{:S(2)}) collective-permute-start(bf16[4,256,128]{2,1,0:T(8,128)(2,1)S(1)} %pad_maximum_fusion.refs_3_), channel_id=1, source_target_pairs={{0,32},{8,40},{16,48},{24,56},{32,0},{40,8},{48,16},{56,24},{64,96... | collective-permute-start | bytes 786440 | tf_op jit(solution)/shard_map/ppermute | solution.py:425
  18.8 0.6 collective-permute-start.15
  19.4 2.6 %collective-permute-start.17 = (bf16[4,256,128]{2,1,0:T(8,128)(2,1)S(1)}, bf16[4,256,128]{2,1,0:T(8,128)(2,1)S(1)}, u32[]{:S(2)}, u32[]{:S(2)}) collective-permute-start(bf16[4,256,128]{2,1,0:T(8,128)(2,1)S(1)} %pad_maximum_fusion.refs_3_), channel_id=1, source_target_pairs={{0,48},{8,56},{16,0},{24,8},{32,16},{40,24},{48,32},{56,40},{64,11... | collective-permute-start | bytes 786440 | tf_op jit(solution)/shard_map/ppermute | solution.py:425
  22.1 1.1 %collective-permute-start.13 = (f32[8,128]{1,0:T(8,128)S(1)}, f32[8,128]{1,0:T(8,128)S(1)}, u32[]{:S(2)}, u32[]{:S(2)}) collective-permute-start(f32[8,128]{1,0:T(8,128)S(1)} %add.20), channel_id=1, source_target_pairs={{0,3},{1,2},{2,1},{3,0},{4,7},{5,6},{6,5},{7,4},{8,11},{9,10},{10,... | collective-permute-start | bytes 12296 | tf_op jit(solution)/shard_map/ppermute | solution.py:437
  23.1 3.8 %collective-permute-done.13 = f32[8,128]{1,0:T(8,128)S(1)} collective-permute-done((f32[8,128]{1,0:T(8,128)S(1)}, f32[8,128]{1,0:T(8,128)S(1)}, u32[]{:S(2)}, u32[]{:S(2)}) %collective-permute-start.13) | collective-permute-done | bytes 4128 | tf_op jit(solution)/shard_map/ppermute | solution.py:437
  26.9 4.6 %collective-permute-start.14 = (f32[8,128]{1,0:T(8,128)S(1)}, f32[8,128]{1,0:T(8,128)S(1)}, u32[]{:S(2)}, u32[]{:S(2)}) collective-permute-start(f32[8,128]{1,0:T(8,128)S(1)} %add.21), channel_id=1, source_target_pairs={{0,132},{1,133},{2,134},{3,135},{4,128},{5,129},{6,130},{7,131},{8... | collective-permute-start | bytes 12296 | tf_op jit(solution)/shard_map/ppermute | solution.py:441
  31.5 1.6 %collective-permute-done.14 = f32[8,128]{1,0:T(8,128)S(1)} collective-permute-done((f32[8,128]{1,0:T(8,128)S(1)}, f32[8,128]{1,0:T(8,128)S(1)}, u32[]{:S(2)}, u32[]{:S(2)}) %collective-permute-start.14) | collective-permute-done | bytes 4128 | tf_op jit(solution)/shard_map/ppermute | solution.py:441
  33.1 0.1 collective-permute-start.19
  33.2 0.5 collective-permute-start.20
  33.7 0.1 collective-permute-start.21
  33.8 0.4 collective-permute-start.22
  34.2 0.1 collective-permute-start.18
  34.3 1.5 %collective-permute-done.18 = f32[8,128]{1,0:T(8,128)S(1)} collective-permute-done((f32[8,128]{1,0:T(8,128)S(1)}, f32[8,128]{1,0:T(8,128)S(1)}, u32[]{:S(2)}, u32[]{:S(2)}) %collective-permute-start.18) | collective-permute-done | bytes 4128 | tf_op jit(solution)/shard_map/ppermute | solution.py:425
  35.9 0.1 collective-permute-start.23
  36.0 2.0 %shard_map.96 = (f32[128,1024]{1,0:T(8,128)S(1)}, bf16[4,4,2,128,128]{4,3,2,1,0:T(8,128)(2,1)S(1)}, bf16[4,4,2,128,128]{4,3,2,1,0:T(8,128)(2,1)S(1)}) custom-call(s32[9]{0:T(128)S(1)} %copy-done.3, bf16[128,1024]{1,0:T(8,128)(2,1)S(1)} %copy-done.1, bf16[128,1024]{1,0:T(8,128)(2,1)S(1)} %copy-done.2, bf16[4,256,128]{2,1,0:T(8,128)(2,1)S(1)} %pad_maximum_fusion.refs_3_, ...), custom_call_target="tpu_custom_call" | custom-call | flops 10000000000 | bytes 5242880 | tf_op jit(solution)/shard_map/pallas_call | solution.py:156
  38.0 1.6 %collective-permute-done.23 = f32[8,128]{1,0:T(8,128)S(1)} collective-permute-done((f32[8,128]{1,0:T(8,128)S(1)}, f32[8,128]{1,0:T(8,128)S(1)}, u32[]{:S(2)}, u32[]{:S(2)}) %collective-permute-start.23) | collective-permute-done | bytes 4128 | tf_op jit(solution)/shard_map/ppermute | solution.py:425
  39.6 3.8 %collective-permute-start.24 = (f32[8,128]{1,0:T(8,128)S(1)}, f32[8,128]{1,0:T(8,128)S(1)}, u32[]{:S(2)}, u32[]{:S(2)}) collective-permute-start(f32[8,128]{1,0:T(8,128)S(1)} %add.24), channel_id=1, source_target_pairs={{0,48},{8,56},{16,32},{24,40},{32,16},{40,24},{48,0},{56,8},{64,11... | collective-permute-start | bytes 12296 | tf_op jit(solution)/shard_map/ppermute | solution.py:425
  43.4 1.2 %shard_map.97 = s32[1]{0:T(128)} custom-call(s32[9]{0:T(128)S(1)} %copy-done.3), custom_call_target="tpu_custom_call" | custom-call | tf_op jit(solution)/shard_map/pallas_call | solution.py:297
  45.3 0.0 copy-start.4
  45.3 0.7 copy-done.4
  46.0 13.5 %conditional.1 = (bf16[2,128,128]{2,1,0:T(8,128)(2,1)S(1)}, bf16[2,128,128]{2,1,0:T(8,128)(2,1)S(1)}, bf16[2,128,128]{2,1,0:T(8,128)(2,1)S(1)}, bf16[2,128,128]{2,1,0:T(8,128)(2,1)S(1)}, f32[8,128]{1,0:T(8,128)S(1)}) conditional(s32[]{:T(128)} %bitcast.4, (f32[8,128]{1,0:T(8,128)S(1)}, s32[9]{0:T(128)S(1)}, s32[8,2]{0,1:T(2,128)S(1)}, ...), branch_computations={%region_0.0_spmd, %region_1.0_spmd, %region_2.0_spmd} | conditional | bytes 3146016 | solution.py:460
  46.0 0.1 copy.10.p_ref
  46.0 1.0 %branch_0_fun.2 = (bf16[2,2,128,128]{3,2,1,0:T(8,128)(2,1)S(1)}, bf16[2,2,128,128]{3,2,1,0:T(8,128)(2,1)S(1)}, bf16[2,2,128,128]{3,2,1,0:T(8,128)(2,1)S(1)}, bf1...) custom-call(f32[8,128]{1,0:T(8,128)S(1)} %get-tuple-element.31.sums_ref, s32[9]{0:T(128)S(1)} %get-tuple-element.30.b_ref, ...), custom_call_target="tpu_custom_call" | custom-call | tf_op jit(solution)/shard_map/cond/branch_0_fun/pallas_call | solution.py:354
  47.1 3.0 %collective-permute-start = (bf16[2,2,128,128]{3,2,1,0:T(8,128)(2,1)S(1)}, bf16[2,2,128,128]{3,2,1,0:T(8,128)(2,1)S(1)}, u32[]{:S(2)}, u32[]{:S(2)}) collective-permute-start(bf16[2,2,128,128]{3,2,1,0:T(8,128)(2,1)S(1)} %get-tuple-element.36), channel_id=1, source_target_pairs={{0,48},{8,56},{16,0},{24,8},{32,16},{40,24},{48,32},{56,40},{64,11... | collective-permute-start | bytes 393224 | tf_op jit(solution)/shard_map/cond/branch_0_fun/ppermute | solution.py:425
  50.1 1.1 %collective-permute-start.2 = (bf16[2,2,128,128]{3,2,1,0:T(8,128)(2,1)S(1)}, bf16[2,2,128,128]{3,2,1,0:T(8,128)(2,1)S(1)}, u32[]{:S(2)}, u32[]{:S(2)}) collective-permute-start(bf16[2,2,128,128]{3,2,1,0:T(8,128)(2,1)S(1)} %get-tuple-element.38), channel_id=1, source_target_pairs={{0,16},{8,24},{16,32},{24,40},{32,48},{40,56},{48,0},{56,8},{64,80... | collective-permute-start | bytes 393224 | tf_op jit(solution)/shard_map/cond/branch_0_fun/ppermute | solution.py:425
  51.1 4.1 %collective-permute-done.i1 = bf16[2,2,128,128]{3,2,1,0:T(8,128)(2,1)S(1)} collective-permute-done((bf16[2,2,128,128]{3,2,1,0:T(8,128)(2,1)S(1)}, bf16[2,2,128,128]{3,2,1,0:T(8,128)(2,1)S(1)}, u32[]{:S(2)}, u32[]{:S(2)}) %collective-permute-start) | collective-permute-done | bytes 131104 | tf_op jit(solution)/shard_map/cond/branch_0_fun/ppermute | solution.py:425
  55.3 2.2 %collective-permute-done.1.i2 = bf16[2,2,128,128]{3,2,1,0:T(8,128)(2,1)S(1)} collective-permute-done((bf16[2,2,128,128]{3,2,1,0:T(8,128)(2,1)S(1)}, bf16[2,2,128,128]{3,2,1,0:T(8,128)(2,1)S(1)}, u32[]{:S(2)}, u32[]{:S(2)}) %collective-permute-start.1) | collective-permute-done | bytes 131104 | tf_op jit(solution)/shard_map/cond/branch_0_fun/ppermute | solution.py:425
  57.5 1.3 %collective-permute-done.2.i3 = bf16[2,2,128,128]{3,2,1,0:T(8,128)(2,1)S(1)} collective-permute-done((bf16[2,2,128,128]{3,2,1,0:T(8,128)(2,1)S(1)}, bf16[2,2,128,128]{3,2,1,0:T(8,128)(2,1)S(1)}, u32[]{:S(2)}, u32[]{:S(2)}) %collective-permute-start.2) | collective-permute-done | bytes 131104 | tf_op jit(solution)/shard_map/cond/branch_0_fun/ppermute | solution.py:425
  58.8 0.7 branch_0_fun.3
  59.5 5.8 %collective-permute-start.26 = (bf16[2,128,128]{2,1,0:T(8,128)(2,1)S(1)}, bf16[2,128,128]{2,1,0:T(8,128)(2,1)S(1)}, u32[]{:S(2)}, u32[]{:S(2)}) collective-permute-start(bf16[2,128,128]{2,1,0:T(8,128)(2,1)S(1)} %get-tuple-element.138), channel_id=1, source_target_pairs={{0,192},{8,200},{16,208},{24,216},{32,224},{40,232},{48,240},{56,2... | collective-permute-start | bytes 196616 | tf_op jit(solution)/shard_map/ppermute | solution.py:425
  65.3 0.7 collective-permute-start.28
  66.0 0.5 slice.19
  66.5 1.4 %multiply_convert_fusion = bf16[128,1024]{1,0:T(8,128)(2,1)} fusion(f32[128,1024]{1,0:T(8,128)S(1)} %get-tuple-element.130, f32[]{:T(128)} %bitcast.5), kind=kLoop, calls=%fused_computation | loop fusion | flops 262144 | bytes 786436 | tf_op jit(solution)/shard_map/convert_element_type | solution.py:463
  67.9 2.7 %collective-permute-done.27.i2 = bf16[2,128,128]{2,1,0:T(8,128)(2,1)S(1)} collective-permute-done((bf16[2,128,128]{2,1,0:T(8,128)(2,1)S(1)}, bf16[2,128,128]{2,1,0:T(8,128)(2,1)S(1)}, u32[]{:S(2)}, u32[]{:S(2)}) %collective-permute-start.27) | collective-permute-done | bytes 65568 | tf_op jit(solution)/shard_map/ppermute | solution.py:425
  70.5 0.8 %collective-permute-done.28.i3 = bf16[2,128,128]{2,1,0:T(8,128)(2,1)S(1)} collective-permute-done((bf16[2,128,128]{2,1,0:T(8,128)(2,1)S(1)}, bf16[2,128,128]{2,1,0:T(8,128)(2,1)S(1)}, u32[]{:S(2)}, u32[]{:S(2)}) %collective-permute-start.28) | collective-permute-done | bytes 65568 | tf_op jit(solution)/shard_map/ppermute | solution.py:425
  71.4 0.7 shard_map.98
  (30 shorter events, 0.1 us)
Async XLA Ops:
  2.1 7.5 %collective-permute-start.11 = (bf16[272,128]{1,0:T(8,128)(2,1)}, bf16[272,128]{1,0:T(8,128)(2,1)S(1)}, u32[]{:S(2)}, u32[]{:S(2)}) collective-permute-start(bf16[272,128]{1,0:T(8,128)(2,1)} %shard_map.94), channel_id=1, source_target_pairs={{0,192},{8,200},{16,208},{24,216},{32,224},{40,232},{48,240},{56,2... | collective-permute-start | bytes 208904 | tf_op jit(solution)/shard_map/ppermute | solution.py:425
  6.7 6.9 %collective-permute-start.10 = (bf16[272,128]{1,0:T(8,128)(2,1)}, bf16[272,128]{1,0:T(8,128)(2,1)S(1)}, u32[]{:S(2)}, u32[]{:S(2)}) collective-permute-start(bf16[272,128]{1,0:T(8,128)(2,1)} %shard_map.94), channel_id=1, source_target_pairs={{0,128},{8,136},{16,144},{24,152},{32,160},{40,168},{48,176},{56,1... | collective-permute-start | bytes 208904 | tf_op jit(solution)/shard_map/ppermute | solution.py:425
  6.7 6.9 %collective-permute-start.9 = (bf16[272,128]{1,0:T(8,128)(2,1)}, bf16[272,128]{1,0:T(8,128)(2,1)S(1)}, u32[]{:S(2)}, u32[]{:S(2)}) collective-permute-start(bf16[272,128]{1,0:T(8,128)(2,1)} %shard_map.94), channel_id=1, source_target_pairs={{0,64},{8,72},{16,80},{24,88},{32,96},{40,104},{48,112},{56,120},{... | collective-permute-start | bytes 208904 | tf_op jit(solution)/shard_map/ppermute | solution.py:425
  13.6 0.7 copy-start
  13.6 0.7 copy-start.3
  13.6 22.3 %copy-start.2 = (bf16[128,1024]{1,0:T(8,128)(2,1)S(1)}, bf16[128,1024]{1,0:T(8,128)(2,1)}, u32[]{:S(2)}) copy-start(bf16[128,1024]{1,0:T(8,128)(2,1)} %refs_2_.1) | copy-start | bytes 786436
  14.3 21.7 %copy-start.1 = (bf16[128,1024]{1,0:T(8,128)(2,1)S(1)}, bf16[128,1024]{1,0:T(8,128)(2,1)}, u32[]{:S(2)}) copy-start(bf16[128,1024]{1,0:T(8,128)(2,1)} %refs_1_.1) | copy-start | bytes 786436
  15.0 4.5 %collective-permute-start.12 = (f32[8,128]{1,0:T(8,128)S(1)}, f32[8,128]{1,0:T(8,128)S(1)}, u32[]{:S(2)}, u32[]{:S(2)}) collective-permute-start(f32[8,128]{1,0:T(8,128)S(1)} %shard_map.95), channel_id=1, source_target_pairs={{0,1},{1,0},{2,3},{3,2},{4,5},{5,4},{6,7},{7,6},{8,9},{9,8},{10,11... | collective-permute-start | bytes 12296 | tf_op jit(solution)/shard_map/ppermute | solution.py:434
  15.8 17.3 %collective-permute-start.16 = (bf16[4,256,128]{2,1,0:T(8,128)(2,1)S(1)}, bf16[4,256,128]{2,1,0:T(8,128)(2,1)S(1)}, u32[]{:S(2)}, u32[]{:S(2)}) collective-permute-start(bf16[4,256,128]{2,1,0:T(8,128)(2,1)S(1)} %pad_maximum_fusion.refs_3_), channel_id=1, source_target_pairs={{0,32},{8,40},{16,48},{24,56},{32,0},{40,8},{48,16},{56,24},{64,96... | collective-permute-start | bytes 786440 | tf_op jit(solution)/shard_map/ppermute | solution.py:425
  18.8 14.2 %collective-permute-start.15 = (bf16[4,256,128]{2,1,0:T(8,128)(2,1)S(1)}, bf16[4,256,128]{2,1,0:T(8,128)(2,1)S(1)}, u32[]{:S(2)}, u32[]{:S(2)}) collective-permute-start(bf16[4,256,128]{2,1,0:T(8,128)(2,1)S(1)} %pad_maximum_fusion.refs_3_), channel_id=1, source_target_pairs={{0,16},{8,24},{16,32},{24,40},{32,48},{40,56},{48,0},{56,8},{64,80... | collective-permute-start | bytes 786440 | tf_op jit(solution)/shard_map/ppermute | solution.py:425
  19.4 13.6 %collective-permute-start.17 = (bf16[4,256,128]{2,1,0:T(8,128)(2,1)S(1)}, bf16[4,256,128]{2,1,0:T(8,128)(2,1)S(1)}, u32[]{:S(2)}, u32[]{:S(2)}) collective-permute-start(bf16[4,256,128]{2,1,0:T(8,128)(2,1)S(1)} %pad_maximum_fusion.refs_3_), channel_id=1, source_target_pairs={{0,48},{8,56},{16,0},{24,8},{32,16},{40,24},{48,32},{56,40},{64,11... | collective-permute-start | bytes 786440 | tf_op jit(solution)/shard_map/ppermute | solution.py:425
  22.1 4.8 %collective-permute-start.13 = (f32[8,128]{1,0:T(8,128)S(1)}, f32[8,128]{1,0:T(8,128)S(1)}, u32[]{:S(2)}, u32[]{:S(2)}) collective-permute-start(f32[8,128]{1,0:T(8,128)S(1)} %add.20), channel_id=1, source_target_pairs={{0,3},{1,2},{2,1},{3,0},{4,7},{5,6},{6,5},{7,4},{8,11},{9,10},{10,... | collective-permute-start | bytes 12296 | tf_op jit(solution)/shard_map/ppermute | solution.py:437
  26.9 6.2 %collective-permute-start.14 = (f32[8,128]{1,0:T(8,128)S(1)}, f32[8,128]{1,0:T(8,128)S(1)}, u32[]{:S(2)}, u32[]{:S(2)}) collective-permute-start(f32[8,128]{1,0:T(8,128)S(1)} %add.21), channel_id=1, source_target_pairs={{0,132},{1,133},{2,134},{3,135},{4,128},{5,129},{6,130},{7,131},{8... | collective-permute-start | bytes 12296 | tf_op jit(solution)/shard_map/ppermute | solution.py:441
  33.1 2.8 %collective-permute-start.19 = (bf16[4,256,128]{2,1,0:T(8,128)(2,1)S(1)}, bf16[4,256,128]{2,1,0:T(8,128)(2,1)S(1)}, u32[]{:S(2)}, u32[]{:S(2)}) collective-permute-start(bf16[4,256,128]{2,1,0:T(8,128)(2,1)S(1)} %pad_maximum_fusion.refs_3_), channel_id=1, source_target_pairs={{0,8},{8,0},{16,24},{24,16},{32,40},{40,32},{48,56},{56,48},{64,72... | collective-permute-start | bytes 786440 | tf_op jit(solution)/shard_map/ppermute | solution.py:425
  33.2 2.7 %collective-permute-start.20 = (bf16[4,256,128]{2,1,0:T(8,128)(2,1)S(1)}, bf16[4,256,128]{2,1,0:T(8,128)(2,1)S(1)}, u32[]{:S(2)}, u32[]{:S(2)}) collective-permute-start(bf16[4,256,128]{2,1,0:T(8,128)(2,1)S(1)} %collective-permute-done.15.refs_4_), channel_id=1, source_target_pairs={{0,8},{8,0},{16,24},{24,16},{32,40},{40,32},{48,56},{56,48},{64,72... | collective-permute-start | bytes 786440 | tf_op jit(solution)/shard_map/ppermute | solution.py:425
  33.7 2.2 %collective-permute-start.21 = (bf16[4,256,128]{2,1,0:T(8,128)(2,1)S(1)}, bf16[4,256,128]{2,1,0:T(8,128)(2,1)S(1)}, u32[]{:S(2)}, u32[]{:S(2)}) collective-permute-start(bf16[4,256,128]{2,1,0:T(8,128)(2,1)S(1)} %collective-permute-done.16.refs_5_), channel_id=1, source_target_pairs={{0,8},{8,0},{16,24},{24,16},{32,40},{40,32},{48,56},{56,48},{64,72... | collective-permute-start | bytes 786440 | tf_op jit(solution)/shard_map/ppermute | solution.py:425
  33.8 2.1 %collective-permute-start.22 = (bf16[4,256,128]{2,1,0:T(8,128)(2,1)S(1)}, bf16[4,256,128]{2,1,0:T(8,128)(2,1)S(1)}, u32[]{:S(2)}, u32[]{:S(2)}) collective-permute-start(bf16[4,256,128]{2,1,0:T(8,128)(2,1)S(1)} %collective-permute-done.17.refs_6_), channel_id=1, source_target_pairs={{0,8},{8,0},{16,24},{24,16},{32,40},{40,32},{48,56},{56,48},{64,72... | collective-permute-start | bytes 786440 | tf_op jit(solution)/shard_map/ppermute | solution.py:425
  34.2 1.6 %collective-permute-start.18 = (f32[8,128]{1,0:T(8,128)S(1)}, f32[8,128]{1,0:T(8,128)S(1)}, u32[]{:S(2)}, u32[]{:S(2)}) collective-permute-start(f32[8,128]{1,0:T(8,128)S(1)} %add.22), channel_id=1, source_target_pairs={{0,8},{8,0},{16,24},{24,16},{32,40},{40,32},{48,56},{56,48},{64,72... | collective-permute-start | bytes 12296 | tf_op jit(solution)/shard_map/ppermute | solution.py:425
  35.9 3.7 %collective-permute-start.23 = (f32[8,128]{1,0:T(8,128)S(1)}, f32[8,128]{1,0:T(8,128)S(1)}, u32[]{:S(2)}, u32[]{:S(2)}) collective-permute-start(f32[8,128]{1,0:T(8,128)S(1)} %add.23), channel_id=1, source_target_pairs={{0,16},{8,24},{16,0},{24,8},{32,48},{40,56},{48,32},{56,40},{64,80... | collective-permute-start | bytes 12296 | tf_op jit(solution)/shard_map/ppermute | solution.py:425
  39.6 5.7 %collective-permute-start.25 = (bf16[4,4,2,128,128]{4,3,2,1,0:T(8,128)(2,1)S(1)}, bf16[4,4,2,128,128]{4,3,2,1,0:T(8,128)(2,1)S(1)}, u32[]{:S(2)}, u32[]{:S(2)}) collective-permute-start(bf16[4,4,2,128,128]{4,3,2,1,0:T(8,128)(2,1)S(1)} %get-tuple-element.135), channel_id=1, source_target_pairs={{0,8},{8,0},{16,24},{24,16},{32,40},{40,32},{48,56},{56,48},{64,72... | collective-permute-start | bytes 3145736 | tf_op jit(solution)/shard_map/ppermute | solution.py:425
  39.6 5.7 %collective-permute-start.24 = (f32[8,128]{1,0:T(8,128)S(1)}, f32[8,128]{1,0:T(8,128)S(1)}, u32[]{:S(2)}, u32[]{:S(2)}) collective-permute-start(f32[8,128]{1,0:T(8,128)S(1)} %add.24), channel_id=1, source_target_pairs={{0,48},{8,56},{16,32},{24,40},{32,16},{40,24},{48,0},{56,8},{64,11... | collective-permute-start | bytes 12296 | tf_op jit(solution)/shard_map/ppermute | solution.py:425
  45.3 0.7 copy-start.4
  47.1 8.2 %collective-permute-start = (bf16[2,2,128,128]{3,2,1,0:T(8,128)(2,1)S(1)}, bf16[2,2,128,128]{3,2,1,0:T(8,128)(2,1)S(1)}, u32[]{:S(2)}, u32[]{:S(2)}) collective-permute-start(bf16[2,2,128,128]{3,2,1,0:T(8,128)(2,1)S(1)} %get-tuple-element.36), channel_id=1, source_target_pairs={{0,48},{8,56},{16,0},{24,8},{32,16},{40,24},{48,32},{56,40},{64,11... | collective-permute-start | bytes 393224 | tf_op jit(solution)/shard_map/cond/branch_0_fun/ppermute | solution.py:425
  50.1 7.4 %collective-permute-start.1 = (bf16[2,2,128,128]{3,2,1,0:T(8,128)(2,1)S(1)}, bf16[2,2,128,128]{3,2,1,0:T(8,128)(2,1)S(1)}, u32[]{:S(2)}, u32[]{:S(2)}) collective-permute-start(bf16[2,2,128,128]{3,2,1,0:T(8,128)(2,1)S(1)} %get-tuple-element.37), channel_id=1, source_target_pairs={{0,32},{8,40},{16,48},{24,56},{32,0},{40,8},{48,16},{56,24},{64,96... | collective-permute-start | bytes 393224 | tf_op jit(solution)/shard_map/cond/branch_0_fun/ppermute | solution.py:425
  50.1 8.7 %collective-permute-start.2 = (bf16[2,2,128,128]{3,2,1,0:T(8,128)(2,1)S(1)}, bf16[2,2,128,128]{3,2,1,0:T(8,128)(2,1)S(1)}, u32[]{:S(2)}, u32[]{:S(2)}) collective-permute-start(bf16[2,2,128,128]{3,2,1,0:T(8,128)(2,1)S(1)} %get-tuple-element.38), channel_id=1, source_target_pairs={{0,16},{8,24},{16,32},{24,40},{32,48},{40,56},{48,0},{56,8},{64,80... | collective-permute-start | bytes 393224 | tf_op jit(solution)/shard_map/cond/branch_0_fun/ppermute | solution.py:425
  59.5 8.4 %collective-permute-start.26 = (bf16[2,128,128]{2,1,0:T(8,128)(2,1)S(1)}, bf16[2,128,128]{2,1,0:T(8,128)(2,1)S(1)}, u32[]{:S(2)}, u32[]{:S(2)}) collective-permute-start(bf16[2,128,128]{2,1,0:T(8,128)(2,1)S(1)} %get-tuple-element.138), channel_id=1, source_target_pairs={{0,192},{8,200},{16,208},{24,216},{32,224},{40,232},{48,240},{56,2... | collective-permute-start | bytes 196616 | tf_op jit(solution)/shard_map/ppermute | solution.py:425
  65.3 5.2 %collective-permute-start.27 = (bf16[2,128,128]{2,1,0:T(8,128)(2,1)S(1)}, bf16[2,128,128]{2,1,0:T(8,128)(2,1)S(1)}, u32[]{:S(2)}, u32[]{:S(2)}) collective-permute-start(bf16[2,128,128]{2,1,0:T(8,128)(2,1)S(1)} %get-tuple-element.139), channel_id=1, source_target_pairs={{0,128},{8,136},{16,144},{24,152},{32,160},{40,168},{48,176},{56,1... | collective-permute-start | bytes 196616 | tf_op jit(solution)/shard_map/ppermute | solution.py:425
  65.3 6.1 %collective-permute-start.28 = (bf16[2,128,128]{2,1,0:T(8,128)(2,1)S(1)}, bf16[2,128,128]{2,1,0:T(8,128)(2,1)S(1)}, u32[]{:S(2)}, u32[]{:S(2)}) collective-permute-start(bf16[2,128,128]{2,1,0:T(8,128)(2,1)S(1)} %get-tuple-element.140), channel_id=1, source_target_pairs={{0,64},{8,72},{16,80},{24,88},{32,96},{40,104},{48,112},{56,120},{... | collective-permute-start | bytes 196616 | tf_op jit(solution)/shard_map/ppermute | solution.py:425

commit v5 on v4

--- a/solution.py
+++ b/solution.py
@@ -232,8 +232,8 @@
     )(keys, values, ratios)
 
 
-def block_sums(bounds, ratios, packets):
-    def kern(b_ref, ratio_ref, p1, p2, p3, sums_ref, rides, sem):
+def block_sums(bounds, total, packets):
+    def kern(b_ref, total_ref, p1, p2, p3, sums_ref, rides, sem):
         copies = [
             pltpu.make_async_copy(p.at[pl.ds(2 * BLOCK, 16)], rides.at[k], sem.at[k])
             for k, p in enumerate((p1, p2, p3))
@@ -242,10 +242,7 @@
             copy.start()
         me = lax.axis_index("seq")
         row = lax.broadcasted_iota(jnp.int32, (RESP, DH), 0)
-        own = ratio_ref[0]
-        for t in range(1, ratios.shape[0]):
-            own = own + ratio_ref[t]
-        part = jnp.full((1, DH), own, f32)
+        part = total_ref[...]
         sums = jnp.zeros((RESP, DH), f32)
         for s in range(4):
             first = (lax.rem(me // 8 - s + 4, 4) * 8 + lax.rem(me, 8)) * BLOCK
@@ -261,11 +258,11 @@
     return pl.pallas_call(
         kern,
         out_shape=jax.ShapeDtypeStruct((RESP, DH), f32),
-        in_specs=[S, S, A, A, A],
+        in_specs=[S, V, A, A, A],
         out_specs=V,
         scratch_shapes=[pltpu.VMEM((3, 16, DH), bf), pltpu.SemaphoreType.DMA((3,))],
         compiler_params=SMALL,
-    )(bounds, ratios, *packets)
+    )(bounds, total, *packets)
 
 
 def live_planes(b_ref, z):
@@ -303,14 +300,14 @@
     )(bounds)
 
 
-def core_add(slots, sums, bounds, pairs, keep, got):
-    def kern(sums_ref, b_ref, p_ref, keep_ref, got_ref, o0, o1, o2, o3, w_ref, mean, coef):
+def core_add(slots, sums, table, keep, got):
+    def kern(sums_ref, b_ref, keep_ref, got_ref, o0, o1, o2, o3, w_ref, mean, coef):
         me = lax.axis_index("seq")
         for r in range(RESP):
             mean[r] = sums_ref[r, 0] / (b_ref[r + 1] - b_ref[r]).astype(f32)
             coef[r] = 0.0
         for p in range(PAIRS):
-            win, lose = p_ref[p, 0], p_ref[p, 1]
+            win, lose = b_ref[RESP + 1 + 2 * p], b_ref[RESP + 2 + 2 * p]
             resid = mean[win] - mean[lose] - 1.0
             coef[win] = coef[win] + resid
             coef[lose] = coef[lose] - resid
@@ -354,11 +351,11 @@
     return pl.pallas_call(
         kern,
         out_shape=(slot, slot, slot, slot, jax.ShapeDtypeStruct((8, 128), f32)),
-        in_specs=[S, S, S, V, V],
+        in_specs=[S, S, V, V],
         out_specs=(V,) * 5,
         scratch_shapes=[pltpu.SMEM((RESP,), f32), pltpu.SMEM((RESP,), f32)],
         compiler_params=SMALL,
-    )(sums, bounds, pairs, keep, got)
+    )(sums, table, keep, got)
 
 
 def x_add(bounds, parts):
@@ -425,12 +422,15 @@
         return lax.ppermute(v, "seq", perm)
 
     packet = pack(key_rows, value_rows, log_ratio)
-    slots = slots_needed(bounds)[0]
     by_z = [packet] + [seq(packet, Z_UP[s]) for s in (1, 2, 3)]
+    table = jnp.concatenate([bounds, pairs.reshape(2 * PAIRS)])
+    total = jnp.broadcast_to(jnp.sum(log_ratio), (1, DH))
+    slots = slots_needed(table)
+    by_z, table, total, slots = lax.optimization_barrier((by_z, table, total, slots))
     column = jnp.stack([p[: 2 * BLOCK] for p in by_z])
     column, by_z = lax.optimization_barrier((column, by_z))
     far = seq(column, X_UP[2])
-    sums, column = lax.optimization_barrier((block_sums(bounds, log_ratio, by_z[1:]), column))
+    sums, column = lax.optimization_barrier((block_sums(table, total, by_z[1:]), column))
     turned = lax.ppermute(sums, "heads", HEAD_Y[0])
     before = seq(column, X_UP[1])
     sums, column = lax.optimization_barrier((sums + turned, column))
@@ -444,21 +444,21 @@
     sums = sums + seq(sums, CORE)
     sums, bufs = lax.optimization_barrier((sums, bufs))
     turned = seq(sums, X_FLIP[0])
-    dq, keep, send = attend(bounds, query_rows, out_grad, bufs)
+    dq, keep, send = attend(table, query_rows, out_grad, bufs)
     sums, send = lax.optimization_barrier((sums + turned, send))
     got = seq(send, CORE)
     sums = sums + seq(sums, X_FLIP[1])
 
     def across_x(slots):
         def branch(sums, keep, got):
-            *by_shift, weight = core_add(slots, sums, bounds, pairs, keep, got)
+            *by_shift, weight = core_add(slots, sums, table, keep, got)
             moved = [seq(by_shift[s], X_DOWN[s]) for s in (1, 2, 3)]
-            return x_add(bounds, [by_shift[0]] + moved), weight
+            return x_add(table, [by_shift[0]] + moved), weight
 
         return branch
 
     summed, weight = lax.switch(
-        slots - 2, [across_x(2), across_x(3), across_x(4)], sums, keep, got
+        slots[0] - 2, [across_x(2), across_x(3), across_x(4)], sums, keep, got
     )
     query_grad = (dq * weight[0, 0]).astype(bf)
     key_grad, value_grad = z_add(summed[0], *[seq(summed[s], Z_DOWN[s]) for s in (1, 2, 3)])

time: 72.4 us -> 77.6 us (1.072)
  starting transfers between devices: 33.6 us -> 36.1 us
  waiting for transfers between devices: 24.9 us -> 27.3 us
    ppermute x20, starting transfers between devices: 27.2 us -> 29.7 us  [seq(): return lax.ppermute(v, 'seq', perm)]
    ppermute x20, waiting for transfers between devices: 19.6 us -> 22 us  [seq(): return lax.ppermute(v, 'seq', perm)]
  transfers between devices with their start and end apart: 23 -> 23, of which waited for: 11 -> 12; matrix products, arithmetic and copies ran while one was open for 4% -> 3% of each run, Pallas kernels for 4% -> 4%
where the time goes in v5:
time: 77.6 us; the launch traced here: 77.5 us
  starting transfers between devices  36.1 us (47%)
  waiting for transfers between devices  27.3 us (35%)
  Pallas kernels  7.65 us (10%)
  local copies, waits for them, and re-layouts  2.79 us (4%)
  other arithmetic  2.12 us (3%)
  between operations  1.46 us (2%)
    ppermute x20, starting transfers between devices, seq(): return lax.ppermute(v, 'seq', perm)  29.7 us
    ppermute x20, waiting for transfers between devices, seq(): return lax.ppermute(v, 'seq', perm)  22 us
    ppermute x1, starting transfers between devices, shards(): sums = sums + lax.ppermute(sums, ('seq', 'heads'), HALVES)  4.6 us
    ppermute x1, waiting for transfers between devices, shards(): turned = lax.ppermute(sums, 'heads', HEAD_Y[1])  3.76 us
    pallas_call x1, Pallas kernels, attend(): pl.pallas_call(kern, out_shape=(jax.ShapeDtypeStruct((BLOCK, ROWS), f32),...  2 us
    ppermute x1, waiting for transfers between devices, shards(): sums = sums + lax.ppermute(sums, ('seq', 'heads'), HALVES)  1.58 us
  transfers between devices with their start and end apart: 23, of which 12 were waited for; matrix products, arithmetic and copies ran while one was open for 3% of the time, Pallas kernels for 4%

profile of v5, /device:TPU:24, one launch (start us, length us, event | category | flops | bytes accessed | tf_op | source)
XLA Modules:
  0.0 77.5 jit_solution(15479941507794312171)
XLA Ops:
  0.6 1.5 %shard_map.94 = bf16[272,128]{1,0:T(8,128)(2,1)} custom-call(bf16[128,128]{1,0:T(8,128)(2,1)} %k_ref.1, bf16[128,128]{1,0:T(8,128)(2,1)} %v_ref.1, f32[16]{0:T(128)} %ratio_ref.1), custom_call_target="tpu_custom_call" | custom-call | tf_op jit(solution)/shard_map/pallas_call | solution.py:227
  2.1 4.6 %collective-permute-start.11 = (bf16[272,128]{1,0:T(8,128)(2,1)}, bf16[272,128]{1,0:T(8,128)(2,1)S(1)}, u32[]{:S(2)}, u32[]{:S(2)}) collective-permute-start(bf16[272,128]{1,0:T(8,128)(2,1)} %shard_map.94), channel_id=1, source_target_pairs={{0,192},{8,200},{16,208},{24,216},{32,224},{40,232},{48,240},{56,2... | collective-permute-start | bytes 208904 | tf_op jit(solution)/shard_map/ppermute | solution.py:422
  6.7 0.7 collective-permute-start.9
  7.4 0.6 reduce_sum.9
  8.0 0.1 copy.11
  8.1 0.1 reshape.14
  8.2 0.6 copy-done.4
  8.7 0.1 pad_add_fusion.b_ref.refs_0_
  8.8 1.2 %shard_map.95 = s32[1]{0:T(128)} custom-call(s32[25]{0:T(128)S(1)} %pad_add_fusion.b_ref.refs_0_), custom_call_target="tpu_custom_call" | custom-call | tf_op jit(solution)/shard_map/pallas_call | solution.py:294
  10.1 3.5 %collective-permute-done.10.p2 = bf16[272,128]{1,0:T(8,128)(2,1)S(1)} collective-permute-done((bf16[272,128]{1,0:T(8,128)(2,1)}, bf16[272,128]{1,0:T(8,128)(2,1)S(1)}, u32[]{:S(2)}, u32[]{:S(2)}) %collective-permute-start.10) | collective-permute-done | bytes 69664 | tf_op jit(solution)/shard_map/ppermute | solution.py:422
  13.6 0.6 broadcast_in_dim.3.total_ref
  14.2 0.9 %slice_bitcast_fusion.2 = (bf16[1,256,128]{2,1,0:T(8,128)(2,1)S(1)}, bf16[1,256,128]{2,1,0:T(8,128)(2,1)S(1)}) fusion(bf16[272,128]{1,0:T(8,128)(2,1)S(1)} %collective-permute-done.9.p1, bf16[272,128]{1,0:T(8,128)(2,1)} %shard_map.94), kind=kLoop, calls=%fused_computation.4 | loop fusion | bytes 262144 | tf_op jit(solution)/shard_map/stack | solution.py:430
  15.2 0.7 shard_map.96
  15.9 0.8 %collective-permute-start.12 = (f32[8,128]{1,0:T(8,128)S(1)}, f32[8,128]{1,0:T(8,128)S(1)}, u32[]{:S(2)}, u32[]{:S(2)}) collective-permute-start(f32[8,128]{1,0:T(8,128)S(1)} %shard_map.96), channel_id=1, source_target_pairs={{0,1},{1,0},{2,3},{3,2},{4,5},{5,4},{6,7},{7,6},{8,9},{9,8},{10,11... | collective-permute-start | bytes 12296 | tf_op jit(solution)/shard_map/ppermute | solution.py:434
  16.7 3.0 %collective-permute-start.16 = (bf16[4,256,128]{2,1,0:T(8,128)(2,1)S(1)}, bf16[4,256,128]{2,1,0:T(8,128)(2,1)S(1)}, u32[]{:S(2)}, u32[]{:S(2)}) collective-permute-start(bf16[4,256,128]{2,1,0:T(8,128)(2,1)S(1)} %pad_maximum_fusion.refs_3_), channel_id=1, source_target_pairs={{0,32},{8,40},{16,48},{24,56},{32,0},{40,8},{48,16},{56,24},{64,96... | collective-permute-start | bytes 786440 | tf_op jit(solution)/shard_map/ppermute | solution.py:422
  19.7 0.6 collective-permute-start.15
  20.3 2.6 %collective-permute-start.17 = (bf16[4,256,128]{2,1,0:T(8,128)(2,1)S(1)}, bf16[4,256,128]{2,1,0:T(8,128)(2,1)S(1)}, u32[]{:S(2)}, u32[]{:S(2)}) collective-permute-start(bf16[4,256,128]{2,1,0:T(8,128)(2,1)S(1)} %pad_maximum_fusion.refs_3_), channel_id=1, source_target_pairs={{0,48},{8,56},{16,0},{24,8},{32,16},{40,24},{48,32},{56,40},{64,11... | collective-permute-start | bytes 786440 | tf_op jit(solution)/shard_map/ppermute | solution.py:422
  23.0 1.1 %collective-permute-start.13 = (f32[8,128]{1,0:T(8,128)S(1)}, f32[8,128]{1,0:T(8,128)S(1)}, u32[]{:S(2)}, u32[]{:S(2)}) collective-permute-start(f32[8,128]{1,0:T(8,128)S(1)} %add.20), channel_id=1, source_target_pairs={{0,3},{1,2},{2,1},{3,0},{4,7},{5,6},{6,5},{7,4},{8,11},{9,10},{10,... | collective-permute-start | bytes 12296 | tf_op jit(solution)/shard_map/ppermute | solution.py:437
  24.0 3.8 %collective-permute-done.13 = f32[8,128]{1,0:T(8,128)S(1)} collective-permute-done((f32[8,128]{1,0:T(8,128)S(1)}, f32[8,128]{1,0:T(8,128)S(1)}, u32[]{:S(2)}, u32[]{:S(2)}) %collective-permute-start.13) | collective-permute-done | bytes 4128 | tf_op jit(solution)/shard_map/ppermute | solution.py:437
  27.8 4.6 %collective-permute-start.14 = (f32[8,128]{1,0:T(8,128)S(1)}, f32[8,128]{1,0:T(8,128)S(1)}, u32[]{:S(2)}, u32[]{:S(2)}) collective-permute-start(f32[8,128]{1,0:T(8,128)S(1)} %add.21), channel_id=1, source_target_pairs={{0,132},{1,133},{2,134},{3,135},{4,128},{5,129},{6,130},{7,131},{8... | collective-permute-start | bytes 12296 | tf_op jit(solution)/shard_map/ppermute | solution.py:441
  32.4 1.6 %collective-permute-done.14 = f32[8,128]{1,0:T(8,128)S(1)} collective-permute-done((f32[8,128]{1,0:T(8,128)S(1)}, f32[8,128]{1,0:T(8,128)S(1)}, u32[]{:S(2)}, u32[]{:S(2)}) %collective-permute-start.14) | collective-permute-done | bytes 4128 | tf_op jit(solution)/shard_map/ppermute | solution.py:441
  34.0 0.1 collective-permute-start.19
  34.1 0.5 collective-permute-start.20
  34.6 0.1 collective-permute-start.21
  34.7 0.4 collective-permute-start.22
  35.1 0.1 collective-permute-start.18
  35.2 1.5 %collective-permute-done.18 = f32[8,128]{1,0:T(8,128)S(1)} collective-permute-done((f32[8,128]{1,0:T(8,128)S(1)}, f32[8,128]{1,0:T(8,128)S(1)}, u32[]{:S(2)}, u32[]{:S(2)}) %collective-permute-start.18) | collective-permute-done | bytes 4128 | tf_op jit(solution)/shard_map/ppermute | solution.py:422
  36.8 0.1 collective-permute-start.23
  36.9 2.0 %shard_map.97 = (f32[128,1024]{1,0:T(8,128)S(1)}, bf16[4,4,2,128,128]{4,3,2,1,0:T(8,128)(2,1)S(1)}, bf16[4,4,2,128,128]{4,3,2,1,0:T(8,128)(2,1)S(1)}) custom-call(s32[25]{0:T(128)S(1)} %pad_add_fusion.b_ref.refs_0_, bf16[128,1024]{1,0:T(8,128)(2,1)S(1)} %copy-done, bf16[128,1024]{1,0:T(8,128)(2,1)S(1)} %copy-done.1, ...), custom_call_target="tpu_custom_call" | custom-call | flops 10000000000 | bytes 5242880 | tf_op jit(solution)/shard_map/pallas_call | solution.py:156
  38.9 1.6 %collective-permute-done.23 = f32[8,128]{1,0:T(8,128)S(1)} collective-permute-done((f32[8,128]{1,0:T(8,128)S(1)}, f32[8,128]{1,0:T(8,128)S(1)}, u32[]{:S(2)}, u32[]{:S(2)}) %collective-permute-start.23) | collective-permute-done | bytes 4128 | tf_op jit(solution)/shard_map/ppermute | solution.py:422
  40.5 3.8 %collective-permute-start.24 = (f32[8,128]{1,0:T(8,128)S(1)}, f32[8,128]{1,0:T(8,128)S(1)}, u32[]{:S(2)}, u32[]{:S(2)}) collective-permute-start(f32[8,128]{1,0:T(8,128)S(1)} %add.24), channel_id=1, source_target_pairs={{0,48},{8,56},{16,32},{24,40},{32,16},{40,24},{48,0},{56,8},{64,11... | collective-permute-start | bytes 12296 | tf_op jit(solution)/shard_map/ppermute | solution.py:422
  45.0 0.9 %collective-permute-done.24 = f32[8,128]{1,0:T(8,128)S(1)} collective-permute-done((f32[8,128]{1,0:T(8,128)S(1)}, f32[8,128]{1,0:T(8,128)S(1)}, u32[]{:S(2)}, u32[]{:S(2)}) %collective-permute-start.24) | collective-permute-done | bytes 4128 | tf_op jit(solution)/shard_map/ppermute | solution.py:422
  45.9 16.2 %conditional.1 = (bf16[2,128,128]{2,1,0:T(8,128)(2,1)S(1)}, bf16[2,128,128]{2,1,0:T(8,128)(2,1)S(1)}, bf16[2,128,128]{2,1,0:T(8,128)(2,1)S(1)}, bf16[2,128,128]{2,1,0:T(8,128)(2,1)S(1)}, f32[8,128]{1,0:T(8,128)S(1)}) conditional(s32[]{:T(128)} %bitcast.4, (f32[8,128]{1,0:T(8,128)S(1)}, s32[25]{0:T(128)S(1)}, ...), branch_computations={%region_1.0_spmd, %region_2.0_spmd, %region_3.0_spmd} | conditional | bytes 3145888 | solution.py:460
  45.9 1.0 %branch_1_fun.2 = (bf16[3,2,128,128]{3,2,1,0:T(8,128)(2,1)S(1)}, bf16[3,2,128,128]{3,2,1,0:T(8,128)(2,1)S(1)}, bf16[3,2,128,128]{3,2,1,0:T(8,128)(2,1)S(1)}, bf1...) custom-call(f32[8,128]{1,0:T(8,128)S(1)} %get-tuple-element.38.sums_ref, s32[25]{0:T(128)S(1)} %get-tuple-element.37.b_ref, ...), custom_call_target="tpu_custom_call" | custom-call | tf_op jit(solution)/shard_map/cond/branch_1_fun/pallas_call | solution.py:351
  46.9 3.3 %collective-permute-start.3 = (bf16[3,2,128,128]{3,2,1,0:T(8,128)(2,1)S(1)}, bf16[3,2,128,128]{3,2,1,0:T(8,128)(2,1)S(1)}, u32[]{:S(2)}, u32[]{:S(2)}) collective-permute-start(bf16[3,2,128,128]{3,2,1,0:T(8,128)(2,1)S(1)} %get-tuple-element.42), channel_id=1, source_target_pairs={{0,48},{8,56},{16,0},{24,8},{32,16},{40,24},{48,32},{56,40},{64,11... | collective-permute-start | bytes 589832 | tf_op jit(solution)/shard_map/cond/branch_1_fun/ppermute | solution.py:422
  50.2 1.0 %collective-permute-start.5 = (bf16[3,2,128,128]{3,2,1,0:T(8,128)(2,1)S(1)}, bf16[3,2,128,128]{3,2,1,0:T(8,128)(2,1)S(1)}, u32[]{:S(2)}, u32[]{:S(2)}) collective-permute-start(bf16[3,2,128,128]{3,2,1,0:T(8,128)(2,1)S(1)} %get-tuple-element.44), channel_id=1, source_target_pairs={{0,16},{8,24},{16,32},{24,40},{32,48},{40,56},{48,0},{56,8},{64,80... | collective-permute-start | bytes 589832 | tf_op jit(solution)/shard_map/cond/branch_1_fun/ppermute | solution.py:422
  51.2 6.9 %collective-permute-done.3.i1 = bf16[3,2,128,128]{3,2,1,0:T(8,128)(2,1)S(1)} collective-permute-done((bf16[3,2,128,128]{3,2,1,0:T(8,128)(2,1)S(1)}, bf16[3,2,128,128]{3,2,1,0:T(8,128)(2,1)S(1)}, u32[]{:S(2)}, u32[]{:S(2)}) %collective-permute-start.3) | collective-permute-done | bytes 196640 | tf_op jit(solution)/shard_map/cond/branch_1_fun/ppermute | solution.py:422
  58.0 1.5 %collective-permute-done.4.i2 = bf16[3,2,128,128]{3,2,1,0:T(8,128)(2,1)S(1)} collective-permute-done((bf16[3,2,128,128]{3,2,1,0:T(8,128)(2,1)S(1)}, bf16[3,2,128,128]{3,2,1,0:T(8,128)(2,1)S(1)}, u32[]{:S(2)}, u32[]{:S(2)}) %collective-permute-start.4) | collective-permute-done | bytes 196640 | tf_op jit(solution)/shard_map/cond/branch_1_fun/ppermute | solution.py:422
  59.5 1.9 %collective-permute-done.5.i3 = bf16[3,2,128,128]{3,2,1,0:T(8,128)(2,1)S(1)} collective-permute-done((bf16[3,2,128,128]{3,2,1,0:T(8,128)(2,1)S(1)}, bf16[3,2,128,128]{3,2,1,0:T(8,128)(2,1)S(1)}, u32[]{:S(2)}, u32[]{:S(2)}) %collective-permute-start.5) | collective-permute-done | bytes 196640 | tf_op jit(solution)/shard_map/cond/branch_1_fun/ppermute | solution.py:422
  61.4 0.7 branch_1_fun.3
  62.1 0.5 slice.19
  62.6 8.2 %collective-permute-start.26 = (bf16[2,128,128]{2,1,0:T(8,128)(2,1)S(1)}, bf16[2,128,128]{2,1,0:T(8,128)(2,1)S(1)}, u32[]{:S(2)}, u32[]{:S(2)}) collective-permute-start(bf16[2,128,128]{2,1,0:T(8,128)(2,1)S(1)} %get-tuple-element.143), channel_id=1, source_target_pairs={{0,192},{8,200},{16,208},{24,216},{32,224},{40,232},{48,240},{56,2... | collective-permute-start | bytes 196616 | tf_op jit(solution)/shard_map/ppermute | solution.py:422
  70.8 0.6 collective-permute-start.28
  71.3 1.4 %multiply_convert_fusion = bf16[128,1024]{1,0:T(8,128)(2,1)} fusion(f32[128,1024]{1,0:T(8,128)S(1)} %get-tuple-element.134, f32[]{:T(128)} %bitcast.5), kind=kLoop, calls=%fused_computation | loop fusion | flops 262144 | bytes 786436 | tf_op jit(solution)/shard_map/convert_element_type | solution.py:463
  72.7 0.6 collective-permute-done.26.i1
  73.3 2.8 %collective-permute-done.27.i2 = bf16[2,128,128]{2,1,0:T(8,128)(2,1)S(1)} collective-permute-done((bf16[2,128,128]{2,1,0:T(8,128)(2,1)S(1)}, bf16[2,128,128]{2,1,0:T(8,128)(2,1)S(1)}, u32[]{:S(2)}, u32[]{:S(2)}) %collective-permute-start.27) | collective-permute-done | bytes 65568 | tf_op jit(solution)/shard_map/ppermute | solution.py:422
  76.1 0.7 collective-permute-done.28.i3
  76.8 0.7 shard_map.98
  (32 shorter events, 0.1 us)
Async XLA Ops:
  0.6 6.8 %copy-start.3 = (f32[16]{0:T(128)S(1)}, f32[16]{0:T(128)}, u32[]{:S(2)}) copy-start(f32[16]{0:T(128)} %ratio_ref.1) | copy-start | bytes 196
  2.1 5.9 %copy-start.2 = (s32[8,2]{0,1:T(2,128)S(1)}, s32[8,2]{0,1:T(2,128)}, u32[]{:S(2)}) copy-start(s32[8,2]{0,1:T(2,128)} %param.17) | copy-start | bytes 196
  2.1 8.0 %collective-permute-start.11 = (bf16[272,128]{1,0:T(8,128)(2,1)}, bf16[272,128]{1,0:T(8,128)(2,1)S(1)}, u32[]{:S(2)}, u32[]{:S(2)}) collective-permute-start(bf16[272,128]{1,0:T(8,128)(2,1)} %shard_map.94), channel_id=1, source_target_pairs={{0,192},{8,200},{16,208},{24,216},{32,224},{40,232},{48,240},{56,2... | collective-permute-start | bytes 208904 | tf_op jit(solution)/shard_map/ppermute | solution.py:422
  6.7 6.9 %collective-permute-start.10 = (bf16[272,128]{1,0:T(8,128)(2,1)}, bf16[272,128]{1,0:T(8,128)(2,1)S(1)}, u32[]{:S(2)}, u32[]{:S(2)}) collective-permute-start(bf16[272,128]{1,0:T(8,128)(2,1)} %shard_map.94), channel_id=1, source_target_pairs={{0,128},{8,136},{16,144},{24,152},{32,160},{40,168},{48,176},{56,1... | collective-permute-start | bytes 208904 | tf_op jit(solution)/shard_map/ppermute | solution.py:422
  6.7 6.9 %collective-permute-start.9 = (bf16[272,128]{1,0:T(8,128)(2,1)}, bf16[272,128]{1,0:T(8,128)(2,1)S(1)}, u32[]{:S(2)}, u32[]{:S(2)}) collective-permute-start(bf16[272,128]{1,0:T(8,128)(2,1)} %shard_map.94), channel_id=1, source_target_pairs={{0,64},{8,72},{16,80},{24,88},{32,96},{40,104},{48,112},{56,120},{... | collective-permute-start | bytes 208904 | tf_op jit(solution)/shard_map/ppermute | solution.py:422
  8.1 0.7 copy-start.4
  15.1 21.8 %copy-start.1 = (bf16[128,1024]{1,0:T(8,128)(2,1)S(1)}, bf16[128,1024]{1,0:T(8,128)(2,1)}, u32[]{:S(2)}) copy-start(bf16[128,1024]{1,0:T(8,128)(2,1)} %refs_2_.1) | copy-start | bytes 786436
  15.2 21.7 %copy-start = (bf16[128,1024]{1,0:T(8,128)(2,1)S(1)}, bf16[128,1024]{1,0:T(8,128)(2,1)}, u32[]{:S(2)}) copy-start(bf16[128,1024]{1,0:T(8,128)(2,1)} %refs_1_.1) | copy-start | bytes 786436
  15.9 4.5 %collective-permute-start.12 = (f32[8,128]{1,0:T(8,128)S(1)}, f32[8,128]{1,0:T(8,128)S(1)}, u32[]{:S(2)}, u32[]{:S(2)}) collective-permute-start(f32[8,128]{1,0:T(8,128)S(1)} %shard_map.96), channel_id=1, source_target_pairs={{0,1},{1,0},{2,3},{3,2},{4,5},{5,4},{6,7},{7,6},{8,9},{9,8},{10,11... | collective-permute-start | bytes 12296 | tf_op jit(solution)/shard_map/ppermute | solution.py:434
  16.7 17.3 %collective-permute-start.16 = (bf16[4,256,128]{2,1,0:T(8,128)(2,1)S(1)}, bf16[4,256,128]{2,1,0:T(8,128)(2,1)S(1)}, u32[]{:S(2)}, u32[]{:S(2)}) collective-permute-start(bf16[4,256,128]{2,1,0:T(8,128)(2,1)S(1)} %pad_maximum_fusion.refs_3_), channel_id=1, source_target_pairs={{0,32},{8,40},{16,48},{24,56},{32,0},{40,8},{48,16},{56,24},{64,96... | collective-permute-start | bytes 786440 | tf_op jit(solution)/shard_map/ppermute | solution.py:422
  19.7 14.3 %collective-permute-start.15 = (bf16[4,256,128]{2,1,0:T(8,128)(2,1)S(1)}, bf16[4,256,128]{2,1,0:T(8,128)(2,1)S(1)}, u32[]{:S(2)}, u32[]{:S(2)}) collective-permute-start(bf16[4,256,128]{2,1,0:T(8,128)(2,1)S(1)} %pad_maximum_fusion.refs_3_), channel_id=1, source_target_pairs={{0,16},{8,24},{16,32},{24,40},{32,48},{40,56},{48,0},{56,8},{64,80... | collective-permute-start | bytes 786440 | tf_op jit(solution)/shard_map/ppermute | solution.py:422
  20.3 13.7 %collective-permute-start.17 = (bf16[4,256,128]{2,1,0:T(8,128)(2,1)S(1)}, bf16[4,256,128]{2,1,0:T(8,128)(2,1)S(1)}, u32[]{:S(2)}, u32[]{:S(2)}) collective-permute-start(bf16[4,256,128]{2,1,0:T(8,128)(2,1)S(1)} %pad_maximum_fusion.refs_3_), channel_id=1, source_target_pairs={{0,48},{8,56},{16,0},{24,8},{32,16},{40,24},{48,32},{56,40},{64,11... | collective-permute-start | bytes 786440 | tf_op jit(solution)/shard_map/ppermute | solution.py:422
  23.0 4.8 %collective-permute-start.13 = (f32[8,128]{1,0:T(8,128)S(1)}, f32[8,128]{1,0:T(8,128)S(1)}, u32[]{:S(2)}, u32[]{:S(2)}) collective-permute-start(f32[8,128]{1,0:T(8,128)S(1)} %add.20), channel_id=1, source_target_pairs={{0,3},{1,2},{2,1},{3,0},{4,7},{5,6},{6,5},{7,4},{8,11},{9,10},{10,... | collective-permute-start | bytes 12296 | tf_op jit(solution)/shard_map/ppermute | solution.py:437
  27.8 6.2 %collective-permute-start.14 = (f32[8,128]{1,0:T(8,128)S(1)}, f32[8,128]{1,0:T(8,128)S(1)}, u32[]{:S(2)}, u32[]{:S(2)}) collective-permute-start(f32[8,128]{1,0:T(8,128)S(1)} %add.21), channel_id=1, source_target_pairs={{0,132},{1,133},{2,134},{3,135},{4,128},{5,129},{6,130},{7,131},{8... | collective-permute-start | bytes 12296 | tf_op jit(solution)/shard_map/ppermute | solution.py:441
  34.0 2.8 %collective-permute-start.19 = (bf16[4,256,128]{2,1,0:T(8,128)(2,1)S(1)}, bf16[4,256,128]{2,1,0:T(8,128)(2,1)S(1)}, u32[]{:S(2)}, u32[]{:S(2)}) collective-permute-start(bf16[4,256,128]{2,1,0:T(8,128)(2,1)S(1)} %pad_maximum_fusion.refs_3_), channel_id=1, source_target_pairs={{0,8},{8,0},{16,24},{24,16},{32,40},{40,32},{48,56},{56,48},{64,72... | collective-permute-start | bytes 786440 | tf_op jit(solution)/shard_map/ppermute | solution.py:422
  34.1 2.7 %collective-permute-start.20 = (bf16[4,256,128]{2,1,0:T(8,128)(2,1)S(1)}, bf16[4,256,128]{2,1,0:T(8,128)(2,1)S(1)}, u32[]{:S(2)}, u32[]{:S(2)}) collective-permute-start(bf16[4,256,128]{2,1,0:T(8,128)(2,1)S(1)} %collective-permute-done.15.refs_4_), channel_id=1, source_target_pairs={{0,8},{8,0},{16,24},{24,16},{32,40},{40,32},{48,56},{56,48},{64,72... | collective-permute-start | bytes 786440 | tf_op jit(solution)/shard_map/ppermute | solution.py:422
  34.6 2.2 %collective-permute-start.21 = (bf16[4,256,128]{2,1,0:T(8,128)(2,1)S(1)}, bf16[4,256,128]{2,1,0:T(8,128)(2,1)S(1)}, u32[]{:S(2)}, u32[]{:S(2)}) collective-permute-start(bf16[4,256,128]{2,1,0:T(8,128)(2,1)S(1)} %collective-permute-done.16.refs_5_), channel_id=1, source_target_pairs={{0,8},{8,0},{16,24},{24,16},{32,40},{40,32},{48,56},{56,48},{64,72... | collective-permute-start | bytes 786440 | tf_op jit(solution)/shard_map/ppermute | solution.py:422
  34.7 2.1 %collective-permute-start.22 = (bf16[4,256,128]{2,1,0:T(8,128)(2,1)S(1)}, bf16[4,256,128]{2,1,0:T(8,128)(2,1)S(1)}, u32[]{:S(2)}, u32[]{:S(2)}) collective-permute-start(bf16[4,256,128]{2,1,0:T(8,128)(2,1)S(1)} %collective-permute-done.17.refs_6_), channel_id=1, source_target_pairs={{0,8},{8,0},{16,24},{24,16},{32,40},{40,32},{48,56},{56,48},{64,72... | collective-permute-start | bytes 786440 | tf_op jit(solution)/shard_map/ppermute | solution.py:422
  35.1 1.6 %collective-permute-start.18 = (f32[8,128]{1,0:T(8,128)S(1)}, f32[8,128]{1,0:T(8,128)S(1)}, u32[]{:S(2)}, u32[]{:S(2)}) collective-permute-start(f32[8,128]{1,0:T(8,128)S(1)} %add.22), channel_id=1, source_target_pairs={{0,8},{8,0},{16,24},{24,16},{32,40},{40,32},{48,56},{56,48},{64,72... | collective-permute-start | bytes 12296 | tf_op jit(solution)/shard_map/ppermute | solution.py:422
  36.8 3.7 %collective-permute-start.23 = (f32[8,128]{1,0:T(8,128)S(1)}, f32[8,128]{1,0:T(8,128)S(1)}, u32[]{:S(2)}, u32[]{:S(2)}) collective-permute-start(f32[8,128]{1,0:T(8,128)S(1)} %add.23), channel_id=1, source_target_pairs={{0,16},{8,24},{16,0},{24,8},{32,48},{40,56},{48,32},{56,40},{64,80... | collective-permute-start | bytes 12296 | tf_op jit(solution)/shard_map/ppermute | solution.py:422
  40.5 5.4 %collective-permute-start.25 = (bf16[4,4,2,128,128]{4,3,2,1,0:T(8,128)(2,1)S(1)}, bf16[4,4,2,128,128]{4,3,2,1,0:T(8,128)(2,1)S(1)}, u32[]{:S(2)}, u32[]{:S(2)}) collective-permute-start(bf16[4,4,2,128,128]{4,3,2,1,0:T(8,128)(2,1)S(1)} %get-tuple-element.140), channel_id=1, source_target_pairs={{0,8},{8,0},{16,24},{24,16},{32,40},{40,32},{48,56},{56,48},{64,72... | collective-permute-start | bytes 3145736 | tf_op jit(solution)/shard_map/ppermute | solution.py:422
  40.5 5.4 %collective-permute-start.24 = (f32[8,128]{1,0:T(8,128)S(1)}, f32[8,128]{1,0:T(8,128)S(1)}, u32[]{:S(2)}, u32[]{:S(2)}) collective-permute-start(f32[8,128]{1,0:T(8,128)S(1)} %add.24), channel_id=1, source_target_pairs={{0,48},{8,56},{16,32},{24,40},{32,16},{40,24},{48,0},{56,8},{64,11... | collective-permute-start | bytes 12296 | tf_op jit(solution)/shard_map/ppermute | solution.py:422
  46.9 11.1 %collective-permute-start.3 = (bf16[3,2,128,128]{3,2,1,0:T(8,128)(2,1)S(1)}, bf16[3,2,128,128]{3,2,1,0:T(8,128)(2,1)S(1)}, u32[]{:S(2)}, u32[]{:S(2)}) collective-permute-start(bf16[3,2,128,128]{3,2,1,0:T(8,128)(2,1)S(1)} %get-tuple-element.42), channel_id=1, source_target_pairs={{0,48},{8,56},{16,0},{24,8},{32,16},{40,24},{48,32},{56,40},{64,11... | collective-permute-start | bytes 589832 | tf_op jit(solution)/shard_map/cond/branch_1_fun/ppermute | solution.py:422
  50.2 9.3 %collective-permute-start.4 = (bf16[3,2,128,128]{3,2,1,0:T(8,128)(2,1)S(1)}, bf16[3,2,128,128]{3,2,1,0:T(8,128)(2,1)S(1)}, u32[]{:S(2)}, u32[]{:S(2)}) collective-permute-start(bf16[3,2,128,128]{3,2,1,0:T(8,128)(2,1)S(1)} %get-tuple-element.43), channel_id=1, source_target_pairs={{0,32},{8,40},{16,48},{24,56},{32,0},{40,8},{48,16},{56,24},{64,96... | collective-permute-start | bytes 589832 | tf_op jit(solution)/shard_map/cond/branch_1_fun/ppermute | solution.py:422
  50.2 11.2 %collective-permute-start.5 = (bf16[3,2,128,128]{3,2,1,0:T(8,128)(2,1)S(1)}, bf16[3,2,128,128]{3,2,1,0:T(8,128)(2,1)S(1)}, u32[]{:S(2)}, u32[]{:S(2)}) collective-permute-start(bf16[3,2,128,128]{3,2,1,0:T(8,128)(2,1)S(1)} %get-tuple-element.44), channel_id=1, source_target_pairs={{0,16},{8,24},{16,32},{24,40},{32,48},{40,56},{48,0},{56,8},{64,80... | collective-permute-start | bytes 589832 | tf_op jit(solution)/shard_map/cond/branch_1_fun/ppermute | solution.py:422
  62.6 10.7 %collective-permute-start.26 = (bf16[2,128,128]{2,1,0:T(8,128)(2,1)S(1)}, bf16[2,128,128]{2,1,0:T(8,128)(2,1)S(1)}, u32[]{:S(2)}, u32[]{:S(2)}) collective-permute-start(bf16[2,128,128]{2,1,0:T(8,128)(2,1)S(1)} %get-tuple-element.143), channel_id=1, source_target_pairs={{0,192},{8,200},{16,208},{24,216},{32,224},{40,232},{48,240},{56,2... | collective-permute-start | bytes 196616 | tf_op jit(solution)/shard_map/ppermute | solution.py:422
  70.8 5.4 %collective-permute-start.27 = (bf16[2,128,128]{2,1,0:T(8,128)(2,1)S(1)}, bf16[2,128,128]{2,1,0:T(8,128)(2,1)S(1)}, u32[]{:S(2)}, u32[]{:S(2)}) collective-permute-start(bf16[2,128,128]{2,1,0:T(8,128)(2,1)S(1)} %get-tuple-element.144), channel_id=1, source_target_pairs={{0,128},{8,136},{16,144},{24,152},{32,160},{40,168},{48,176},{56,1... | collective-permute-start | bytes 196616 | tf_op jit(solution)/shard_map/ppermute | solution.py:422
  70.8 6.1 %collective-permute-start.28 = (bf16[2,128,128]{2,1,0:T(8,128)(2,1)S(1)}, bf16[2,128,128]{2,1,0:T(8,128)(2,1)S(1)}, u32[]{:S(2)}, u32[]{:S(2)}) collective-permute-start(bf16[2,128,128]{2,1,0:T(8,128)(2,1)S(1)} %get-tuple-element.145), channel_id=1, source_target_pairs={{0,64},{8,72},{16,80},{24,88},{32,96},{40,104},{48,112},{56,120},{... | collective-permute-start | bytes 196616 | tf_op jit(solution)/shard_map/ppermute | solution.py:422
